TPU v7x, 32 devices: a whole 2x2x4 slice. The times are simulated.
32 devices in a mesh: dp: 8 (over z, y), expert: 4 (over x, core).
Axes of the slice: x: 2, y: 2, z: 4, core: 2. Of those that a mesh axis runs over, the one named last changes fastest.
Arguments:
- tokens: bfloat16 [4096, 2048], P(('dp', 'expert')), may hold values from -6 to 6
- cotangent: bfloat16 [4096, 2048], P(('dp', 'expert')), may hold values from -6 to 6
- segments: int32 [32, 128], P(('dp', 'expert')), may hold values from 0 to 5, never falling along the last dimension, each value on 1 to 64 neighbouring positions
- routes: int32 [4096, 8], P(('dp', 'expert')), may hold values from 0 to 31, as said below
- slot_index: int32 [4096, 8], P(('dp', 'expert')), may hold values from 0 to 35, as said below
- in_projection: bfloat16 [2048, 6144], P(('dp', 'expert')), may hold values from -0.13258252 to 0.13258252
- out_projection: bfloat16 [2048, 2048], P(('dp', 'expert')), may hold values from -0.375 to 0.375
- router_weight: bfloat16 [2048, 32], P(('dp', 'expert')), may hold values from -0.06629126 to 0.06629126
- norm_gains: bfloat16 [4, 2048], P(None, ('dp', 'expert')), may hold values from 0.4 to 2
- expert_in: bfloat16 [32, 2048, 2048], P('expert', 'dp'), may hold values from -0.125 to 0.125
- expert_down: bfloat16 [32, 1024, 2048], P('expert', 'dp'), may hold values from -1.5 to 1.5
Outputs:
- block_out: float32 [4096, 2048], P(('dp', 'expert'))
- input_grad: float32 [4096, 2048], P(('dp', 'expert'))
- grad_in_projection: float32 [2048, 6144], P(('dp', 'expert'))
- grad_out_projection: float32 [2048, 2048], P(('dp', 'expert'))
- grad_router: float32 [2048, 32], P(('dp', 'expert'))
- grad_norm_gains: float32 [4, 2048], P(None, ('dp', 'expert'))
- grad_expert_in: float32 [32, 2048, 2048], P('expert', 'dp')
- grad_expert_down: float32 [32, 1024, 2048], P('expert', 'dp')
Inputs may be any that keep to these rules, and one draw needn't show every extreme that they name: `routes`: each token names 8 different experts. Among the 128 tokens of one device no expert is named more than 36 times, and on every device one expert is named exactly 36 times, the same one on all devices of one index of dp. `slot_index`: among the tokens of one device, an expert named c times takes each slot 0 to c - 1 once.
All inputs are finite; a program needn't handle non-finite values.
Results may differ from a plain program's by a relative error of at most 0.012.
The roundings to bfloat16 on the way count: a program that leaves them out, or rounds other values in their place, can miss the bound.
Values may be sent and summed in bfloat16 or wider, within the bound.
No kernel may reach another device: no remote copies, remote signals or barrier semaphores. Data moves between devices by JAX's collectives and lax.ppermute only.
A program may use at most 320 MiB of HBM per device.

v0:
```python
import jax
import jax.numpy as jnp
from jax import lax
from jax.sharding import PartitionSpec as P

HEADS = 16
HEAD_DIM = 128
TOP = 8
SPREAD = 4


EPSILON = 1e-05
ROPE_BASE = 10000.0
MASKED = -1e30


def normalize(tensor):
    factor = lax.rsqrt(jnp.mean(tensor * tensor, axis=-1, keepdims=True) + EPSILON)
    return (tensor * factor, factor)


def normalize_back(upstream, normed, factor):
    return factor * (upstream - normed * jnp.mean(upstream * normed, axis=-1, keepdims=True))


def rope_tables(length):
    half_dim = HEAD_DIM // 2
    position = jnp.arange(length).astype(jnp.float32)
    frequency = ROPE_BASE ** (-2.0 * jnp.arange(half_dim).astype(jnp.float32) / HEAD_DIM)
    angles = position[:, None] * frequency[None, :]
    return (jnp.cos(angles)[:, None, :], jnp.sin(angles)[:, None, :])


def rotate(tensor, cosine, sine_table, inverse):
    length = tensor.shape[0]
    halves = tensor.reshape(length, HEADS, 2, HEAD_DIM // 2)
    first_half = halves[:, :, 0, :]
    second_half = halves[:, :, 1, :]
    if inverse:
        sine_table = -sine_table
    turned = jnp.stack(
        [
            first_half * cosine - second_half * sine_table,
            second_half * cosine + first_half * sine_table,
        ],
        axis=2,
    )
    return turned.reshape(length, HEADS * HEAD_DIM)


def split_heads(tensor):
    return tensor.reshape(tensor.shape[0], HEADS, HEAD_DIM)


def masked_scores(queries, key_rows, segment):
    length = queries.shape[0]
    raw_scores = jnp.einsum(
        "qhd,khd->hqk",
        split_heads(queries),
        split_heads(key_rows),
        preferred_element_type=jnp.float32,
    ) * HEAD_DIM ** (-0.5)
    row_index = lax.broadcasted_iota(jnp.int32, (length, length), 0)
    col_index = lax.broadcasted_iota(jnp.int32, (length, length), 1)
    allowed = (segment[:, None] == segment[None, :]) & (col_index <= row_index)
    return (jnp.where(allowed[None], raw_scores, MASKED), allowed)


def attend(queries, key_rows, values, segment):
    length = queries.shape[0]
    scores, allowed = masked_scores(queries, key_rows, segment)
    row_max = jnp.max(scores, axis=-1, keepdims=True)
    exp_terms = jnp.exp(scores - row_max)
    row_total = jnp.sum(exp_terms, axis=-1, keepdims=True)
    log_total = row_max + jnp.log(row_total)
    weights_b = (exp_terms / row_total).astype(jnp.bfloat16)
    attended = jnp.einsum(
        "hqk,khd->qhd", weights_b, split_heads(values), preferred_element_type=jnp.float32
    )
    return (attended.astype(jnp.bfloat16).reshape(length, HEADS * HEAD_DIM), log_total)


def attend_back(queries, key_rows, values, segment, log_total, attended, grad_attended):
    length = queries.shape[0]
    scores, allowed = masked_scores(queries, key_rows, segment)
    weights_f = jnp.where(allowed[None], jnp.exp(scores - log_total), 0.0)
    weights_b = weights_f.astype(jnp.bfloat16)
    grad_heads = split_heads(grad_attended)
    grad_values = jnp.einsum(
        "hqk,qhd->khd", weights_b, grad_heads, preferred_element_type=jnp.float32
    )
    grad_weights = jnp.einsum(
        "qhd,khd->hqk", grad_heads, split_heads(values), preferred_element_type=jnp.float32
    )
    row_delta = jnp.sum(
        grad_heads.astype(jnp.float32) * split_heads(attended).astype(jnp.float32), axis=-1
    ).T
    grad_scores = (weights_f * (grad_weights - row_delta[:, :, None]) * HEAD_DIM ** (-0.5)).astype(
        jnp.bfloat16
    )
    grad_queries = jnp.einsum(
        "hqk,khd->qhd", grad_scores, split_heads(key_rows), preferred_element_type=jnp.float32
    )
    grad_keys = jnp.einsum(
        "hqk,qhd->khd", grad_scores, split_heads(queries), preferred_element_type=jnp.float32
    )
    width = HEADS * HEAD_DIM
    return (
        grad_queries.reshape(length, width),
        grad_keys.reshape(length, width),
        grad_values.reshape(length, width),
    )


def activate(pre_act):
    half_width = pre_act.shape[1] // 2
    return (jax.nn.silu(pre_act[:, :half_width]) * pre_act[:, half_width:]).astype(jnp.bfloat16)


def expert_back(pre_act, row_block, grad_rows, weight_in, weight_down):
    half_width = pre_act.shape[1] // 2
    gate_part = pre_act[:, :half_width]
    up_part = pre_act[:, half_width:]
    act_rows = activate(pre_act)
    grad_weight_down = jnp.dot(act_rows.T, grad_rows, preferred_element_type=jnp.float32)
    grad_act = jnp.dot(grad_rows, weight_down.T, preferred_element_type=jnp.float32)
    gate_sigmoid = jax.nn.sigmoid(gate_part)
    grad_gate = grad_act * up_part * gate_sigmoid * (1.0 + gate_part * (1.0 - gate_sigmoid))
    grad_up = grad_act * gate_part * gate_sigmoid
    grad_pre = jnp.concatenate([grad_gate, grad_up], axis=1).astype(jnp.bfloat16)
    grad_weight_in = jnp.dot(row_block.T, grad_pre, preferred_element_type=jnp.float32)
    grad_in_rows = jnp.dot(grad_pre, weight_in.T, preferred_element_type=jnp.float32).astype(
        jnp.bfloat16
    )
    return (grad_weight_in, grad_weight_down, grad_in_rows)


def per_device(
    tokens,
    cotangent,
    segments,
    routes,
    slot_index,
    in_projection,
    out_projection,
    router_weight,
    norm_gains,
    expert_in,
    expert_down,
):
    length = tokens.shape[0]
    width = tokens.shape[1]
    local_count = expert_in.shape[0]
    expert_count = lax.axis_size("expert") * local_count
    capacity = length * TOP // expert_count + SPREAD
    segment = segments[0]
    cosine, sine_table = rope_tables(length)
    dense_proj, dense_out, dense_router, dense_gains = (
        lax.all_gather(in_projection, ("dp", "expert"), axis=0, tiled=True),
        lax.all_gather(out_projection, ("dp", "expert"), axis=0, tiled=True),
        lax.all_gather(router_weight, ("dp", "expert"), axis=0, tiled=True),
        lax.all_gather(norm_gains, ("dp", "expert"), axis=1, tiled=True),
    )
    gain_rows = dense_gains.astype(jnp.float32)
    residual = tokens.astype(jnp.float32)
    normed1, factor1 = normalize(residual)
    hidden1 = (normed1 * gain_rows[0]).astype(jnp.bfloat16)
    projected = jnp.dot(hidden1, dense_proj, preferred_element_type=jnp.float32)
    query_normed, query_factor = normalize(projected[:, :width])
    key_normed, key_factor = normalize(projected[:, width : 2 * width])
    queries = rotate(query_normed * gain_rows[2], cosine, sine_table, False).astype(jnp.bfloat16)
    key_rows = rotate(key_normed * gain_rows[3], cosine, sine_table, False).astype(jnp.bfloat16)
    values = projected[:, 2 * width :].astype(jnp.bfloat16)
    attended, log_total = attend(queries, key_rows, values, segment)
    middle = residual + jnp.dot(attended, dense_out, preferred_element_type=jnp.float32)
    normed2, factor2 = normalize(middle)
    hidden2 = (normed2 * gain_rows[1]).astype(jnp.bfloat16)
    logits = jnp.dot(hidden2, dense_router, preferred_element_type=jnp.float32)
    router_probs = jax.nn.softmax(logits, axis=-1)
    chosen = (
        routes[:, :, None] == jnp.arange(expert_count, dtype=jnp.int32)[None, None, :]
    ).astype(jnp.float32)
    gate_values = jnp.sum(router_probs[:, None, :] * chosen, axis=-1)
    copies = jnp.broadcast_to(hidden2[:, None, :], (length, TOP, width)).reshape(
        length * TOP, width
    )
    grad_top = cotangent.astype(jnp.float32)
    grad_rows = (
        (gate_values[:, :, None] * grad_top[:, None, :])
        .astype(jnp.bfloat16)
        .reshape(length * TOP, width)
    )
    dp_count = lax.axis_size("dp")
    expert_axis = lax.axis_size("expert")
    replicas = dp_count // local_count
    per_dest = (capacity + replicas - 1) // replicas
    dest_count = dp_count * expert_axis
    target = (
        routes % local_count * replicas + slot_index // per_dest
    ) * expert_axis + routes // local_count
    ep_place = (target * per_dest + slot_index % per_dest).reshape(-1)
    send_rows = jnp.zeros((dest_count * per_dest, width), jnp.bfloat16).at[ep_place].set(copies)
    send_grads = jnp.zeros((dest_count * per_dest, width), jnp.bfloat16).at[ep_place].set(grad_rows)
    fetched_in, fetched_down = (
        lax.all_to_all(
            jnp.repeat(expert_in, replicas, axis=0), "dp", split_axis=0, concat_axis=1, tiled=True
        ),
        lax.all_to_all(
            jnp.repeat(expert_down, replicas, axis=0), "dp", split_axis=0, concat_axis=1, tiled=True
        ),
    )
    got_rows, got_grads = (
        lax.all_to_all(
            send_rows.reshape(dest_count, per_dest, width),
            ("dp", "expert"),
            split_axis=0,
            concat_axis=0,
            tiled=True,
        ),
        lax.all_to_all(
            send_grads.reshape(dest_count, per_dest, width),
            ("dp", "expert"),
            split_axis=0,
            concat_axis=0,
            tiled=True,
        ),
    )
    row_block = got_rows.reshape(dest_count * per_dest, width)
    grad_block = got_grads.reshape(dest_count * per_dest, width)
    whole_in = fetched_in[0]
    whole_down = fetched_down[0]
    pre_act = jnp.dot(row_block, whole_in, preferred_element_type=jnp.float32)
    outputs = jnp.dot(activate(pre_act), whole_down, preferred_element_type=jnp.float32).astype(
        jnp.bfloat16
    )
    grad_weight_in, grad_weight_down, grad_in_rows = expert_back(
        pre_act, row_block, grad_block, whole_in, whole_down
    )
    back_rows, back_grads = (
        lax.all_to_all(
            outputs.reshape(dest_count, per_dest, width),
            ("dp", "expert"),
            split_axis=0,
            concat_axis=0,
            tiled=True,
        ),
        lax.all_to_all(
            grad_in_rows.reshape(dest_count, per_dest, width),
            ("dp", "expert"),
            split_axis=0,
            concat_axis=0,
            tiled=True,
        ),
    )
    home_in, home_down = (
        lax.all_to_all(grad_weight_in[None], "dp", split_axis=1, concat_axis=0, tiled=True),
        lax.all_to_all(grad_weight_down[None], "dp", split_axis=1, concat_axis=0, tiled=True),
    )
    grad_expert_in = jnp.sum(
        home_in.reshape(local_count, replicas, home_in.shape[1], home_in.shape[2]), axis=1
    )
    grad_expert_down = jnp.sum(
        home_down.reshape(local_count, replicas, home_down.shape[1], home_down.shape[2]), axis=1
    )
    picked = (
        back_rows.reshape(dest_count * per_dest, width)[ep_place]
        .reshape(length, TOP, width)
        .astype(jnp.float32)
    )
    grad_expert_rows = jnp.sum(
        back_grads.reshape(dest_count * per_dest, width)[ep_place]
        .reshape(length, TOP, width)
        .astype(jnp.float32),
        axis=1,
    )
    mixture = jnp.sum(gate_values[:, :, None] * picked, axis=1)
    block_out = middle + mixture
    back_proj, back_out, back_router = (dense_proj, dense_out, dense_router)
    grad_gates = jnp.sum(grad_top[:, None, :] * picked, axis=-1)
    grad_probs = jnp.sum(grad_gates[:, :, None] * chosen, axis=1)
    grad_logits = (
        router_probs * (grad_probs - jnp.sum(router_probs * grad_probs, axis=-1, keepdims=True))
    ).astype(jnp.bfloat16)
    grad_router_part = jnp.dot(hidden2.T, grad_logits, preferred_element_type=jnp.float32)
    grad_hidden2 = grad_expert_rows + jnp.dot(
        grad_logits, back_router.T, preferred_element_type=jnp.float32
    )
    grad_gain_moe = jnp.sum(grad_hidden2 * normed2, axis=0)
    grad_middle = grad_top + normalize_back(grad_hidden2 * gain_rows[1], normed2, factor2)
    grad_mid_b = grad_middle.astype(jnp.bfloat16)
    grad_out_part = jnp.dot(attended.T, grad_mid_b, preferred_element_type=jnp.float32)
    grad_attended = jnp.dot(grad_mid_b, back_out.T, preferred_element_type=jnp.float32).astype(
        jnp.bfloat16
    )
    grad_queries, grad_keys, grad_values = attend_back(
        queries, key_rows, values, segment, log_total, attended, grad_attended
    )
    grad_qscaled = rotate(grad_queries, cosine, sine_table, True)
    grad_kscaled = rotate(grad_keys, cosine, sine_table, True)
    grad_query_raw = normalize_back(grad_qscaled * gain_rows[2], query_normed, query_factor)
    grad_key_raw = normalize_back(grad_kscaled * gain_rows[3], key_normed, key_factor)
    grad_projected = jnp.concatenate([grad_query_raw, grad_key_raw, grad_values], axis=1).astype(
        jnp.bfloat16
    )
    grad_proj_part = jnp.dot(hidden1.T, grad_projected, preferred_element_type=jnp.float32)
    grad_hidden1 = jnp.dot(grad_projected, back_proj.T, preferred_element_type=jnp.float32)
    grad_gain_part = jnp.stack(
        [
            jnp.sum(grad_hidden1 * normed1, axis=0),
            grad_gain_moe,
            jnp.sum(grad_qscaled * query_normed, axis=0),
            jnp.sum(grad_kscaled * key_normed, axis=0),
        ]
    )
    input_grad = grad_middle + normalize_back(grad_hidden1 * gain_rows[0], normed1, factor1)
    grad_in_projection, grad_out_projection, grad_router, grad_norm_gains = (
        lax.psum_scatter(grad_proj_part, ("dp", "expert"), scatter_dimension=0, tiled=True),
        lax.psum_scatter(grad_out_part, ("dp", "expert"), scatter_dimension=0, tiled=True),
        lax.psum_scatter(grad_router_part, ("dp", "expert"), scatter_dimension=0, tiled=True),
        lax.psum_scatter(grad_gain_part, ("dp", "expert"), scatter_dimension=1, tiled=True),
    )
    return (
        block_out,
        input_grad,
        grad_in_projection,
        grad_out_projection,
        grad_router,
        grad_norm_gains,
        grad_expert_in,
        grad_expert_down,
    )


def solution(mesh):
    in_specs = (
        P(("dp", "expert"), None),
        P(("dp", "expert"), None),
        P(("dp", "expert"), None),
        P(("dp", "expert"), None),
        P(("dp", "expert"), None),
        P(("dp", "expert"), None),
        P(("dp", "expert"), None),
        P(("dp", "expert"), None),
        P(None, ("dp", "expert")),
        P("expert", "dp", None),
        P("expert", "dp", None),
    )
    out_specs = (
        P(("dp", "expert"), None),
        P(("dp", "expert"), None),
        P(("dp", "expert"), None),
        P(("dp", "expert"), None),
        P(("dp", "expert"), None),
        P(None, ("dp", "expert")),
        P("expert", "dp", None),
        P("expert", "dp", None),
    )
    return jax.shard_map(
        per_device, mesh=mesh, in_specs=in_specs, out_specs=out_specs, check_vma=False
    )
```

profile of v0, /device:TPU:0, one launch (start us, length us, event | category | flops | bytes accessed | tf_op | source)
XLA Modules:
  0.0 2304.9 jit_solution(9352461960969198733)
XLA Ops:
  16.2 219.3 %all-gather = bf16[32,64,4]{1,2,0:T(4,128)(2,1)S(1)} all-gather(bf16[1,64,4]{1,2,0:T(4,128)(2,1)S(1)} %bitcast.153), channel_id=1, replica_groups=mesh['dp'=8,'expert'=4] {'dp','expert'}, dimensions={0}, use_global_device_ids=true | all-gather | bytes 16896 | tf_op jit(solution)/shard_map/all_gather | solution.py:162
  235.8 125.0 %all-gather.1 = bf16[32,64,32]{1,2,0:T(8,128)(2,1)S(1)} all-gather(bf16[1,64,32]{1,2,0:T(8,128)(2,1)S(1)} %bitcast.150), channel_id=1, replica_groups=mesh['dp'=8,'expert'=4] {'dp','expert'}, dimensions={0}, use_global_device_ids=true | all-gather | bytes 135168 | tf_op jit(solution)/shard_map/all_gather | solution.py:161
  386.6 14.1 all-gather.7.cloned.1.call-done
  446.2 99.9 %all-to-all-done.4 = bf16[32,36,2048]{2,1,0:T(8,128)(2,1)} async-done(((bf16[32,36,2048]{2,1,0:T(8,128)(2,1)}), bf16[32,36,2048]{2,1,0:T(8,128)(2,1)}, u32[]{:S(2)}, u32[]{:S(2)}) %all-to-all-start.4) | async-done | bytes 4718624 | tf_op jit(solution)/shard_map/all_to_all | solution.py:220
  546.1 119.7 %all_to_all.56 = bf16[32,36,2048]{2,1,0:T(8,128)(2,1)} all-to-all(bf16[32,36,2048]{2,1,0:T(8,128)(2,1)} %reshape.347), channel_id=1, replica_groups=mesh['dp'=8,'expert'=4] {'dp','expert'}, dimensions={0} | all-to-all | bytes 9437184 | tf_op jit(solution)/shard_map/all_to_all | solution.py:213
  685.1 15.9 fusion.72
  701.0 62.5 %all-to-all-done.2 = bf16[8,128,2048]{2,1,0:T(8,128)(2,1)} async-done(((bf16[8,128,2048]{2,1,0:T(8,128)(2,1)}), bf16[8,128,2048]{2,1,0:T(8,128)(2,1)}, u32[]{:S(2)}, u32[]{:S(2)}) %all-to-all-start.2) | async-done | bytes 4194336 | tf_op jit(solution)/shard_map/all_to_all | solution.py:208
  763.5 13.4 multiply_convert_fusion.1
  779.1 13.9 convolution_convert_fusion.1
  821.0 100.5 %all-to-all-done.5 = bf16[32,36,2048]{2,1,0:T(8,128)(2,1)} async-done(((bf16[32,36,2048]{2,1,0:T(8,128)(2,1)}), bf16[32,36,2048]{2,1,0:T(8,128)(2,1)}, u32[]{:S(2)}, u32[]{:S(2)}) %all-to-all-start.5) | async-done | bytes 4718624 | tf_op jit(solution)/shard_map/all_to_all | solution.py:247
  932.5 11.8 gather_fusion.1
  950.3 91.7 %all-to-all-done.3 = bf16[32,36,2048]{2,1,0:T(8,128)(2,1)} async-done(((bf16[32,36,2048]{2,1,0:T(8,128)(2,1)}), bf16[32,36,2048]{2,1,0:T(8,128)(2,1)}, u32[]{:S(2)}, u32[]{:S(2)}) %all-to-all-start.3) | async-done | bytes 4718624 | tf_op jit(solution)/shard_map/all_to_all | solution.py:240
  1049.2 11.8 gather_fusion
  1108.1 14.5 fusion.25
  1135.3 19.6 fusion.31
  1163.4 12.5 copy.175
  1181.1 14.8 convolution_bitcast_fusion
  1195.9 20.2 copy.174
  1216.1 152.9 %all-to-all-done.7 = f32[1,1024,2048]{2,0,1:T(1,128)} async-done(((f32[1,1024,2048]{2,0,1:T(1,128)}), f32[1,1024,2048]{2,0,1:T(1,128)}, u32[]{:S(2)}, u32[]{:S(2)}) %all-to-all-start.7) | async-done | bytes 8388640 | tf_op jit(solution)/shard_map/all_to_all | solution.py:257
  1377.7 94.1 %reduce-scatter.13.cloned.1.call-done = f32[64,32]{1,0:T(8,128)} async-done(((f32[2048,32]{1,0:T(8,128)}), f32[64,32]{1,0:T(8,128)}) %reduce-scatter.13.cloned.1.call-update) | async-done | bytes 8208
  1484.1 301.4 %all-to-all-done.6 = f32[1,2048,2048]{2,0,1:T(1,128)} async-done(((f32[1,2048,2048]{2,0,1:T(1,128)}), f32[1,2048,2048]{2,0,1:T(1,128)}, u32[]{:S(2)}, u32[]{:S(2)}) %all-to-all-start.6) | async-done | bytes 16777248 | tf_op jit(solution)/shard_map/all_to_all | solution.py:256
  1785.5 15.9 copy.190
  1801.4 23.6 %reduce-scatter.11.cloned.1.call-done = f32[64,2048]{1,0:T(8,128)} async-done(((f32[2048,2048]{1,0:T(8,128)}), f32[64,2048]{1,0:T(8,128)}) %reduce-scatter.11.cloned.1.call-update) | async-done | bytes 524304 | tf_op jit(solution)/shard_map/reduce_scatter | solution.py:318
  1825.0 472.6 %reduce-scatter.9.cloned.1.call-done = f32[64,6144]{1,0:T(8,128)} async-done(((f32[2048,6144]{1,0:T(8,128)}), f32[64,6144]{1,0:T(8,128)}) %reduce-scatter.9.cloned.1.call-update) | async-done | bytes 1572880 | tf_op jit(solution)/shard_map/reduce_scatter | solution.py:317
  (172 shorter events, 248.5 us)
Async XLA Ops:
  7.2 356.3 %all-gather.5.cloned.1.call-start = ((), (), s32[]{:S(2)}) async-start(), calls=%async_computation.12 | async-start | bytes 25952256 | tf_op jit(solution)/shard_map/all_gather | solution.py:159
  7.9 392.8 %all-gather.7.cloned.1.call-start = ((), (), s32[]{:S(2)}) async-start(), calls=%async_computation.13 | async-start | bytes 8650752 | tf_op jit(solution)/shard_map/all_gather | solution.py:160
  8.7 7.5 copy-start.29
  8.7 226.9 %copy-start.23 = (s32[128,8]{0,1:T(8,128)S(1)}, s32[128,8]{0,1:T(8,128)}, u32[]{:S(2)}) copy-start(s32[128,8]{0,1:T(8,128)} %param.14) | copy-start | bytes 12292
  8.7 226.9 %copy-start.27 = (s32[128,8]{0,1:T(8,128)S(1)}, s32[128,8]{0,1:T(8,128)}, u32[]{:S(2)}) copy-start(s32[128,8]{0,1:T(8,128)} %param.15) | copy-start | bytes 12292
  8.7 227.1 %copy-start.26 = (bf16[64,32]{0,1:T(8,128)(2,1)S(1)}, bf16[64,32]{0,1:T(8,128)(2,1)}, u32[]{:S(2)}) copy-start(bf16[64,32]{0,1:T(8,128)(2,1)} %param.18) | copy-start | bytes 12292
  8.7 352.4 %copy-start.18 = (bf16[128,2048]{1,0:T(8,128)(2,1)S(1)}, bf16[128,2048]{1,0:T(8,128)(2,1)}, u32[]{:S(2)}) copy-start(bf16[128,2048]{1,0:T(8,128)(2,1)} %param.12) | copy-start | bytes 1572868
  8.7 353.5 %copy-start.4 = (bf16[128,2048]{1,0:T(8,128)(2,1)S(1)}, bf16[128,2048]{1,0:T(8,128)(2,1)}, u32[]{:S(2)}) copy-start(bf16[128,2048]{1,0:T(8,128)(2,1)} %param.11) | copy-start | bytes 1572868
  8.7 353.7 %copy-start.28 = (s32[1,128]{1,0:T(1,128)S(1)}, s32[1,128]{1,0:T(1,128)}, u32[]{:S(2)}) copy-start(s32[1,128]{1,0:T(1,128)} %param.13) | copy-start | bytes 1540
  8.7 417.0 %all-to-all-start.1 = ((bf16[8,256,2048]{2,1,0:T(8,128)(2,1)}), bf16[8,256,2048]{2,1,0:T(8,128)(2,1)}, u32[]{:S(2)}, u32[]{:S(2)}) async-start(bf16[8,256,2048]{2,1,0:T(8,128)(2,1)} %param.20), calls=%async_computation.1 | async-start | bytes 16777216 | tf_op jit(solution)/shard_map/all_to_all | solution.py:205
  362.4 12.0 copy-start.24
  363.4 11.0 copy-start.20
  425.7 120.4 %all-to-all-start.4 = ((bf16[32,36,2048]{2,1,0:T(8,128)(2,1)}), bf16[32,36,2048]{2,1,0:T(8,128)(2,1)}, u32[]{:S(2)}, u32[]{:S(2)}) async-start(bf16[32,36,2048]{2,1,0:T(8,128)(2,1)} %reshape.351), calls=%async_computation.4 | async-start | bytes 10485760 | tf_op jit(solution)/shard_map/all_to_all | solution.py:220
  665.8 97.7 %all-to-all-start.2 = ((bf16[8,128,2048]{2,1,0:T(8,128)(2,1)}), bf16[8,128,2048]{2,1,0:T(8,128)(2,1)}, u32[]{:S(2)}, u32[]{:S(2)}) async-start(bf16[8,128,2048]{2,1,0:T(8,128)(2,1)} %param.21), calls=%async_computation.2 | async-start | bytes 8388608 | tf_op jit(solution)/shard_map/all_to_all | solution.py:208
  800.2 121.3 %all-to-all-start.5 = ((bf16[32,36,2048]{2,1,0:T(8,128)(2,1)}), bf16[32,36,2048]{2,1,0:T(8,128)(2,1)}, u32[]{:S(2)}, u32[]{:S(2)}) async-start(bf16[32,36,2048]{2,1,0:T(8,128)(2,1)} %reshape.353), calls=%async_computation.5 | async-start | bytes 10485760 | tf_op jit(solution)/shard_map/all_to_all | solution.py:247
  921.5 120.4 %all-to-all-start.3 = ((bf16[32,36,2048]{2,1,0:T(8,128)(2,1)}), bf16[32,36,2048]{2,1,0:T(8,128)(2,1)}, u32[]{:S(2)}, u32[]{:S(2)}) async-start(bf16[32,36,2048]{2,1,0:T(8,128)(2,1)} %reshape.349), calls=%async_computation.3 | async-start | bytes 10485760 | tf_op jit(solution)/shard_map/all_to_all | solution.py:240
  925.2 451.1 %reduce-scatter.15.cloned.1.call-start = ((), (), s32[]{:S(2)}) async-start(), calls=%async_computation.17 | async-start | bytes 1081344
  1108.1 16.0 copy-start.9
  1124.1 347.7 %reduce-scatter.13.cloned.1.call-start = ((), (), s32[]{:S(2)}) async-start(), calls=%async_computation.16 | async-start | bytes 1081344
  1125.5 699.5 %reduce-scatter.11.cloned.1.call-start = ((), (), s32[]{:S(2)}) async-start(), calls=%async_computation.15 | async-start | bytes 17301504 | tf_op jit(solution)/shard_map/reduce_scatter | solution.py:318
  1133.9 1163.7 %reduce-scatter.9.cloned.1.call-start = ((), (), s32[]{:S(2)}) async-start(), calls=%async_computation.14 | async-start | bytes 51904512 | tf_op jit(solution)/shard_map/reduce_scatter | solution.py:317
  1175.9 193.0 %all-to-all-start.7 = ((f32[1,1024,2048]{2,0,1:T(1,128)}), f32[1,1024,2048]{2,0,1:T(1,128)}, u32[]{:S(2)}, u32[]{:S(2)}) async-start(f32[1,1024,2048]{2,0,1:T(1,128)} %copy.175), calls=%async_computation.9 | async-start | bytes 16777216 | tf_op jit(solution)/shard_map/all_to_all | solution.py:257
  1216.1 158.9 %copy-start.19 = (f32[128,2048]{1,0:T(8,128)S(1)}, f32[128,2048]{1,0:T(8,128)}, u32[]{:S(2)}) copy-start(f32[128,2048]{1,0:T(8,128)} %get-tuple-element.57) | copy-start | bytes 3145732
  1368.9 416.6 %all-to-all-start.6 = ((f32[1,2048,2048]{2,0,1:T(1,128)}), f32[1,2048,2048]{2,0,1:T(1,128)}, u32[]{:S(2)}, u32[]{:S(2)}) async-start(f32[1,2048,2048]{2,0,1:T(1,128)} %copy.174), calls=%async_computation.8 | async-start | bytes 33554432 | tf_op jit(solution)/shard_map/all_to_all | solution.py:256
  (21 other events, 52.9 us)
Sparse Core Ops, SparseCore 0:
  10.9 310.1 all-gather.4
  323.9 76.7 all-gather.6
  1124.2 140.0 reduce-scatter.14
  1266.5 205.2 reduce-scatter.12
  1474.5 350.3 reduce-scatter.10
  1831.8 465.6 reduce-scatter.8
where the time goes:
time: 2320 us; the launch traced here: 2300 us
  waiting for transfers between devices  1410 us (61%)
  blocking collectives  464 us (20%)
  local copies, waits for them, and re-layouts  178 us (8%)
  matrix products  153 us (7%)
  other arithmetic  44.7 us (2%)
  starting transfers between devices  35.8 us (2%)
    reduce_scatter x1, waiting for transfers between devices, per_device(): lax.psum_scatter(grad_proj_part, ('dp', 'expert'), scatter_dimension=0, t...  473 us
    all_to_all x1, waiting for transfers between devices, per_device(): lax.all_to_all(grad_weight_in[None], 'dp', split_axis=1, concat_axis=0, t...  301 us
    all_gather x1, blocking collectives, per_device(): lax.all_gather(norm_gains, ('dp', 'expert'), axis=1, tiled=True)  219 us
    all_to_all x1, waiting for transfers between devices, per_device(): lax.all_to_all(grad_weight_down[None], 'dp', split_axis=1, concat_axis=0,...  153 us
    all_gather x1, blocking collectives, per_device(): lax.all_gather(router_weight, ('dp', 'expert'), axis=0, tiled=True)  125 us
    all_to_all x1, blocking collectives, per_device(): lax.all_to_all(send_rows.reshape(dest_count, per_dest, width), ('dp', 'ex...  120 us
    all_to_all x1, waiting for transfers between devices, per_device(): lax.all_to_all(grad_in_rows.reshape(dest_count, per_dest, width), ('dp',...  101 us
    all_to_all x1, waiting for transfers between devices, per_device(): lax.all_to_all(send_grads.reshape(dest_count, per_dest, width), ('dp', 'e...  99.9 us
  transfers between devices with their start and end apart: 13, of which 10 were waited for; matrix products, arithmetic and copies ran while one was open for 11% of the time, Pallas kernels for 0%

commit v1 on v0

v1 whole, which is shorter than its diff:
```python
import functools

import jax
import jax.numpy as jnp
import numpy as np
from jax import lax
from jax.experimental import pallas as pl
from jax.experimental.pallas import tpu as pltpu
from jax.sharding import PartitionSpec as P

HEADS = 16
HEAD_DIM = 128
EPSILON = 1e-05
ROPE_BASE = 10000.0
MASKED = -1e30
AXES = ("dp", "expert")
BF16 = jnp.bfloat16
F32 = jnp.float32
ROWS_BACK = (((1,), (1,)), ((), ()))
SUM_ROWS = (((0,), (0,)), ((), ()))


def dot(left, right, dims=(((1,), (0,)), ((), ()))):
    return lax.dot_general(left, right, dims, preferred_element_type=F32)


def after(value, *others):
    return lax.optimization_barrier((value,) + others)[0]


def normalize(tensor):
    factor = lax.rsqrt(jnp.mean(tensor * tensor, axis=-1, keepdims=True) + EPSILON)
    return (tensor * factor, factor)


def normalize_back(upstream, normed, factor):
    return factor * (upstream - normed * jnp.mean(upstream * normed, axis=-1, keepdims=True))


def rope_tables(length):
    half_dim = HEAD_DIM // 2
    position = jnp.arange(length).astype(F32)
    frequency = ROPE_BASE ** (-2.0 * jnp.arange(half_dim).astype(F32) / HEAD_DIM)
    angles = position[:, None] * frequency[None, :]
    return (jnp.cos(angles), jnp.sin(angles))


def rotate(tensor, cosine, sine_table, inverse):
    half = HEAD_DIM // 2
    first_half, second_half = tensor[..., :half], tensor[..., half:]
    cosine, sine_table = cosine[None, :, None, :], sine_table[None, :, None, :]
    if inverse:
        sine_table = -sine_table
    return jnp.concatenate(
        [
            first_half * cosine - second_half * sine_table,
            second_half * cosine + first_half * sine_table,
        ],
        axis=-1,
    )


class Grid:
    def __init__(self, swap=True):
        self.dp = lax.axis_size("dp")
        self.ex = lax.axis_size("expert")
        self.count = self.dp * self.ex
        self.size = {"z": 4, "y": self.dp // 4, "x": self.ex // 2, "c": 2}
        self.swap = swap and self.size["x"] == self.size["y"]
        self.size["A"], self.size["B"] = self.size["y"], self.size["x"]
        d, e = lax.axis_index("dp"), lax.axis_index("expert")
        self.linear = d * self.ex + e
        ny = self.size["y"]
        self.at = {"z": d // ny, "y": d % ny, "x": e // 2, "c": e % 2}

    def real(self, axis, core):
        if axis in "AB":
            return "yx"[(axis == "B") != (core == 1 and self.swap)]
        return axis

    def index(self, p):
        return (p["z"] * self.size["y"] + p["y"]) * self.ex + p["x"] * 2 + p["c"]

    def move(self, value, axis, kind="pair"):
        s = self.size
        if s[axis] == 2:
            moves = {0: 1, 1: 0}
        else:
            moves = {
                "pair": {0: 1, 1: 0, 2: 3, 3: 2},
                "mid": {1: 2, 2: 1},
                "out": {1: 0, 2: 3},
                "in": {0: 1, 3: 2},
            }[kind]
        pairs = []
        for i in range(self.count):
            d, e = divmod(i, self.ex)
            here = {"z": d // s["y"], "y": d % s["y"], "x": e // 2, "c": e % 2}
            line = self.real(axis, here["c"])
            if here[line] in moves:
                pairs.append((i, self.index({**here, line: moves[here[line]]})))
        return lax.ppermute(value, AXES, pairs)

    def position(self, axis):
        if axis in "AB" and self.swap:
            other = self.real(axis, 1)
            return jnp.where(self.at["c"] == 0, self.at[self.real(axis, 0)], self.at[other])
        return self.at[self.real(axis, 0)]

    def slots(self, axis):
        n = self.size[axis]
        table = {
            1: [[0]],
            2: [[0, 1], [1, 0]],
            4: [[0, 1, 2, 3], [1, 0, 2, 3], [2, 3, 1, 0], [3, 2, 1, 0]],
        }[n]
        return jnp.asarray(np.array(table, np.int32))[self.at[axis]]

    def sources(self):
        c, y, x, z = [self.slots(a) for a in "cyxz"]
        z = z.reshape(2, 1, 1, 1, 2)
        c = c.reshape(1, -1, 1, 1, 1)
        along_a = (1, 1, 1, -1, 1)
        along_b = (1, 1, -1, 1, 1)
        xs, ys = x.reshape(along_b), y.reshape(along_a)
        if self.swap:
            xs = jnp.where(c == 0, xs, x.reshape(along_a))
            ys = jnp.where(c == 0, ys, y.reshape(along_b))
        return ((z * self.size["y"] + ys) * self.ex + xs * 2 + c).reshape(-1)

    def dp_sources(self):
        z = self.slots("z").reshape(2, 1, 2)
        return (z * self.size["y"] + self.slots("y").reshape(1, -1, 1)).reshape(-1)

    def line_gather(self, value, axis):
        n = self.size[axis]
        if n == 1:
            return [value]
        pair = self.move(value, axis)
        if n == 2:
            return [value, pair]
        m0, m1 = self.move(value, axis, "mid"), self.move(pair, axis, "mid")
        o0, o1 = self.move(m0, axis, "out"), self.move(m1, axis, "out")
        at = self.position(axis)
        mid = (at == 1) | (at == 2)
        return [value, pair, jnp.where(mid, m0, o0), jnp.where(mid, m1, o1)]

    def line_reduce(self, slots, axis, kind=BF16):
        n = self.size[axis]

        def sent(value, *way):
            return self.move(value.astype(kind), axis, *way).astype(F32)

        if n == 1:
            return slots[0]
        if n == 2:
            return slots[0] + sent(slots[1])
        m3 = sent(slots[3] + sent(slots[3], "in"), "mid")
        m2 = sent(slots[2] + sent(slots[2], "in"), "mid")
        return slots[0] + m2 + sent(slots[1] + m3)

    def gather(self, value):
        pieces = self.line_gather(value, "z")
        out = []
        for h in range(2):
            near = jnp.stack(pieces[2 * h : 2 * h + 2])
            table = [self.line_gather(a, "B") for a in self.line_gather(near, "A")]
            block = jnp.concatenate([row[b] for b in range(self.size["B"]) for row in table])
            out += self.line_gather(block, "c")
        return out

    def scatter(self, groups):
        halves = [None, None]
        for h in (1, 0):
            total = self.line_reduce(groups[2 * h : 2 * h + 2], "c")
            nb, na = self.size["B"], self.size["A"]
            total = total.reshape((nb, na, 2) + total.shape[1:])
            total = self.line_reduce([total[i] for i in range(nb)], "B")
            halves[h] = self.line_reduce([total[i] for i in range(na)], "A")
        return self.line_reduce([halves[0][0], halves[0][1], halves[1][0], halves[1][1]], "z")

    def dp_gather(self, value):
        pieces = self.line_gather(value, "z")
        z, y = self.slots("z"), self.slots("y")
        n = value.shape[0]
        whole = jnp.zeros((n * self.dp,) + value.shape[1:], value.dtype)
        for h in range(2):
            near = jnp.stack(pieces[2 * h : 2 * h + 2])
            for j, got in enumerate(self.line_gather(near, "y")):
                for k in range(2):
                    place = (z[2 * h + k] * self.size["y"] + y[j]) * n
                    whole = lax.dynamic_update_slice_in_dim(whole, got[k], place, 0)
        return whole, pieces[3]

    def dp_scatter(self, halves):
        sums = [None, None]
        for h in (1, 0):
            sums[h] = self.line_reduce([halves[h][i] for i in range(self.size["y"])], "y")
        return self.line_reduce([sums[0][0], sums[0][1], sums[1][0], sums[1][1]], "z")

    def flip(self, value, bit):
        return lax.ppermute(value, AXES, [(i, i ^ bit) for i in range(self.count)])

    def small_gather(self, value):
        held, bit = value[None], 1
        while bit < self.count:
            held = jnp.concatenate([held, self.flip(held, bit)])
            bit *= 2
        return held[self.linear ^ jnp.arange(self.count)]

    def small_scatter(self, value):
        held = value[self.linear ^ jnp.arange(self.count)]
        bit = self.count // 2
        while bit:
            held = held[:bit] + self.flip(held[bit:], bit)
            bit //= 2
        return held[0]

    def group_sum(self, value):
        total = value
        for r in range(1, self.ex):
            total = total + self.flip(value, r)
        return total


def exchange(value):
    return lax.all_to_all(value, "expert", split_axis=0, concat_axis=0, tiled=True)


def moe_kernel(ff, local, x_ref, lift_ref, gate_ref, w_ref, grad_ref, act_ref, sum_ref, back_ref):
    x = x_ref[...]
    per = 128 // ff
    lane = lax.broadcasted_iota(jnp.int32, (x.shape[0], 128), 1)
    for b in range(local // per):
        wide, narrow = pl.ds(256 * b, 256), pl.ds(128 * b, 128)
        pre_act = dot(x, w_ref[:, wide])
        gate_part, up_part = pre_act[:, :128], pre_act[:, 128:]
        spread = jnp.broadcast_to(gate_ref[:, pl.ds(b * per, 1)], lane.shape)
        for k in range(1, per):
            spread = jnp.where(
                lane < k * ff,
                spread,
                jnp.broadcast_to(gate_ref[:, pl.ds(b * per + k, 1)], lane.shape),
            )
        lifted = lift_ref[:, narrow]
        sig = 1.0 / (1.0 + jnp.exp(-gate_part))
        act = (gate_part * sig * up_part).astype(BF16).astype(F32)
        act_ref[:, narrow] = (act * spread).astype(BF16)
        terms = act * lifted
        for k in range(per):
            mine = jnp.where((lane >= k * ff) & (lane < (k + 1) * ff), terms, 0.0)
            sum_ref[:, pl.ds(b * per + k, 1)] = jnp.sum(mine, axis=1, keepdims=True)
        grad_act = lifted * spread
        grad_gate = grad_act * up_part * sig * (1.0 + gate_part * (1.0 - sig))
        grad_ref[:, pl.ds(256 * b, 128)] = grad_gate.astype(BF16)
        grad_ref[:, pl.ds(256 * b + 128, 128)] = (grad_act * gate_part * sig).astype(BF16)
    back_ref[...] = dot(grad_ref[...], w_ref[...], ROWS_BACK).astype(back_ref.dtype)


def moe_rows(x, lifted, gates, weight, ff, start, total, kind):
    width, wide = weight.shape
    local = gates.shape[1]
    tile = 256 if total % 256 == 0 else 128
    skip = start // tile
    row = lambda n: pl.BlockSpec((tile, n), lambda i: (i + skip, 0))
    out = lambda n: pl.BlockSpec((tile, n), lambda i: (i, 0))
    return pl.pallas_call(
        functools.partial(moe_kernel, ff, local),
        grid=(total // tile,),
        in_specs=[
            row(width),
            row(wide // 2),
            row(local),
            pl.BlockSpec((width, wide), lambda i: (0, 0)),
        ],
        out_specs=[out(wide), out(wide // 2), out(local), out(width)],
        out_shape=[
            jax.ShapeDtypeStruct((total, wide), BF16),
            jax.ShapeDtypeStruct((total, wide // 2), BF16),
            jax.ShapeDtypeStruct((total, local), F32),
            jax.ShapeDtypeStruct((total, width), kind),
        ],
        compiler_params=pltpu.CompilerParams(vmem_limit_bytes=56 * 1024 * 1024),
        cost_estimate=pl.CostEstimate(
            flops=4 * total * width * wide, bytes_accessed=total * width * 12, transcendentals=0
        ),
    )(x, lifted, gates, weight)


def deal_kernel(dp, stage_ref, in_ref, *out_refs):
    for r in range(dp):
        place = pl.multiple_of(lax.bitwise_xor(stage_ref[0], r) * 128, 128)
        out_refs[r][...] = in_ref[0, :, pl.ds(place, 128)]


def deal(expert_in, stage, dp):
    local, rows, wide = expert_in.shape
    half = wide // 2
    return pl.pallas_call(
        functools.partial(deal_kernel, dp),
        grid_spec=pltpu.PrefetchScalarGridSpec(
            num_scalar_prefetch=1,
            grid=(local, 2),
            in_specs=[pl.BlockSpec((1, rows, half), lambda e, g, s: (e, 0, g))],
            out_specs=[pl.BlockSpec((rows, 128), lambda e, g, s: (0, 2 * e + g))] * dp,
        ),
        out_shape=[jax.ShapeDtypeStruct((rows, local * 256), expert_in.dtype)] * dp,
        compiler_params=pltpu.CompilerParams(vmem_limit_bytes=32 * 1024 * 1024),
    )(stage.reshape(1), expert_in)


def undeal_kernel(dp, stage_ref, *refs):
    out_ref = refs[dp]
    e, g = pl.program_id(0), pl.program_id(1)
    column = pl.multiple_of((2 * e + g) * 128, 128)
    for r in range(dp):
        place = pl.multiple_of(lax.bitwise_xor(stage_ref[0], r) * 128, 128)
        out_ref[0, :, pl.ds(place, 128)] = refs[r][:, pl.ds(column, 128)].astype(F32)


def undeal(pieces, stage):
    dp = len(pieces)
    rows, wide = pieces[0].shape
    local = wide // 256
    return pl.pallas_call(
        functools.partial(undeal_kernel, dp),
        grid_spec=pltpu.PrefetchScalarGridSpec(
            num_scalar_prefetch=1,
            grid=(local, 2),
            in_specs=[pl.BlockSpec((rows, wide), lambda e, g, s: (0, 0))] * dp,
            out_specs=pl.BlockSpec((1, rows, dp * 128), lambda e, g, s: (e, 0, g)),
        ),
        out_shape=jax.ShapeDtypeStruct((local, rows, 2 * dp * 128), F32),
        compiler_params=pltpu.CompilerParams(vmem_limit_bytes=48 * 1024 * 1024),
    )(stage.reshape(1), *pieces)


def deal_narrow(expert_in, stage, dp):
    local, rows, wide = expert_in.shape
    ff = wide // 2 // dp
    split = expert_in.reshape(local * ff // 128, 128 // ff, rows, 2, dp, ff)
    out = []
    for r in range(dp):
        piece = lax.dynamic_index_in_dim(split, stage ^ r, 4, False)
        out.append(piece.transpose(2, 0, 3, 1, 4).reshape(rows, 2 * local * ff))
    return out


def undeal_narrow(pieces, stage, local):
    dp = len(pieces)
    rows, wide = pieces[0].shape
    ff = wide // 2 // local
    whole = jnp.stack(pieces)[stage ^ jnp.arange(dp)]
    whole = whole.reshape(dp, rows, wide // 256, 2, 128 // ff, ff).astype(F32)
    return whole.transpose(2, 4, 1, 3, 0, 5).reshape(local, rows, 2 * dp * ff)


def masked(segment):
    length = segment.shape[1]
    row_index = lax.broadcasted_iota(jnp.int32, (length, length), 0)
    col_index = lax.broadcasted_iota(jnp.int32, (length, length), 1)
    return (segment[:, :, None] == segment[:, None, :]) & (col_index <= row_index)[None]


def attend(queries, key_rows, values, allowed):
    raw = jnp.einsum("sqhd,skhd->shqk", queries, key_rows, preferred_element_type=F32)
    scores = jnp.where(allowed[:, None], raw * HEAD_DIM ** (-0.5), MASKED)
    row_max = jnp.max(scores, axis=-1, keepdims=True)
    exp_terms = jnp.exp(scores - row_max)
    weights_f = exp_terms / jnp.sum(exp_terms, axis=-1, keepdims=True)
    attended = jnp.einsum(
        "shqk,skhd->sqhd", weights_f.astype(BF16), values, preferred_element_type=F32
    )
    return (attended.astype(BF16), weights_f)


def attend_back(queries, key_rows, values, weights_f, attended, grad_heads):
    weights_b = weights_f.astype(BF16)
    grad_values = jnp.einsum("shqk,sqhd->skhd", weights_b, grad_heads, preferred_element_type=F32)
    grad_weights = jnp.einsum("sqhd,skhd->shqk", grad_heads, values, preferred_element_type=F32)
    row_delta = jnp.sum(grad_heads.astype(F32) * attended.astype(F32), axis=-1)
    row_delta = jnp.swapaxes(row_delta, 1, 2)[..., None]
    grad_scores = (weights_f * (grad_weights - row_delta) * HEAD_DIM ** (-0.5)).astype(BF16)
    grad_queries = jnp.einsum(
        "shqk,skhd->sqhd", grad_scores, key_rows, preferred_element_type=F32
    )
    grad_keys = jnp.einsum("shqk,sqhd->skhd", grad_scores, queries, preferred_element_type=F32)
    return (grad_queries, grad_keys, grad_values)


def per_device(
    tokens,
    cotangent,
    segments,
    routes,
    slot_index,
    in_projection,
    out_projection,
    router_weight,
    norm_gains,
    expert_in,
    expert_down,
):
    grid, wide_x = Grid(), Grid(False)
    length, width = tokens.shape
    count, dp, ex = grid.count, grid.dp, grid.ex
    local = expert_in.shape[0]
    expert_count = ex * local
    top = routes.shape[1]
    ff = expert_down.shape[1]
    rows = width // count
    block = width // dp
    heads = HEADS // ex
    span = heads * HEAD_DIM
    group = lax.axis_index("expert")
    stage = lax.axis_index("dp")
    cosine, sine_table = rope_tables(length)
    source, out_source = grid.sources(), wide_x.sources()
    back, out_back = jnp.argsort(source), jnp.argsort(out_source)
    dp_source = grid.dp_sources()

    def reorder(tensor, order):
        parts = order.shape[0]
        return jnp.take(
            tensor.reshape(tensor.shape[0], parts, width // parts), order, axis=1
        ).reshape(tensor.shape[0], width)

    small = jnp.concatenate(
        [
            norm_gains.reshape(-1),
            router_weight.reshape(-1),
            routes.astype(BF16).reshape(-1),
            segments.astype(BF16).reshape(-1),
        ]
    )
    small = jnp.pad(small, (0, -small.shape[0] % 128)).reshape(-1, 128)
    small = grid.small_gather(small).reshape(count, -1)
    cuts = np.cumsum([4 * rows, rows * expert_count, length * top, length])
    all_gains, all_router, all_routes, all_segments, _ = jnp.split(small, cuts, axis=1)
    gains = jnp.swapaxes(all_gains.reshape(count, 4, rows), 0, 1).reshape(4, width).astype(F32)
    router = all_router.reshape(width, expert_count)
    all_routes = all_routes.reshape(count, length, top).astype(jnp.int32)
    segment = lax.dynamic_slice_in_dim(
        all_segments.reshape(dp, ex, length), stage, 1, 0
    )[0].astype(jnp.int32)
    allowed = masked(segment)
    gain_q = lax.dynamic_slice_in_dim(gains[2], group * span, span)
    gain_k = lax.dynamic_slice_in_dim(gains[3], group * span, span)

    piece = in_projection.reshape(rows, 3, ex, span).transpose(2, 0, 1, 3)
    piece = exchange(piece.reshape(ex, rows, 3 * span)).reshape(block, 3 * span)
    tokens_g = exchange(jnp.broadcast_to(tokens[None], (ex, length, width)))
    proj, arrived = grid.dp_gather(piece)
    proj_out = jnp.concatenate(wide_x.gather(after(out_projection, arrived))).reshape(width, width)

    others = list(range(dp - 1, 0, -1))
    weight_in = jnp.zeros((width, 2 * local * ff), BF16)
    dealt = (deal if ff == 128 else deal_narrow)(expert_in, stage, dp)
    gone = [arrived, arrived]
    for r in [0] + others:
        got = dealt[r]
        if r:
            got = lax.ppermute(after(got, gone[-2]), "dp", [(i, i ^ r) for i in range(dp)])
            gone.append(got)
        weight_in = lax.dynamic_update_slice_in_dim(weight_in, got, (stage ^ r) * block, 0)
    weight_down = expert_down.reshape(local * ff, width)

    chunks = max(1, length * count // 4096)
    size = length // chunks

    def gather_rows(tensor, i):
        return jnp.concatenate(grid.gather(tensor[i * size : (i + 1) * size])).reshape(-1, width)

    normed1_g, factor1 = normalize(tokens_g.reshape(ex * length, width).astype(F32))
    hidden1_g = (normed1_g * gains[0]).astype(BF16)
    projected = dot(hidden1_g, proj)
    query_raw, key_raw = projected[:, :span], projected[:, span : 2 * span]
    squares = jnp.stack([jnp.sum(query_raw**2, axis=-1), jnp.sum(key_raw**2, axis=-1)])
    factors = lax.rsqrt(grid.group_sum(squares) / width + EPSILON)[:, :, None]
    query_factor, key_factor = factors[0], factors[1]
    query_normed, key_normed = query_raw * query_factor, key_raw * key_factor

    def by_heads(tensor):
        return tensor.reshape(ex, length, heads, HEAD_DIM)

    queries = rotate(by_heads(query_normed * gain_q), cosine, sine_table, False).astype(BF16)
    key_rows = rotate(by_heads(key_normed * gain_k), cosine, sine_table, False).astype(BF16)
    values = by_heads(projected[:, 2 * span :].astype(BF16))
    attended_h, weights_f = attend(queries, key_rows, values, allowed)
    attended = exchange(attended_h.reshape(ex, length, span))
    attended_s = reorder(jnp.swapaxes(attended, 0, 1).reshape(length, width), out_source)
    residual = tokens.astype(F32)
    middle = residual + dot(attended_s, proj_out)
    normed2, factor2 = normalize(middle)
    hidden2 = (normed2 * gains[1]).astype(BF16)
    router_probs = jax.nn.softmax(dot(hidden2, router), axis=-1)
    grad_top = cotangent.astype(F32)

    routes_s = all_routes[source]
    mine = group * local + jnp.arange(local, dtype=jnp.int32)
    mixtures, grad_h2s, probs_parts = [], [], []
    grad_in_w, grad_down_w = [0.0] * dp, 0.0
    for i in range(chunks):
        ready = (grad_h2s[-1], mixtures[-1], grad_in_w, grad_down_w) if i else (arrived,)
        cot = gather_rows(after(cotangent, *ready), i)
        hid = gather_rows(after(hidden2, *ready), i)
        total = hid.shape[0]
        probs = jax.nn.softmax(dot(hid, router), axis=-1)
        probs = lax.dynamic_slice_in_dim(probs, group * local, local, 1)
        named = routes_s[:, i * size : (i + 1) * size, :].reshape(total, top)
        chosen = jnp.any(named[:, :, None] == mine[None, None, :], axis=1)
        gate_dense = jnp.where(chosen, probs, 0.0)
        lifted = dot(cot, weight_down, ROWS_BACK)
        part = total // 4
        slotted = (count // 4, size, width)
        done = [None] * 4
        for j in (3, 2, 1, 0):
            kind = BF16 if j % 2 else F32
            done[j] = moe_rows(
                hid, lifted, gate_dense, weight_in, ff, j * part, part, kind
            )
        grad_h2s.append(grid.scatter([d[3].reshape(slotted) for d in done]))
        mixtures.append(grid.scatter([dot(d[1], weight_down).reshape(slotted) for d in done]))
        probs_part = jnp.where(chosen, jnp.concatenate([d[2] for d in done]), 0.0)
        probs_parts.append(probs_part.reshape(count, size, local))
        grad_pre = jnp.concatenate([d[0] for d in done])
        act_gated = jnp.concatenate([d[1] for d in done])
        grad_down_w += dot(act_gated, cot, SUM_ROWS)
        for r in others + [0]:
            rows_in = lax.dynamic_slice_in_dim(hid, (stage ^ r) * block, block, 1)
            grad_in_w[r] += dot(rows_in, grad_pre, SUM_ROWS)

    home = [None] * dp
    gone = []
    for r in others + [0]:
        piece = grad_in_w[r].astype(BF16)
        if r:
            if len(gone) > 1:
                piece = after(piece, gone[-2])
            piece = lax.ppermute(piece, "dp", [(i, i ^ r) for i in range(dp)])
            gone.append(piece)
        home[r] = piece
    grad_expert_in = undeal(home, stage) if ff == 128 else undeal_narrow(home, stage, local)
    grad_expert_down = grad_down_w.reshape(local, ff, width)

    probs_all = jnp.concatenate(probs_parts, axis=1)[back]
    place = (jnp.arange(expert_count) // local == group).astype(F32)
    probs_wide = (jnp.tile(probs_all, (1, 1, ex)) * place).reshape(
        count, length * expert_count // 128, 128
    )
    grad_probs = grid.small_scatter(probs_wide).reshape(length, expert_count)

    block_out = middle + jnp.concatenate(mixtures)
    grad_logits = (
        router_probs * (grad_probs - jnp.sum(router_probs * grad_probs, axis=-1, keepdims=True))
    ).astype(BF16)
    grad_router_part = dot(hidden2, grad_logits, SUM_ROWS)
    grad_hidden2 = jnp.concatenate(grad_h2s) + dot(grad_logits, router, ROWS_BACK)
    grad_gain_moe = jnp.sum(grad_hidden2 * normed2, axis=0)
    grad_middle = grad_top + normalize_back(grad_hidden2 * gains[1], normed2, factor2)
    grad_mid_b = grad_middle.astype(BF16)
    grad_attended = reorder(dot(grad_mid_b, proj_out, ROWS_BACK).astype(BF16), out_back)
    grad_heads = by_heads(
        exchange(jnp.swapaxes(grad_attended.reshape(length, ex, span), 0, 1)).reshape(
            ex * length, span
        )
    )
    quarter = width // 4
    grad_out_projection = wide_x.scatter(
        [
            dot(attended_s[:, j * quarter : (j + 1) * quarter], grad_mid_b, SUM_ROWS).reshape(
                count // 4, rows, width
            )
            for j in range(4)
        ]
    )
    grad_queries, grad_keys, grad_values = attend_back(
        queries, key_rows, values, weights_f, attended_h, grad_heads
    )
    flat = (ex * length, span)
    grad_qscaled = rotate(grad_queries, cosine, sine_table, True).reshape(flat)
    grad_kscaled = rotate(grad_keys, cosine, sine_table, True).reshape(flat)
    up_q, up_k = grad_qscaled * gain_q, grad_kscaled * gain_k
    along = jnp.stack([jnp.sum(up_q * query_normed, axis=-1), jnp.sum(up_k * key_normed, axis=-1)])
    along = (grid.group_sum(along) / width)[:, :, None]
    grad_projected = jnp.concatenate(
        [
            query_factor * (up_q - query_normed * along[0]),
            key_factor * (up_k - key_normed * along[1]),
            grad_values.reshape(flat),
        ],
        axis=1,
    ).astype(BF16)
    mid = width // 2
    hidden1_s = reorder(hidden1_g, dp_source)
    grad_proj = grid.dp_scatter(
        [
            dot(hidden1_s[:, h * mid : (h + 1) * mid], grad_projected, SUM_ROWS).reshape(
                grid.size["y"], 2, block, 3 * span
            )
            for h in range(2)
        ]
    )
    grad_proj = exchange(grad_proj.astype(BF16).reshape(ex, rows, 3 * span)).astype(F32)
    grad_in_projection = (
        grad_proj.reshape(ex, rows, 3, span).transpose(1, 2, 0, 3).reshape(rows, 3 * width)
    )
    grad_hidden1 = dot(grad_projected, proj, ROWS_BACK).astype(BF16)
    grad_hidden1 = jnp.sum(exchange(grad_hidden1.reshape(ex, length, width)).astype(F32), axis=0)
    own = lax.dynamic_slice_in_dim(normed1_g, group * length, length, 0)
    own_factor = lax.dynamic_slice_in_dim(factor1, group * length, length, 0)
    gain_one = jnp.sum(grad_hidden1 * own, axis=0)
    input_grad = grad_middle + normalize_back(grad_hidden1 * gains[0], own, own_factor)

    def widen(values):
        return lax.dynamic_update_slice_in_dim(jnp.zeros((width,), F32), values, group * span, 0)

    grad_gain_part = jnp.stack(
        [
            gain_one,
            grad_gain_moe,
            widen(jnp.sum(grad_qscaled * query_normed, axis=0)),
            widen(jnp.sum(grad_kscaled * key_normed, axis=0)),
        ]
    )
    last = jnp.concatenate(
        [
            jnp.swapaxes(grad_gain_part.reshape(4, count, rows), 0, 1).reshape(count, -1),
            grad_router_part.reshape(count, -1),
        ],
        axis=1,
    )
    last = grid.small_scatter(last.reshape(count, -1, 128 if last.shape[1] % 128 == 0 else 64))
    last = last.reshape(-1)
    grad_norm_gains = last[: 4 * rows].reshape(4, rows)
    grad_router = last[4 * rows :].reshape(rows, expert_count)
    return (
        block_out,
        input_grad,
        grad_in_projection,
        grad_out_projection,
        grad_router,
        grad_norm_gains,
        grad_expert_in,
        grad_expert_down,
    )


def solution(mesh):
    both = P(AXES, None)
    split = P("expert", "dp", None)
    in_specs = (both,) * 8 + (P(None, AXES), split, split)
    out_specs = (both,) * 5 + (P(None, AXES), split, split)
    return jax.shard_map(
        per_device, mesh=mesh, in_specs=in_specs, out_specs=out_specs, check_vma=False
    )
```

time: 2320 us -> 1540 us (0.66)
  waiting for transfers between devices: 1410 us -> 594 us
  blocking collectives: 464 us -> 0 us
  starting transfers between devices: 35.8 us -> 265 us
  Pallas kernels: 0 us -> 125 us
  other arithmetic: 44.7 us -> 117 us
  matrix products: 153 us -> 200 us
  local copies, waits for them, and re-layouts: 178 us -> 212 us
    all_to_all x7 -> x6, waiting for transfers between devices: 809 us -> 23.8 us  [exchange(): lax.all_to_all(value, 'expert', split_axis=0, concat_axis=0, tiled=True)]
    ppermute x0 -> x121, waiting for transfers between devices: none -> 570 us  [the longest x86 374 us: move(): return lax.ppermute(value, AXES, pairs)]
    reduce_scatter x2 -> x0, waiting for transfers between devices: 496 us -> none  [the longest x1 473 us: per_device(): lax.psum_scatter(grad_proj_part, ('dp', 'expert'), scatter_dimension=0, t...]
    all_gather x2 -> x0, blocking collectives: 344 us -> none  [the longest x1 219 us: per_device(): lax.all_gather(norm_gains, ('dp', 'expert'), axis=1, tiled=True)]
    ppermute x0 -> x121, starting transfers between devices: none -> 240 us  [the longest x86 155 us: move(): return lax.ppermute(value, AXES, pairs)]
    pallas_call x0 -> x6, Pallas kernels: none -> 125 us  [the longest x4 105 us: moe_rows(): pl.pallas_call(functools.partial(moe_kernel, ff, local), grid=(total // t...]
    all_to_all x1 -> x0, blocking collectives: 120 us -> none  [per_device(): lax.all_to_all(send_rows.reshape(dest_count, per_dest, width), ('dp', 'ex...]
    unnamed x8 -> x0, waiting for transfers between devices: 95.5 us -> none
  transfers between devices with their start and end apart: 13 -> 127, of which waited for: 10 -> 47; matrix products, arithmetic and copies ran while one was open for 11% -> 27% of each run, Pallas kernels for 0% -> 1%
where the time goes in v1:
time: 1540 us; the launch traced here: 1520 us
  waiting for transfers between devices  594 us (39%)
  starting transfers between devices  265 us (17%)
  local copies, waits for them, and re-layouts  212 us (14%)
  matrix products  200 us (13%)
  Pallas kernels  125 us (8%)
  other arithmetic  117 us (8%)
    ppermute x86, waiting for transfers between devices, move(): return lax.ppermute(value, AXES, pairs)  374 us
    dot_general x28, matrix products, dot(): return lax.dot_general(left, right, dims, preferred_element_type=F32)  187 us
    ppermute x86, starting transfers between devices, move(): return lax.ppermute(value, AXES, pairs)  155 us
    pallas_call x4, Pallas kernels, moe_rows(): pl.pallas_call(functools.partial(moe_kernel, ff, local), grid=(total // t...  105 us
    unnamed x278, local copies, waits for them, and re-layouts  84.7 us
    ppermute x7, waiting for transfers between devices, per_device(): piece = lax.ppermute(piece, 'dp', [(i, i ^ r) for i in range(dp)])  73.4 us
    ppermute x21, waiting for transfers between devices, flip(): return lax.ppermute(value, AXES, [(i, i ^ bit) for i in range(self.count)])  63.5 us
    ppermute x7, waiting for transfers between devices, per_device(): lax.ppermute(after(got, gone[-2]), 'dp', [(i, i ^ r) for i in range(dp)])  59.2 us
  transfers between devices with their start and end apart: 127, of which 47 were waited for; matrix products, arithmetic and copies ran while one was open for 27% of the time, Pallas kernels for 1%

profile of v1, /device:TPU:0, one launch (start us, length us, event | category | flops | bytes accessed | tf_op | source)
XLA Modules:
  0.0 1524.8 jit_solution(996121448505244531)
XLA Ops:
  186.2 20.3 %collective-permute-done.16 = bf16[2,64,2048]{2,1,0:T(8,128)(2,1)S(1)} collective-permute-done((bf16[2,64,2048]{2,1,0:T(8,128)(2,1)S(1)}, bf16[2,64,2048]{2,1,0:T(8,128)(2,1)S(1)}, u32[]{:S(2)}, u32[]{:S(2)}) %collective-permute-start.16) | collective-permute-done | bytes 524320 | tf_op jit(solution)/shard_map/ppermute | solution.py:102
  242.4 38.2 %collective-permute-done.24 = bf16[2,64,2048]{2,1,0:T(8,128)(2,1)} collective-permute-done((bf16[2,64,2048]{2,1,0:T(8,128)(2,1)}, bf16[2,64,2048]{2,1,0:T(8,128)(2,1)}, u32[]{:S(2)}, u32[]{:S(2)}) %collective-permute-start.24) | collective-permute-done | bytes 524320 | tf_op jit(solution)/shard_map/ppermute | solution.py:102
  343.5 20.9 %collective-permute-done.47 = bf16[128,2048]{1,0:T(8,128)(2,1)S(1)} collective-permute-done((bf16[128,2048]{1,0:T(8,128)(2,1)}, bf16[128,2048]{1,0:T(8,128)(2,1)S(1)}, u32[]{:S(2)}, u32[]{:S(2)}) %collective-permute-start.47) | collective-permute-done | bytes 524320 | tf_op jit(solution)/shard_map/ppermute | solution.py:102
  370.8 24.7 %collective-permute-done.28 = bf16[128,2048]{1,0:T(8,128)(2,1)S(1)} collective-permute-done((bf16[128,2048]{1,0:T(8,128)(2,1)S(1)}, bf16[128,2048]{1,0:T(8,128)(2,1)S(1)}, u32[]{:S(2)}, u32[]{:S(2)}) %collective-permute-start.28) | collective-permute-done | bytes 524320 | tf_op jit(solution)/shard_map/ppermute | solution.py:102
  399.0 39.4 %collective-permute-done.56 = bf16[256,2048]{1,0:T(8,128)(2,1)S(1)} collective-permute-done((bf16[256,2048]{1,0:T(8,128)(2,1)S(1)}, bf16[256,2048]{1,0:T(8,128)(2,1)S(1)}, u32[]{:S(2)}, u32[]{:S(2)}) %collective-permute-start.56) | collective-permute-done | bytes 1048608 | tf_op jit(solution)/shard_map/ppermute | solution.py:463
  467.0 19.3 %collective-permute-start.32 = (bf16[8,128,2048]{2,1,0:T(8,128)(2,1)}, bf16[8,128,2048]{2,1,0:T(8,128)(2,1)S(1)}, u32[]{:S(2)}, u32[]{:S(2)}) collective-permute-start(bf16[8,128,2048]{2,1,0:T(8,128)(2,1)} %get-tuple-element.214), channel_id=1, source_target_pairs={{0,1},{1,0},{2,3},{3,2},{4,5},{5,4},{6,7},{7,6},{8,9},{9,8},{10,11... | collective-permute-start | bytes 12582920 | tf_op jit(solution)/shard_map/ppermute | solution.py:102
  499.3 15.8 %collective-permute-start.53 = (bf16[8,128,2048]{2,1,0:T(8,128)(2,1)}, bf16[8,128,2048]{2,1,0:T(8,128)(2,1)S(1)}, u32[]{:S(2)}, u32[]{:S(2)}) collective-permute-start(bf16[8,128,2048]{2,1,0:T(8,128)(2,1)} %get-tuple-element.196), channel_id=1, source_target_pairs={{0,1},{1,0},{2,3},{3,2},{4,5},{5,4},{6,7},{7,6},{8,9},{9,8},{10,11... | collective-permute-start | bytes 12582920 | tf_op jit(solution)/shard_map/ppermute | solution.py:102
  529.7 19.8 %collective-permute-done.59 = bf16[256,2048]{1,0:T(8,128)(2,1)S(1)} collective-permute-done((bf16[256,2048]{1,0:T(8,128)(2,1)S(1)}, bf16[256,2048]{1,0:T(8,128)(2,1)S(1)}, u32[]{:S(2)}, u32[]{:S(2)}) %collective-permute-start.59) | collective-permute-done | bytes 1048608 | tf_op jit(solution)/shard_map/ppermute | solution.py:463
  586.0 22.5 %fusion.128.lift_ref = f32[4096,1024]{1,0:T(8,128)} fusion(bf16[4096,2048]{1,0:T(8,128)(2,1)} %bitcast.502, bf16[1024,2048]{1,0:T(8,128)(2,1)S(1)} %bitcast.511), kind=kOutput, calls=%fused_computation.459 | convolution fusion | flops 17179869184 | bytes 37748736 | tf_op jit(solution)/shard_map/dot_general | solution.py:24
  625.8 26.7 %shard_map.270 = (bf16[1024,2048]{1,0:T(8,128)(2,1)}, bf16[1024,1024]{1,0:T(8,128)(2,1)}, f32[1024,8]{1,0:T(8,128)}, f32[1024,2048]{1,0:T(8,128)}) custom-call(bf16[4096,2048]{1,0:T(8,128)(2,1)} %bitcast.50.x_ref, f32[4096,1024]{1,0:T(8,128)} %fusion.128.lift_ref, f32[4096,8]{1,0:T(8,128)} %fusion.9.gate_ref, bf16[2048,2048]{1,0:T(8,128)(2,1)} %copy-done.32), custom_call_target="tpu_custom_call" | custom-call | flops 17179869184 | bytes 25165824 | tf_op jit(solution)/shard_map/pallas_call | solution.py:267
  652.5 25.9 %shard_map.271 = (bf16[1024,2048]{1,0:T(8,128)(2,1)}, bf16[1024,1024]{1,0:T(8,128)(2,1)}, f32[1024,8]{1,0:T(8,128)}, bf16[1024,2048]{1,0:T(8,128)(2,1)}) custom-call(bf16[4096,2048]{1,0:T(8,128)(2,1)} %bitcast.50.x_ref, f32[4096,1024]{1,0:T(8,128)} %fusion.128.lift_ref, f32[4096,8]{1,0:T(8,128)} %fusion.9.gate_ref, bf16[2048,2048]{1,0:T(8,128)(2,1)} %copy-done.32), custom_call_target="tpu_custom_call" | custom-call | flops 17179869184 | bytes 25165824 | tf_op jit(solution)/shard_map/pallas_call | solution.py:267
  678.4 26.7 %shard_map.272 = (bf16[1024,2048]{1,0:T(8,128)(2,1)}, bf16[1024,1024]{1,0:T(8,128)(2,1)}, f32[1024,8]{1,0:T(8,128)}, f32[1024,2048]{1,0:T(8,128)}) custom-call(bf16[4096,2048]{1,0:T(8,128)(2,1)} %bitcast.50.x_ref, f32[4096,1024]{1,0:T(8,128)} %fusion.128.lift_ref, f32[4096,8]{1,0:T(8,128)} %fusion.9.gate_ref, bf16[2048,2048]{1,0:T(8,128)(2,1)} %copy-done.32), custom_call_target="tpu_custom_call" | custom-call | flops 17179869184 | bytes 25165824 | tf_op jit(solution)/shard_map/pallas_call | solution.py:267
  705.1 26.1 %shard_map.273 = (bf16[1024,2048]{1,0:T(8,128)(2,1)}, bf16[1024,1024]{1,0:T(8,128)(2,1)}, f32[1024,8]{1,0:T(8,128)}, bf16[1024,2048]{1,0:T(8,128)(2,1)}) custom-call(bf16[4096,2048]{1,0:T(8,128)(2,1)} %bitcast.50.x_ref, f32[4096,1024]{1,0:T(8,128)} %fusion.128.lift_ref, f32[4096,8]{1,0:T(8,128)} %fusion.9.gate_ref, bf16[2048,2048]{1,0:T(8,128)(2,1)} %copy-done.32), custom_call_target="tpu_custom_call" | custom-call | flops 17179869184 | bytes 25165824 | tf_op jit(solution)/shard_map/pallas_call | solution.py:267
  802.3 24.5 %fusion.130 = f32[8,128,2048]{2,1,0:T(8,128)} fusion(bf16[8,128,4096]{2,1,0:T(8,128)(2,1)} %bitcast.443, bf16[4096,2048,1]{1,0,2:T(8,128)(2,1)} %bitcast.503), kind=kOutput, calls=%fused_computation.461 | convolution fusion | flops 17179869184 | bytes 33554432 | tf_op jit(solution)/shard_map/dot_general | solution.py:24
  871.8 35.7 %collective-permute-start.119 = (bf16[256,2048]{1,0:T(8,128)(2,1)S(1)}, bf16[256,2048]{1,0:T(8,128)(2,1)S(1)}, u32[]{:S(2)}, u32[]{:S(2)}) collective-permute-start(bf16[256,2048]{1,0:T(8,128)(2,1)S(1)} %convolution_convert_fusion.6), channel_id=1, source_target_pairs={{0,16},{4,20},{8,24},{12,28},{16,0},{20,4},{24,8},{28,12},{1,17},{... | collective-permute-start | bytes 3145736 | tf_op jit(solution)/shard_map/ppermute | solution.py:540
  907.5 44.1 %collective-permute-done.115.refs_5_ = bf16[256,2048]{1,0:T(8,128)(2,1)S(1)} collective-permute-done((bf16[256,2048]{1,0:T(8,128)(2,1)S(1)}, bf16[256,2048]{1,0:T(8,128)(2,1)S(1)}, u32[]{:S(2)}, u32[]{:S(2)}) %collective-permute-start.115) | collective-permute-done | bytes 1048608 | tf_op jit(solution)/shard_map/ppermute | solution.py:540
  958.3 15.2 collective-permute-done.119.refs_4_
  1065.1 14.3 collective-permute-done.76
  1082.8 34.2 %collective-permute-done.62 = bf16[2,2,128,2048]{3,2,1,0:T(8,128)(2,1)S(1)} collective-permute-done((bf16[2,2,128,2048]{3,2,1,0:T(8,128)(2,1)}, bf16[2,2,128,2048]{3,2,1,0:T(8,128)(2,1)S(1)}, u32[]{:S(2)}, u32[]{:S(2)}) %collective-permute-start.62) | collective-permute-done | bytes 2097184 | tf_op jit(solution)/shard_map/ppermute | solution.py:102
  1119.0 31.7 %collective-permute-done.65 = bf16[2,2,128,2048]{3,2,1,0:T(8,128)(2,1)S(1)} collective-permute-done((bf16[2,2,128,2048]{3,2,1,0:T(8,128)(2,1)}, bf16[2,2,128,2048]{3,2,1,0:T(8,128)(2,1)S(1)}, u32[]{:S(2)}, u32[]{:S(2)}) %collective-permute-start.65) | collective-permute-done | bytes 2097184 | tf_op jit(solution)/shard_map/ppermute | solution.py:102
  1329.9 28.8 %collective-permute-done.92 = bf16[2,256,1536]{2,1,0:T(8,128)(2,1)} collective-permute-done((bf16[2,256,1536]{2,1,0:T(8,128)(2,1)}, bf16[2,256,1536]{2,1,0:T(8,128)(2,1)}, u32[]{:S(2)}, u32[]{:S(2)}) %collective-permute-start.92) | collective-permute-done | bytes 1572896 | tf_op jit(solution)/shard_map/ppermute | solution.py:102
  1384.3 30.7 %collective-permute-done.110 = f32[8,18,128]{2,1,0:T(8,128)S(1)} collective-permute-done((f32[8,18,128]{2,1,0:T(8,128)S(1)}, f32[8,18,128]{2,1,0:T(8,128)S(1)}, u32[]{:S(2)}, u32[]{:S(2)}) %collective-permute-start.110) | collective-permute-done | bytes 73760 | tf_op jit(solution)/shard_map/ppermute | solution.py:202
  1426.9 18.6 %collective-permute-done.112 = f32[2,18,128]{2,1,0:T(8,128)S(1)} collective-permute-done((f32[2,18,128]{2,1,0:T(8,128)S(1)}, f32[2,18,128]{2,1,0:T(8,128)S(1)}, u32[]{:S(2)}, u32[]{:S(2)}) %collective-permute-start.112) | collective-permute-done | bytes 18464 | tf_op jit(solution)/shard_map/ppermute | solution.py:202
  1449.4 16.7 %collective-permute-done.99 = bf16[2,2,64,2048]{3,2,1,0:T(8,128)(2,1)S(1)} collective-permute-done((bf16[2,2,64,2048]{3,2,1,0:T(8,128)(2,1)S(1)}, bf16[2,2,64,2048]{3,2,1,0:T(8,128)(2,1)S(1)}, u32[]{:S(2)}, u32[]{:S(2)}) %collective-permute-start.99) | collective-permute-done | bytes 1048608 | tf_op jit(solution)/shard_map/ppermute | solution.py:102
  (844 shorter events, 893.0 us)
Async XLA Ops:
  156.2 171.4 %collective-permute-start.46 = (bf16[128,2048]{1,0:T(8,128)(2,1)}, bf16[128,2048]{1,0:T(8,128)(2,1)}, u32[]{:S(2)}, u32[]{:S(2)}) collective-permute-start(bf16[128,2048]{1,0:T(8,128)(2,1)} %param.26), channel_id=1, source_target_pairs={{8,16},{9,17},{10,18},{11,19},{12,20},{13,21},{14,22},{15,23},{16,... | collective-permute-start | bytes 1572872 | tf_op jit(solution)/shard_map/ppermute | solution.py:102
  230.1 135.2 %collective-permute-start.54 = (bf16[256,2048]{1,0:T(8,128)(2,1)}, bf16[256,2048]{1,0:T(8,128)(2,1)}, u32[]{:S(2)}, u32[]{:S(2)}) collective-permute-start(bf16[256,2048]{1,0:T(8,128)(2,1)} %get-tuple-element.55), channel_id=1, source_target_pairs={{0,28},{4,24},{8,20},{12,16},{16,12},{20,8},{24,4},{28,0},{1,29},{... | collective-permute-start | bytes 3145736 | tf_op jit(solution)/shard_map/ppermute | solution.py:463
  335.0 132.0 %collective-permute-start.45 = (bf16[8,128,2048]{2,1,0:T(8,128)(2,1)}, bf16[8,128,2048]{2,1,0:T(8,128)(2,1)S(1)}, u32[]{:S(2)}, u32[]{:S(2)}) collective-permute-start(bf16[8,128,2048]{2,1,0:T(8,128)(2,1)} %get-tuple-element.202), channel_id=1, source_target_pairs={{0,1},{1,0},{2,3},{3,2},{4,5},{5,4},{6,7},{7,6},{8,9},{9,8},{10,11... | collective-permute-start | bytes 12582920 | tf_op jit(solution)/shard_map/ppermute | solution.py:102
  365.2 73.2 %collective-permute-start.56 = (bf16[256,2048]{1,0:T(8,128)(2,1)S(1)}, bf16[256,2048]{1,0:T(8,128)(2,1)S(1)}, u32[]{:S(2)}, u32[]{:S(2)}) collective-permute-start(bf16[256,2048]{1,0:T(8,128)(2,1)S(1)} %copy-done.6), channel_id=1, source_target_pairs={{0,20},{4,16},{8,28},{12,24},{16,4},{20,0},{24,12},{28,8},{1,21},{... | collective-permute-start | bytes 3145736 | tf_op jit(solution)/shard_map/ppermute | solution.py:463
  369.5 129.8 %collective-permute-start.57 = (bf16[256,2048]{1,0:T(8,128)(2,1)S(1)}, bf16[256,2048]{1,0:T(8,128)(2,1)S(1)}, u32[]{:S(2)}, u32[]{:S(2)}) collective-permute-start(bf16[256,2048]{1,0:T(8,128)(2,1)S(1)} %copy-done.4), channel_id=1, source_target_pairs={{0,16},{4,20},{8,24},{12,28},{16,0},{20,4},{24,8},{28,12},{1,17},{... | collective-permute-start | bytes 3145736 | tf_op jit(solution)/shard_map/ppermute | solution.py:463
  467.0 91.0 %collective-permute-start.32 = (bf16[8,128,2048]{2,1,0:T(8,128)(2,1)}, bf16[8,128,2048]{2,1,0:T(8,128)(2,1)S(1)}, u32[]{:S(2)}, u32[]{:S(2)}) collective-permute-start(bf16[8,128,2048]{2,1,0:T(8,128)(2,1)} %get-tuple-element.214), channel_id=1, source_target_pairs={{0,1},{1,0},{2,3},{3,2},{4,5},{5,4},{6,7},{7,6},{8,9},{9,8},{10,11... | collective-permute-start | bytes 12582920 | tf_op jit(solution)/shard_map/ppermute | solution.py:102
  499.3 83.0 %collective-permute-start.53 = (bf16[8,128,2048]{2,1,0:T(8,128)(2,1)}, bf16[8,128,2048]{2,1,0:T(8,128)(2,1)S(1)}, u32[]{:S(2)}, u32[]{:S(2)}) collective-permute-start(bf16[8,128,2048]{2,1,0:T(8,128)(2,1)} %get-tuple-element.196), channel_id=1, source_target_pairs={{0,1},{1,0},{2,3},{3,2},{4,5},{5,4},{6,7},{7,6},{8,9},{9,8},{10,11... | collective-permute-start | bytes 12582920 | tf_op jit(solution)/shard_map/ppermute | solution.py:102
  779.9 74.8 %collective-permute-start.114 = (bf16[256,2048]{1,0:T(8,128)(2,1)}, bf16[256,2048]{1,0:T(8,128)(2,1)S(1)}, u32[]{:S(2)}, u32[]{:S(2)}) collective-permute-start(bf16[256,2048]{1,0:T(8,128)(2,1)} %convolution_convert_fusion.8), channel_id=1, source_target_pairs={{0,28},{4,24},{8,20},{12,16},{16,12},{20,8},{24,4},{28,0},{1,29},{... | collective-permute-start | bytes 3145736 | tf_op jit(solution)/shard_map/ppermute | solution.py:540
  782.2 89.5 %collective-permute-start.118 = (bf16[256,2048]{1,0:T(8,128)(2,1)}, bf16[256,2048]{1,0:T(8,128)(2,1)}, u32[]{:S(2)}, u32[]{:S(2)}) collective-permute-start(bf16[256,2048]{1,0:T(8,128)(2,1)} %convolution_convert_fusion.5), channel_id=1, source_target_pairs={{0,24},{4,28},{8,16},{12,20},{16,8},{20,12},{24,0},{28,4},{1,25},{... | collective-permute-start | bytes 3145736 | tf_op jit(solution)/shard_map/ppermute | solution.py:540
  853.5 146.2 %collective-permute-start.72 = (bf16[8,128,2048]{2,1,0:T(8,128)(2,1)}, bf16[8,128,2048]{2,1,0:T(8,128)(2,1)}, u32[]{:S(2)}, u32[]{:S(2)}) collective-permute-start(bf16[8,128,2048]{2,1,0:T(8,128)(2,1)} %bitcast.517), channel_id=1, source_target_pairs={{0,1},{1,0},{2,3},{3,2},{4,5},{5,4},{6,7},{7,6},{8,9},{9,8},{10,11... | collective-permute-start | bytes 12582920 | tf_op jit(solution)/shard_map/ppermute | solution.py:102
  853.5 158.1 %collective-permute-start.75 = (bf16[8,128,2048]{2,1,0:T(8,128)(2,1)}, bf16[8,128,2048]{2,1,0:T(8,128)(2,1)}, u32[]{:S(2)}, u32[]{:S(2)}) collective-permute-start(bf16[8,128,2048]{2,1,0:T(8,128)(2,1)} %bitcast.516), channel_id=1, source_target_pairs={{0,1},{1,0},{2,3},{3,2},{4,5},{5,4},{6,7},{7,6},{8,9},{9,8},{10,11... | collective-permute-start | bytes 12582920 | tf_op jit(solution)/shard_map/ppermute | solution.py:102
  854.8 96.9 %collective-permute-start.115 = (bf16[256,2048]{1,0:T(8,128)(2,1)S(1)}, bf16[256,2048]{1,0:T(8,128)(2,1)S(1)}, u32[]{:S(2)}, u32[]{:S(2)}) collective-permute-start(bf16[256,2048]{1,0:T(8,128)(2,1)S(1)} %convolution_convert_fusion.9), channel_id=1, source_target_pairs={{0,20},{4,16},{8,28},{12,24},{16,4},{20,0},{24,12},{28,8},{1,21},{... | collective-permute-start | bytes 3145736 | tf_op jit(solution)/shard_map/ppermute | solution.py:540
  871.7 152.6 %collective-permute-start.61 = (bf16[8,128,2048]{2,1,0:T(8,128)(2,1)}, bf16[8,128,2048]{2,1,0:T(8,128)(2,1)}, u32[]{:S(2)}, u32[]{:S(2)}) collective-permute-start(bf16[8,128,2048]{2,1,0:T(8,128)(2,1)} %convolution_convert_fusion.1), channel_id=1, source_target_pairs={{0,1},{1,0},{2,3},{3,2},{4,5},{5,4},{6,7},{7,6},{8,9},{9,8},{10,11... | collective-permute-start | bytes 12582920 | tf_op jit(solution)/shard_map/ppermute | solution.py:102
  871.8 101.7 %collective-permute-start.119 = (bf16[256,2048]{1,0:T(8,128)(2,1)S(1)}, bf16[256,2048]{1,0:T(8,128)(2,1)S(1)}, u32[]{:S(2)}, u32[]{:S(2)}) collective-permute-start(bf16[256,2048]{1,0:T(8,128)(2,1)S(1)} %convolution_convert_fusion.6), channel_id=1, source_target_pairs={{0,16},{4,20},{8,24},{12,28},{16,0},{20,4},{24,8},{28,12},{1,17},{... | collective-permute-start | bytes 3145736 | tf_op jit(solution)/shard_map/ppermute | solution.py:540
  957.8 78.9 %collective-permute-start.64 = (bf16[8,128,2048]{2,1,0:T(8,128)(2,1)}, bf16[8,128,2048]{2,1,0:T(8,128)(2,1)}, u32[]{:S(2)}, u32[]{:S(2)}) collective-permute-start(bf16[8,128,2048]{2,1,0:T(8,128)(2,1)} %convolution_convert_fusion), channel_id=1, source_target_pairs={{0,1},{1,0},{2,3},{3,2},{4,5},{5,4},{6,7},{7,6},{8,9},{9,8},{10,11... | collective-permute-start | bytes 12582920 | tf_op jit(solution)/shard_map/ppermute | solution.py:102
  1048.1 68.9 %collective-permute-start.62 = (bf16[2,2,128,2048]{3,2,1,0:T(8,128)(2,1)}, bf16[2,2,128,2048]{3,2,1,0:T(8,128)(2,1)S(1)}, u32[]{:S(2)}, u32[]{:S(2)}) collective-permute-start(bf16[2,2,128,2048]{3,2,1,0:T(8,128)(2,1)} %bitcast.67), channel_id=1, source_target_pairs={{0,2},{1,5},{2,0},{3,7},{4,6},{5,1},{6,4},{7,3},{8,10},{9,13},{10,... | collective-permute-start | bytes 6291464 | tf_op jit(solution)/shard_map/ppermute | solution.py:102
  1049.1 101.6 %collective-permute-start.65 = (bf16[2,2,128,2048]{3,2,1,0:T(8,128)(2,1)}, bf16[2,2,128,2048]{3,2,1,0:T(8,128)(2,1)S(1)}, u32[]{:S(2)}, u32[]{:S(2)}) collective-permute-start(bf16[2,2,128,2048]{3,2,1,0:T(8,128)(2,1)} %bitcast.74), channel_id=1, source_target_pairs={{0,2},{1,5},{2,0},{3,7},{4,6},{5,1},{6,4},{7,3},{8,10},{9,13},{10,... | collective-permute-start | bytes 6291464 | tf_op jit(solution)/shard_map/ppermute | solution.py:102
  1064.1 106.9 %collective-permute-start.74 = (bf16[2,128,2048]{2,1,0:T(8,128)(2,1)S(1)}, bf16[2,128,2048]{2,1,0:T(8,128)(2,1)S(1)}, u32[]{:S(2)}, u32[]{:S(2)}) collective-permute-start(bf16[2,128,2048]{2,1,0:T(8,128)(2,1)S(1)} %fusion.35), channel_id=1, source_target_pairs={{0,4},{1,3},{2,6},{3,1},{4,0},{5,7},{6,2},{7,5},{8,12},{9,11},{10,... | collective-permute-start | bytes 3145736 | tf_op jit(solution)/shard_map/ppermute | solution.py:102
  1082.2 70.6 %collective-permute-start.77 = (bf16[2,128,2048]{2,1,0:T(8,128)(2,1)S(1)}, bf16[2,128,2048]{2,1,0:T(8,128)(2,1)S(1)}, u32[]{:S(2)}, u32[]{:S(2)}) collective-permute-start(bf16[2,128,2048]{2,1,0:T(8,128)(2,1)S(1)} %fusion.36), channel_id=1, source_target_pairs={{0,4},{1,3},{2,6},{3,1},{4,0},{5,7},{6,2},{7,5},{8,12},{9,11},{10,... | collective-permute-start | bytes 3145736 | tf_op jit(solution)/shard_map/ppermute | solution.py:102
  1118.1 88.1 %collective-permute-start.63 = (bf16[2,128,2048]{2,1,0:T(8,128)(2,1)S(1)}, bf16[2,128,2048]{2,1,0:T(8,128)(2,1)S(1)}, u32[]{:S(2)}, u32[]{:S(2)}) collective-permute-start(bf16[2,128,2048]{2,1,0:T(8,128)(2,1)S(1)} %fusion.33), channel_id=1, source_target_pairs={{0,4},{1,3},{2,6},{3,1},{4,0},{5,7},{6,2},{7,5},{8,12},{9,11},{10,... | collective-permute-start | bytes 3145736 | tf_op jit(solution)/shard_map/ppermute | solution.py:102
  1206.6 172.2 %collective-permute-start.68 = (bf16[128,2048]{1,0:T(8,128)(2,1)}, bf16[128,2048]{1,0:T(8,128)(2,1)}, u32[]{:S(2)}, u32[]{:S(2)}) collective-permute-start(bf16[128,2048]{1,0:T(8,128)(2,1)} %get-tuple-element.180), channel_id=1, source_target_pairs={{8,16},{9,17},{10,18},{11,19},{12,20},{13,21},{14,22},{15,23},{16,... | collective-permute-start | bytes 1572872 | tf_op jit(solution)/shard_map/ppermute | solution.py:102
  1209.0 171.4 %collective-permute-start.71 = (bf16[128,2048]{1,0:T(8,128)(2,1)}, bf16[128,2048]{1,0:T(8,128)(2,1)}, u32[]{:S(2)}, u32[]{:S(2)}) collective-permute-start(bf16[128,2048]{1,0:T(8,128)(2,1)} %fusion.51), channel_id=1, source_target_pairs={{0,8},{1,9},{2,10},{3,11},{4,12},{5,13},{6,14},{7,15},{8,0},{9,1},... | collective-permute-start | bytes 1572872 | tf_op jit(solution)/shard_map/ppermute | solution.py:102
  1298.4 122.6 %collective-permute-start.98 = (bf16[8,64,2048]{2,1,0:T(8,128)(2,1)}, bf16[8,64,2048]{2,1,0:T(8,128)(2,1)}, u32[]{:S(2)}, u32[]{:S(2)}) collective-permute-start(bf16[8,64,2048]{2,1,0:T(8,128)(2,1)} %bitcast.131), channel_id=1, source_target_pairs={{0,1},{1,0},{2,3},{3,2},{4,5},{5,4},{6,7},{7,6},{8,9},{9,8},{10,11... | collective-permute-start | bytes 6291464 | tf_op jit(solution)/shard_map/ppermute | solution.py:102
  1325.3 90.7 %collective-permute-start.101 = (bf16[8,64,2048]{2,1,0:T(8,128)(2,1)}, bf16[8,64,2048]{2,1,0:T(8,128)(2,1)}, u32[]{:S(2)}, u32[]{:S(2)}) collective-permute-start(bf16[8,64,2048]{2,1,0:T(8,128)(2,1)} %bitcast.457), channel_id=1, source_target_pairs={{0,1},{1,0},{2,3},{3,2},{4,5},{5,4},{6,7},{7,6},{8,9},{9,8},{10,11... | collective-permute-start | bytes 6291464 | tf_op jit(solution)/shard_map/ppermute | solution.py:102
  (230 other events, 5361.0 us)

commit v2 on v1

--- a/solution.py
+++ b/solution.py
@@ -25,7 +25,27 @@
 
 
 def after(value, *others):
-    return lax.optimization_barrier((value,) + others)[0]
+    return lax.optimization_barrier((value,) + others)[0] if others else value
+
+
+class Flow:
+    def __init__(self, steps):
+        self.steps, self.hops, self.result = steps, [], None
+        next(steps)
+
+    def go(self, *events):
+        if self.result is not None:
+            return
+        try:
+            self.hops.append(self.steps.send(events))
+        except StopIteration as stop:
+            self.result = stop.value
+            assert self.result is not None
+
+    def finish(self):
+        while self.result is None:
+            self.go()
+        return self.result
 
 
 def normalize(tensor):
@@ -61,13 +81,13 @@
 
 
 class Grid:
-    def __init__(self, swap=True):
+    def __init__(self):
         self.dp = lax.axis_size("dp")
         self.ex = lax.axis_size("expert")
         self.count = self.dp * self.ex
         self.size = {"z": 4, "y": self.dp // 4, "x": self.ex // 2, "c": 2}
-        self.swap = swap and self.size["x"] == self.size["y"]
         self.size["A"], self.size["B"] = self.size["y"], self.size["x"]
+        self.swap = self.size["x"] == self.size["y"]
         d, e = lax.axis_index("dp"), lax.axis_index("expert")
         self.linear = d * self.ex + e
         ny = self.size["y"]
@@ -101,11 +121,11 @@
                 pairs.append((i, self.index({**here, line: moves[here[line]]})))
         return lax.ppermute(value, AXES, pairs)
 
-    def position(self, axis):
+    def middle(self, axis):
+        at = self.at[self.real(axis, 0)]
         if axis in "AB" and self.swap:
-            other = self.real(axis, 1)
-            return jnp.where(self.at["c"] == 0, self.at[self.real(axis, 0)], self.at[other])
-        return self.at[self.real(axis, 0)]
+            at = jnp.where(self.at["c"] == 0, at, self.at[self.real(axis, 1)])
+        return (at == 1) | (at == 2)
 
     def slots(self, axis):
         n = self.size[axis]
@@ -118,10 +138,8 @@
 
     def sources(self):
         c, y, x, z = [self.slots(a) for a in "cyxz"]
-        z = z.reshape(2, 1, 1, 1, 2)
-        c = c.reshape(1, -1, 1, 1, 1)
-        along_a = (1, 1, 1, -1, 1)
-        along_b = (1, 1, -1, 1, 1)
+        z, c = z.reshape(2, 1, 1, 1, 2), c.reshape(1, -1, 1, 1, 1)
+        along_b, along_a = (1, 1, -1, 1, 1), (1, 1, 1, -1, 1)
         xs, ys = x.reshape(along_b), y.reshape(along_a)
         if self.swap:
             xs = jnp.where(c == 0, xs, x.reshape(along_a))
@@ -141,12 +159,12 @@
             return [value, pair]
         m0, m1 = self.move(value, axis, "mid"), self.move(pair, axis, "mid")
         o0, o1 = self.move(m0, axis, "out"), self.move(m1, axis, "out")
-        at = self.position(axis)
-        mid = (at == 1) | (at == 2)
+        mid = self.middle(axis)
         return [value, pair, jnp.where(mid, m0, o0), jnp.where(mid, m1, o1)]
 
     def line_reduce(self, slots, axis, kind=BF16):
         n = self.size[axis]
+        slots = [slots[0].astype(F32)] + list(slots[1:])
 
         def sent(value, *way):
             return self.move(value.astype(kind), axis, *way).astype(F32)
@@ -159,44 +177,122 @@
         m2 = sent(slots[2] + sent(slots[2], "in"), "mid")
         return slots[0] + m2 + sent(slots[1] + m3)
 
+    def z_hops(self, value, events):
+        value = after(value, *events)
+        pair, m0 = self.move(value, "z"), self.move(value, "z", "mid")
+        events = yield (pair, m0)
+        pair, m0 = after((pair, m0), *events)
+        m1, o0 = self.move(pair, "z", "mid"), self.move(m0, "z", "out")
+        events = yield (m1, o0)
+        mid = self.middle("z")
+        near = jnp.stack([value, pair])
+        m1, near = after((m1, near), *events)
+        o1 = self.move(m1, "z", "out")
+        return near, lambda o1: jnp.stack([jnp.where(mid, m0, o0), jnp.where(mid, m1, o1)]), o1
+
     def gather(self, value):
-        pieces = self.line_gather(value, "z")
-        out = []
-        for h in range(2):
-            near = jnp.stack(pieces[2 * h : 2 * h + 2])
-            table = [self.line_gather(a, "B") for a in self.line_gather(near, "A")]
-            block = jnp.concatenate([row[b] for b in range(self.size["B"]) for row in table])
-            out += self.line_gather(block, "c")
-        return out
-
-    def scatter(self, groups):
-        halves = [None, None]
-        for h in (1, 0):
-            total = self.line_reduce(groups[2 * h : 2 * h + 2], "c")
-            nb, na = self.size["B"], self.size["A"]
-            total = total.reshape((nb, na, 2) + total.shape[1:])
-            total = self.line_reduce([total[i] for i in range(nb)], "B")
-            halves[h] = self.line_reduce([total[i] for i in range(na)], "A")
-        return self.line_reduce([halves[0][0], halves[0][1], halves[1][0], halves[1][1]], "z")
+        events = yield
+        near, far, o1 = yield from self.z_hops(value, events)
+        na = self.line_gather(near, "A")
+        events = yield (o1, *na[1:])
+        o1, na = after((o1, na), *events)
+        fa, nb = self.line_gather(far(o1), "A"), [self.line_gather(na[0], "B")]
+        events = yield (*fa[1:], *nb[0][1:])
+        na, fa = after((na, fa), *events)
+        nb += [self.line_gather(v, "B") for v in na[1:]]
+        fb = [self.line_gather(fa[0], "B")]
+        events = yield (*nb[1][1:], *fb[0][1:])
+        nb, fa = after((nb, fa), *events)
+        fb += [self.line_gather(v, "B") for v in fa[1:]]
+        count = self.size["B"]
+        block = jnp.concatenate([row[i] for i in range(count) for row in nb])
+        nc = self.line_gather(block, "c")
+        events = yield (*fb[1][1:], *nc[1:])
+        fb = after(fb, *events)
+        block = jnp.concatenate([row[i] for i in range(count) for row in fb])
+        return nc + self.line_gather(block, "c")
+
+    def lines(self, total):
+        return [total[i] for i in range(total.shape[0])]
+
+    def z_sum(self, near, far, events):
+        def sent(value, way="pair"):
+            return self.move(value.astype(BF16), "z", way)
+
+        near, far = after((near, far), *events)
+        o3, o2 = sent(far[1], "in"), sent(far[0], "in")
+        events = yield (o3, o2)
+        far, o3, o2 = after((far, o3, o2), *events)
+        m3, m2 = sent(far[1] + o3.astype(F32), "mid"), sent(far[0] + o2.astype(F32), "mid")
+        events = yield (m3, m2)
+        near, m3, m2 = after((near, m3, m2), *events)
+        pair = sent(near[1] + m3.astype(F32))
+        events = yield (pair,)
+        return near[0] + m2.astype(F32) + after(pair, *events).astype(F32)
+
+    def unfold(self, total):
+        return total.reshape((self.size["B"], self.size["A"], 2) + total.shape[1:])
+
+    def scatter(self, groups, kind=F32):
+        events = yield
+        far, near = after((groups[2:], groups[:2]), *events)
+        far = self.unfold(self.line_reduce(far, "c").astype(kind))
+        near = self.unfold(self.line_reduce(near, "c").astype(kind))
+        for axis in "BA":
+            events = yield (far, near)
+            far, near = after((far, near), *events)
+            far = self.line_reduce(self.lines(far), axis).astype(kind)
+            near = self.line_reduce(self.lines(near), axis).astype(kind)
+        events = yield (far, near)
+        return (yield from self.z_sum(near, far, events))
+
+    def scatter_early(self, groups, late):
+        yield
+        far = self.unfold(self.line_reduce(groups[2:], "c"))
+        yield (far,)
+        far = self.line_reduce(self.lines(far), "B")
+        yield (far,)
+        far = self.line_reduce(self.lines(far), "A")
+        near = self.unfold(self.line_reduce(late(), "c"))
+        events = yield (far, near)
+        near = self.line_reduce(self.lines(after(near, *events)), "B")
+        o3, o2 = self.move(far[1].astype(BF16), "z", "in"), self.move(far[0].astype(BF16), "z", "in")
+        events = yield (near, o3, o2)
+        near, o3, o2 = after((near, o3, o2), *events)
+        near = self.line_reduce(self.lines(near), "A")
+        m3 = self.move((far[1] + o3.astype(F32)).astype(BF16), "z", "mid")
+        m2 = self.move((far[0] + o2.astype(F32)).astype(BF16), "z", "mid")
+        events = yield (near, m3, m2)
+        near, m3, m2 = after((near, m3, m2), *events)
+        pair = self.move((near[1] + m3.astype(F32)).astype(BF16), "z")
+        events = yield (pair,)
+        return near[0] + m2.astype(F32) + after(pair, *events).astype(F32)
 
     def dp_gather(self, value):
-        pieces = self.line_gather(value, "z")
+        events = yield
+        near, far, o1 = yield from self.z_hops(value, events)
+        ny = self.line_gather(near, "y")
+        events = yield (o1, *ny[1:])
+        fy = self.line_gather(far(after(o1, *events)), "y")
+        events = yield (*fy[1:],)
         z, y = self.slots("z"), self.slots("y")
         n = value.shape[0]
         whole = jnp.zeros((n * self.dp,) + value.shape[1:], value.dtype)
-        for h in range(2):
-            near = jnp.stack(pieces[2 * h : 2 * h + 2])
-            for j, got in enumerate(self.line_gather(near, "y")):
+        for h, line in enumerate((ny, fy)):
+            for j, got in enumerate(line):
                 for k in range(2):
                     place = (z[2 * h + k] * self.size["y"] + y[j]) * n
                     whole = lax.dynamic_update_slice_in_dim(whole, got[k], place, 0)
-        return whole, pieces[3]
+        return whole
 
     def dp_scatter(self, halves):
-        sums = [None, None]
-        for h in (1, 0):
-            sums[h] = self.line_reduce([halves[h][i] for i in range(self.size["y"])], "y")
-        return self.line_reduce([sums[0][0], sums[0][1], sums[1][0], sums[1][1]], "z")
+        events = yield
+        near, far = after(halves, *events)
+        far = self.line_reduce(self.lines(far), "y")
+        events = yield (far,)
+        far, near = after((far, near), *events)
+        near = self.line_reduce(self.lines(near), "y")
+        return (yield from self.z_sum(near, far, ()))
 
     def flip(self, value, bit):
         return lax.ppermute(value, AXES, [(i, i ^ bit) for i in range(self.count)])
@@ -204,6 +300,8 @@
     def small_gather(self, value):
         held, bit = value[None], 1
         while bit < self.count:
+            events = yield (held,)
+            held = after(held, *events)
             held = jnp.concatenate([held, self.flip(held, bit)])
             bit *= 2
         return held[self.linear ^ jnp.arange(self.count)]
@@ -287,72 +385,66 @@
     )(x, lifted, gates, weight)
 
 
-def deal_kernel(dp, stage_ref, in_ref, *out_refs):
-    for r in range(dp):
-        place = pl.multiple_of(lax.bitwise_xor(stage_ref[0], r) * 128, 128)
-        out_refs[r][...] = in_ref[0, :, pl.ds(place, 128)]
-
-
-def deal(expert_in, stage, dp):
+def deal_kernel(dp, in_ref, out_ref):
+    for p in range(dp):
+        out_ref[p] = in_ref[0, :, 128 * p : 128 * (p + 1)]
+
+
+def deal(expert_in, dp):
     local, rows, wide = expert_in.shape
-    half = wide // 2
     return pl.pallas_call(
         functools.partial(deal_kernel, dp),
-        grid_spec=pltpu.PrefetchScalarGridSpec(
-            num_scalar_prefetch=1,
-            grid=(local, 2),
-            in_specs=[pl.BlockSpec((1, rows, half), lambda e, g, s: (e, 0, g))],
-            out_specs=[pl.BlockSpec((rows, 128), lambda e, g, s: (0, 2 * e + g))] * dp,
-        ),
-        out_shape=[jax.ShapeDtypeStruct((rows, local * 256), expert_in.dtype)] * dp,
+        grid=(local, 2),
+        in_specs=[pl.BlockSpec((1, rows, wide // 2), lambda e, g: (e, 0, g))],
+        out_specs=pl.BlockSpec((dp, rows, 128), lambda e, g: (0, 0, 2 * e + g)),
+        out_shape=jax.ShapeDtypeStruct((dp, rows, local * 256), expert_in.dtype),
         compiler_params=pltpu.CompilerParams(vmem_limit_bytes=32 * 1024 * 1024),
-    )(stage.reshape(1), expert_in)
-
-
-def undeal_kernel(dp, stage_ref, *refs):
-    out_ref = refs[dp]
+    )(expert_in)
+
+
+def undeal_kernel(parts, each, *refs):
+    out_ref = refs[parts]
     e, g = pl.program_id(0), pl.program_id(1)
-    column = pl.multiple_of((2 * e + g) * 128, 128)
-    for r in range(dp):
-        place = pl.multiple_of(lax.bitwise_xor(stage_ref[0], r) * 128, 128)
-        out_ref[0, :, pl.ds(place, 128)] = refs[r][:, pl.ds(column, 128)].astype(F32)
-
-
-def undeal(pieces, stage):
-    dp = len(pieces)
-    rows, wide = pieces[0].shape
-    local = wide // 256
+    for h in range(parts):
+
+        @pl.when(e // each == h)
+        def _():
+            column = pl.multiple_of((2 * (e - h * each) + g) * 128, 128)
+            for p in range(refs[h].shape[0]):
+                piece = refs[h][p, :, pl.ds(column, 128)]
+                out_ref[0, :, 128 * p : 128 * (p + 1)] = piece.astype(F32)
+
+
+def undeal(pieces):
+    parts = len(pieces)
+    dp, rows, wide = pieces[0].shape
+    each = wide // 256
     return pl.pallas_call(
-        functools.partial(undeal_kernel, dp),
-        grid_spec=pltpu.PrefetchScalarGridSpec(
-            num_scalar_prefetch=1,
-            grid=(local, 2),
-            in_specs=[pl.BlockSpec((rows, wide), lambda e, g, s: (0, 0))] * dp,
-            out_specs=pl.BlockSpec((1, rows, dp * 128), lambda e, g, s: (e, 0, g)),
-        ),
-        out_shape=jax.ShapeDtypeStruct((local, rows, 2 * dp * 128), F32),
+        functools.partial(undeal_kernel, parts, each),
+        grid=(parts * each, 2),
+        in_specs=[pl.BlockSpec((dp, rows, wide), lambda e, g: (0, 0, 0))] * parts,
+        out_specs=pl.BlockSpec((1, rows, dp * 128), lambda e, g: (e, 0, g)),
+        out_shape=jax.ShapeDtypeStruct((parts * each, rows, 2 * dp * 128), F32),
         compiler_params=pltpu.CompilerParams(vmem_limit_bytes=48 * 1024 * 1024),
-    )(stage.reshape(1), *pieces)
-
-
-def deal_narrow(expert_in, stage, dp):
+    )(*pieces)
+
+
+def deal_narrow(expert_in, dp):
     local, rows, wide = expert_in.shape
     ff = wide // 2 // dp
     split = expert_in.reshape(local * ff // 128, 128 // ff, rows, 2, dp, ff)
-    out = []
-    for r in range(dp):
-        piece = lax.dynamic_index_in_dim(split, stage ^ r, 4, False)
-        out.append(piece.transpose(2, 0, 3, 1, 4).reshape(rows, 2 * local * ff))
-    return out
-
-
-def undeal_narrow(pieces, stage, local):
-    dp = len(pieces)
-    rows, wide = pieces[0].shape
-    ff = wide // 2 // local
-    whole = jnp.stack(pieces)[stage ^ jnp.arange(dp)]
+    return split.transpose(4, 2, 0, 3, 1, 5).reshape(dp, rows, 2 * local * ff)
+
+
+def undeal_narrow(pieces, ff):
+    whole = jnp.concatenate(pieces, axis=2)
+    dp, rows, wide = whole.shape
     whole = whole.reshape(dp, rows, wide // 256, 2, 128 // ff, ff).astype(F32)
-    return whole.transpose(2, 4, 1, 3, 0, 5).reshape(local, rows, 2 * dp * ff)
+    return whole.transpose(2, 4, 1, 3, 0, 5).reshape(wide // 2 // ff, rows, 2 * dp * ff)
+
+
+def swap(value):
+    return lax.all_to_all(value, "dp", split_axis=0, concat_axis=0, tiled=True)
 
 
 def masked(segment):
@@ -401,12 +493,11 @@
     expert_in,
     expert_down,
 ):
-    grid, wide_x = Grid(), Grid(False)
+    grid = Grid()
     length, width = tokens.shape
     count, dp, ex = grid.count, grid.dp, grid.ex
     local = expert_in.shape[0]
     expert_count = ex * local
-    top = routes.shape[1]
     ff = expert_down.shape[1]
     rows = width // count
     block = width // dp
@@ -415,9 +506,12 @@
     group = lax.axis_index("expert")
     stage = lax.axis_index("dp")
     cosine, sine_table = rope_tables(length)
-    source, out_source = grid.sources(), wide_x.sources()
-    back, out_back = jnp.argsort(source), jnp.argsort(out_source)
+    source = grid.sources()
+    ids = jnp.arange(count, dtype=source.dtype)
+    back = jnp.sum(jnp.where(source[None, :] == ids[:, None], ids[None, :], 0), axis=1)
     dp_source = grid.dp_sources()
+    chunks = 1 if length * count <= 4096 else length * count // 4096
+    size = length // chunks
 
     def reorder(tensor, order):
         parts = order.shape[0]
@@ -429,17 +523,54 @@
         [
             norm_gains.reshape(-1),
             router_weight.reshape(-1),
-            routes.astype(BF16).reshape(-1),
             segments.astype(BF16).reshape(-1),
         ]
     )
     small = jnp.pad(small, (0, -small.shape[0] % 128)).reshape(-1, 128)
-    small = grid.small_gather(small).reshape(count, -1)
-    cuts = np.cumsum([4 * rows, rows * expert_count, length * top, length])
-    all_gains, all_router, all_routes, all_segments, _ = jnp.split(small, cuts, axis=1)
+    small_flow = Flow(grid.small_gather(small))
+    small_flow.go()
+
+    piece = in_projection.reshape(rows, 3, ex, span).transpose(2, 0, 1, 3)
+    piece = exchange(piece.reshape(ex, rows, 3 * span)).reshape(block, 3 * span)
+    tokens_g = exchange(
+        after(jnp.broadcast_to(tokens[None], (ex, length, width)), piece)
+    )
+    dense = Flow(grid.dp_gather(piece))
+    out_flow = Flow(grid.gather(out_projection))
+    cot_flow = Flow(grid.gather(cotangent[:size]))
+    dealt = (deal if ff == 128 else deal_narrow)(after(expert_in, piece), dp)
+    weight_down = expert_down.reshape(local * ff, width)
+
+    quarter = local * ff // 2
+    weights = []
+
+    def fetch(*events):
+        columns = slice(len(weights) * quarter, (len(weights) + 1) * quarter)
+        weights.append(swap(after(dealt[:, :, columns], *events)).reshape(width, quarter))
+
+    dense.go()
+    small_flow.go(piece)
+    out_flow.go(*dense.hops[0])
+    cot_flow.go(*dense.hops[0])
+    small_flow.go(*dense.hops[0])
+    dense.go(tokens_g)
+    out_flow.go(*dense.hops[1])
+    cot_flow.go(*dense.hops[1])
+    small_flow.go(*dense.hops[1])
+    dense.go(dealt, *out_flow.hops[0], *cot_flow.hops[0])
+    fetch(*dense.hops[2])
+    out_flow.go(*dense.hops[2])
+    small_flow.go(*dense.hops[2])
+    dense.go(*out_flow.hops[1], *cot_flow.hops[1])
+    cot_flow.go(*dense.hops[3])
+    out_flow.go(*dense.hops[3], *out_flow.hops[2])
+    proj = after(dense.finish(), weights[0])
+    fetch(*dense.hops[3])
+    small = small_flow.finish().reshape(count, -1)
+    cuts = np.cumsum([4 * rows, rows * expert_count, length])
+    all_gains, all_router, all_segments, _ = jnp.split(small, cuts, axis=1)
     gains = jnp.swapaxes(all_gains.reshape(count, 4, rows), 0, 1).reshape(4, width).astype(F32)
     router = all_router.reshape(width, expert_count)
-    all_routes = all_routes.reshape(count, length, top).astype(jnp.int32)
     segment = lax.dynamic_slice_in_dim(
         all_segments.reshape(dp, ex, length), stage, 1, 0
     )[0].astype(jnp.int32)
@@ -447,37 +578,19 @@
     gain_q = lax.dynamic_slice_in_dim(gains[2], group * span, span)
     gain_k = lax.dynamic_slice_in_dim(gains[3], group * span, span)
 
-    piece = in_projection.reshape(rows, 3, ex, span).transpose(2, 0, 1, 3)
-    piece = exchange(piece.reshape(ex, rows, 3 * span)).reshape(block, 3 * span)
-    tokens_g = exchange(jnp.broadcast_to(tokens[None], (ex, length, width)))
-    proj, arrived = grid.dp_gather(piece)
-    proj_out = jnp.concatenate(wide_x.gather(after(out_projection, arrived))).reshape(width, width)
-
-    others = list(range(dp - 1, 0, -1))
-    weight_in = jnp.zeros((width, 2 * local * ff), BF16)
-    dealt = (deal if ff == 128 else deal_narrow)(expert_in, stage, dp)
-    gone = [arrived, arrived]
-    for r in [0] + others:
-        got = dealt[r]
-        if r:
-            got = lax.ppermute(after(got, gone[-2]), "dp", [(i, i ^ r) for i in range(dp)])
-            gone.append(got)
-        weight_in = lax.dynamic_update_slice_in_dim(weight_in, got, (stage ^ r) * block, 0)
-    weight_down = expert_down.reshape(local * ff, width)
-
-    chunks = max(1, length * count // 4096)
-    size = length // chunks
-
-    def gather_rows(tensor, i):
-        return jnp.concatenate(grid.gather(tensor[i * size : (i + 1) * size])).reshape(-1, width)
-
     normed1_g, factor1 = normalize(tokens_g.reshape(ex * length, width).astype(F32))
     hidden1_g = (normed1_g * gains[0]).astype(BF16)
     projected = dot(hidden1_g, proj)
     query_raw, key_raw = projected[:, :span], projected[:, span : 2 * span]
     squares = jnp.stack([jnp.sum(query_raw**2, axis=-1), jnp.sum(key_raw**2, axis=-1)])
-    factors = lax.rsqrt(grid.group_sum(squares) / width + EPSILON)[:, :, None]
+    squares = grid.group_sum(squares)
+    squares = after(squares, weights[1], *out_flow.hops[3], *cot_flow.hops[2])
+    fetch(squares)
+    out_flow.go(squares)
+    cot_flow.go(squares)
+    factors = lax.rsqrt(squares / width + EPSILON)[:, :, None]
     query_factor, key_factor = factors[0], factors[1]
+    proj_out = jnp.concatenate(out_flow.finish()).reshape(width, width)
     query_normed, key_normed = query_raw * query_factor, key_raw * key_factor
 
     def by_heads(tensor):
@@ -487,61 +600,113 @@
     key_rows = rotate(by_heads(key_normed * gain_k), cosine, sine_table, False).astype(BF16)
     values = by_heads(projected[:, 2 * span :].astype(BF16))
     attended_h, weights_f = attend(queries, key_rows, values, allowed)
+    cot_flow.go(attended_h, *cot_flow.hops[3])
     attended = exchange(attended_h.reshape(ex, length, span))
-    attended_s = reorder(jnp.swapaxes(attended, 0, 1).reshape(length, width), out_source)
+    attended = after(attended, weights[2])
+    fetch(attended)
+    attended_c = jnp.swapaxes(attended, 0, 1).reshape(length, width)
+    attended_s = reorder(attended_c, source)
     residual = tokens.astype(F32)
     middle = residual + dot(attended_s, proj_out)
     normed2, factor2 = normalize(middle)
     hidden2 = (normed2 * gains[1]).astype(BF16)
+    hidden2 = after(hidden2, weights[3], *cot_flow.hops[4])
+    weight_in = jnp.concatenate(weights, axis=1)
     router_probs = jax.nn.softmax(dot(hidden2, router), axis=-1)
     grad_top = cotangent.astype(F32)
-
-    routes_s = all_routes[source]
-    mine = group * local + jnp.arange(local, dtype=jnp.int32)
-    mixtures, grad_h2s, probs_parts = [], [], []
-    grad_in_w, grad_down_w = [0.0] * dp, 0.0
+    named = jnp.arange(expert_count, dtype=jnp.int32)
+    chosen = jnp.any(routes[:, :, None] == named[None, None, :], axis=1)
+    gates = jnp.where(chosen, router_probs, 0.0).reshape(-1, 128)
+
+    hid_flow = Flow(grid.gather(hidden2[:size]))
+    gate_flow = Flow(grid.small_gather(gates))
+    cot_flow.go(hidden2)
+    hid_flow.go()
+    gate_flow.go()
+    hid_flow.go(weight_in, *cot_flow.hops[5])
+    cot_flow.go(*hid_flow.hops[0])
+    gate_flow.go(*hid_flow.hops[0])
+    for k in (1, 2, 3):
+        gate_flow.go(*hid_flow.hops[k])
+        hid_flow.go(*gate_flow.hops[k])
+    gates = gate_flow.finish().reshape(count, length, expert_count)
+    gates = lax.dynamic_slice_in_dim(gates[source], group * local, local, 2)
+    back_flows, mix_flows, probs_parts = [], [], []
+    grad_in_w, grad_down_w = [0.0] * 4, 0.0
     for i in range(chunks):
-        ready = (grad_h2s[-1], mixtures[-1], grad_in_w, grad_down_w) if i else (arrived,)
-        cot = gather_rows(after(cotangent, *ready), i)
-        hid = gather_rows(after(hidden2, *ready), i)
+        if i:
+            ready = (back_flows[-1].finish(), mix_flows[-1].finish(), grad_in_w, grad_down_w)
+            part = slice(i * size, (i + 1) * size)
+            cot_flow = Flow(grid.gather(after(cotangent[part], *ready)))
+            hid_flow = Flow(grid.gather(after(hidden2[part], *ready)))
+        cot = jnp.concatenate(cot_flow.finish()).reshape(-1, width)
+        lifted = dot(cot, weight_down, ROWS_BACK)
+        while len(hid_flow.hops) < 5:
+            hid_flow.go()
+        hid_flow.go(lifted)
+        hid = jnp.concatenate(hid_flow.finish()).reshape(-1, width)
         total = hid.shape[0]
-        probs = jax.nn.softmax(dot(hid, router), axis=-1)
-        probs = lax.dynamic_slice_in_dim(probs, group * local, local, 1)
-        named = routes_s[:, i * size : (i + 1) * size, :].reshape(total, top)
-        chosen = jnp.any(named[:, :, None] == mine[None, None, :], axis=1)
-        gate_dense = jnp.where(chosen, probs, 0.0)
-        lifted = dot(cot, weight_down, ROWS_BACK)
+        gate_dense = gates[:, i * size : (i + 1) * size].reshape(total, local)
         part = total // 4
         slotted = (count // 4, size, width)
         done = [None] * 4
-        for j in (3, 2, 1, 0):
+
+        def run(j, *events):
             kind = BF16 if j % 2 else F32
-            done[j] = moe_rows(
-                hid, lifted, gate_dense, weight_in, ff, j * part, part, kind
-            )
-        grad_h2s.append(grid.scatter([d[3].reshape(slotted) for d in done]))
-        mixtures.append(grid.scatter([dot(d[1], weight_down).reshape(slotted) for d in done]))
-        probs_part = jnp.where(chosen, jnp.concatenate([d[2] for d in done]), 0.0)
+            gates = after(gate_dense, *events)
+            done[j] = moe_rows(hid, lifted, gates, weight_in, ff, j * part, part, kind)
+            return done[j][3].reshape(slotted)
+
+        far = [None, None, None, run(3)]
+        far[2] = run(2, done[3][3])
+        near = [None, None]
+        flow = Flow(grid.scatter_early(far, lambda: near))
+        flow.go()
+        near[1] = run(1, *flow.hops[0])
+        flow.go()
+        near[0] = run(0, *flow.hops[1], done[1][3])
+        flow.go()
+        last = done[0][3]
+        acts = [d[1] for d in done]
+        grad_pre = jnp.concatenate([d[0] for d in done])
+        wide = 2 * local * ff // 4
+        columns = [grad_pre[:, q * wide : (q + 1) * wide] for q in range(4)]
+
+        def weigh(q, *events):
+            part = dot(after(hid, *events), columns[q], SUM_ROWS)
+            grad_in_w[q] += part
+            return part
+
+        def mixed(j, *events):
+            return dot(after(acts[j], *events), weight_down).astype(BF16).reshape(slotted)
+
+        first = weigh(0, last)
+        flow.go(first)
+        mix = [None, None, mixed(2, *flow.hops[2]), mixed(3, *flow.hops[2])]
+        flow.go(mix[2], mix[3])
+        mix[0], mix[1] = mixed(0, *flow.hops[3]), mixed(1, *flow.hops[3])
+        second = weigh(1, *flow.hops[3])
+        if i == chunks - 1:
+            gone = [g.astype(BF16).reshape(dp, block, wide) for g in grad_in_w[:1]]
+            home = [swap(gone[0])]
+            flow.go(mix[0], mix[1], second, home[0])
+        else:
+            flow.go()
+        third = weigh(2, *flow.hops[4])
+        fourth = weigh(3, *flow.hops[4])
+        flow.go(third, fourth)
+        back_flows.append(flow)
+        mix_flow = Flow(grid.scatter(mix, BF16))
+        mix_flow.go(*flow.hops[4])
+        mix_flows.append(mix_flow)
+        probs_part = jnp.concatenate([d[2] for d in done])
         probs_parts.append(probs_part.reshape(count, size, local))
-        grad_pre = jnp.concatenate([d[0] for d in done])
-        act_gated = jnp.concatenate([d[1] for d in done])
-        grad_down_w += dot(act_gated, cot, SUM_ROWS)
-        for r in others + [0]:
-            rows_in = lax.dynamic_slice_in_dim(hid, (stage ^ r) * block, block, 1)
-            grad_in_w[r] += dot(rows_in, grad_pre, SUM_ROWS)
-
-    home = [None] * dp
-    gone = []
-    for r in others + [0]:
-        piece = grad_in_w[r].astype(BF16)
-        if r:
-            if len(gone) > 1:
-                piece = after(piece, gone[-2])
-            piece = lax.ppermute(piece, "dp", [(i, i ^ r) for i in range(dp)])
-            gone.append(piece)
-        home[r] = piece
-    grad_expert_in = undeal(home, stage) if ff == 128 else undeal_narrow(home, stage, local)
-    grad_expert_down = grad_down_w.reshape(local, ff, width)
+        act_gated = jnp.concatenate(acts)
+        if i < chunks - 1:
+            grad_down_w += dot(act_gated, cot, SUM_ROWS)
+
+    def send(q, *events):
+        home.append(swap(after(grad_in_w[q].astype(BF16).reshape(dp, block, wide), *events)))
 
     probs_all = jnp.concatenate(probs_parts, axis=1)[back]
     place = (jnp.arange(expert_count) // local == group).astype(F32)
@@ -549,31 +714,36 @@
         count, length * expert_count // 128, 128
     )
     grad_probs = grid.small_scatter(probs_wide).reshape(length, expert_count)
-
-    block_out = middle + jnp.concatenate(mixtures)
+    grad_probs = jnp.where(chosen, grad_probs, 0.0)
+
     grad_logits = (
         router_probs * (grad_probs - jnp.sum(router_probs * grad_probs, axis=-1, keepdims=True))
     ).astype(BF16)
     grad_router_part = dot(hidden2, grad_logits, SUM_ROWS)
-    grad_hidden2 = jnp.concatenate(grad_h2s) + dot(grad_logits, router, ROWS_BACK)
+    grad_hidden2 = jnp.concatenate([f.finish() for f in back_flows]) + dot(grad_logits, router, ROWS_BACK)
     grad_gain_moe = jnp.sum(grad_hidden2 * normed2, axis=0)
     grad_middle = grad_top + normalize_back(grad_hidden2 * gains[1], normed2, factor2)
     grad_mid_b = grad_middle.astype(BF16)
-    grad_attended = reorder(dot(grad_mid_b, proj_out, ROWS_BACK).astype(BF16), out_back)
+    grad_attended = reorder(dot(grad_mid_b, proj_out, ROWS_BACK).astype(BF16), back)
     grad_heads = by_heads(
         exchange(jnp.swapaxes(grad_attended.reshape(length, ex, span), 0, 1)).reshape(
             ex * length, span
         )
     )
     quarter = width // 4
-    grad_out_projection = wide_x.scatter(
-        [
-            dot(attended_s[:, j * quarter : (j + 1) * quarter], grad_mid_b, SUM_ROWS).reshape(
-                count // 4, rows, width
-            )
-            for j in range(4)
-        ]
-    )
+    out_parts = [
+        dot(attended_s[:, j * quarter : (j + 1) * quarter], grad_mid_b, SUM_ROWS).reshape(
+            count // 4, rows, width
+        )
+        for j in range(4)
+    ]
+    out_flow = Flow(grid.scatter(out_parts))
+    send(1, grad_mid_b)
+    mix_flow.go(grad_mid_b)
+    grad_heads = after(grad_heads, *mix_flow.hops[1])
+    send(2, grad_heads)
+    mix_flow.go(grad_heads)
+    out_flow.go(grad_heads)
     grad_queries, grad_keys, grad_values = attend_back(
         queries, key_rows, values, weights_f, attended_h, grad_heads
     )
@@ -583,6 +753,9 @@
     up_q, up_k = grad_qscaled * gain_q, grad_kscaled * gain_k
     along = jnp.stack([jnp.sum(up_q * query_normed, axis=-1), jnp.sum(up_k * key_normed, axis=-1)])
     along = (grid.group_sum(along) / width)[:, :, None]
+    along = after(along, *mix_flow.hops[2], *out_flow.hops[0])
+    mix_flow.go(along)
+    out_flow.go(along)
     grad_projected = jnp.concatenate(
         [
             query_factor * (up_q - query_normed * along[0]),
@@ -593,14 +766,31 @@
     ).astype(BF16)
     mid = width // 2
     hidden1_s = reorder(hidden1_g, dp_source)
-    grad_proj = grid.dp_scatter(
-        [
-            dot(hidden1_s[:, h * mid : (h + 1) * mid], grad_projected, SUM_ROWS).reshape(
-                grid.size["y"], 2, block, 3 * span
-            )
-            for h in range(2)
-        ]
-    )
+    proj_flow = Flow(
+        grid.dp_scatter(
+            [
+                dot(hidden1_s[:, h * mid : (h + 1) * mid], grad_projected, SUM_ROWS).reshape(
+                    grid.size["y"], 2, block, 3 * span
+                )
+                for h in range(2)
+            ]
+        )
+    )
+    proj_flow.go(home[1], home[2])
+    send(3, grad_projected)
+    proj_flow.go(*mix_flow.hops[3], *out_flow.hops[1])
+    mix_flow.go(*proj_flow.hops[0])
+    out_flow.go(*proj_flow.hops[0])
+    proj_flow.go(*mix_flow.hops[4], *out_flow.hops[2])
+    mix_flow.go(*proj_flow.hops[1])
+    out_flow.go(*proj_flow.hops[1])
+    grad_down_w += dot(after(act_gated, *proj_flow.hops[0]), cot, SUM_ROWS)
+    proj_flow.go(*mix_flow.hops[5], *out_flow.hops[3])
+    out_flow.go(*proj_flow.hops[2])
+    grad_proj = proj_flow.finish()
+    block_out = middle + jnp.concatenate([f.finish() for f in mix_flows])
+    grad_out_projection = out_flow.finish()
+    grad_expert_down = grad_down_w.reshape(local, ff, width)
     grad_proj = exchange(grad_proj.astype(BF16).reshape(ex, rows, 3 * span)).astype(F32)
     grad_in_projection = (
         grad_proj.reshape(ex, rows, 3, span).transpose(1, 2, 0, 3).reshape(rows, 3 * width)
@@ -611,6 +801,9 @@
     own_factor = lax.dynamic_slice_in_dim(factor1, group * length, length, 0)
     gain_one = jnp.sum(grad_hidden1 * own, axis=0)
     input_grad = grad_middle + normalize_back(grad_hidden1 * gains[0], own, own_factor)
+
+    home = after(home, grad_proj)
+    grad_expert_in = undeal(home) if ff == 128 else undeal_narrow(home, ff)
 
     def widen(values):
         return lax.dynamic_update_slice_in_dim(jnp.zeros((width,), F32), values, group * span, 0)

time: 1540 us -> 1380 us (0.90)
  waiting for transfers between devices: 594 us -> 372 us
  other arithmetic: 117 us -> 163 us
  local copies, waits for them, and re-layouts: 212 us -> 239 us
  starting transfers between devices: 265 us -> 242 us
  blocking collectives: 0 us -> 15.8 us
    ppermute x86, waiting for transfers between devices: 374 us -> 235 us  [move(): return lax.ppermute(value, AXES, pairs)]
    ppermute x14 -> x0, waiting for transfers between devices: 133 us -> none  [the longest x7 73.4 us: per_device(): piece = lax.ppermute(piece, 'dp', [(i, i ^ r) for i in range(dp)])]
    ppermute x14 -> x0, starting transfers between devices: 65.7 us -> none  [the longest x7 51.7 us: per_device(): piece = lax.ppermute(piece, 'dp', [(i, i ^ r) for i in range(dp)])]
    all_to_all x0 -> x8, starting transfers between devices: none -> 49.6 us  [swap(): return lax.all_to_all(value, 'dp', split_axis=0, concat_axis=0, tiled=True)]
    all_to_all x0 -> x8, waiting for transfers between devices: none -> 31.1 us  [swap(): return lax.all_to_all(value, 'dp', split_axis=0, concat_axis=0, tiled=True)]
    convert_element_type x10 -> x14, other arithmetic: 3.37 us -> 31.9 us  [the longest x1 7.6 us: scatter(): near = self.unfold(self.line_reduce(near, 'c').astype(kind))]
    concatenate x1 -> x8, other arithmetic: 0.02 us -> 27.7 us  [the longest x3 8.99 us: gather(): block = jnp.concatenate([row[i] for i in range(count) for row in nb])]
    ppermute x21 -> x26, waiting for transfers between devices: 63.5 us -> 88.9 us  [flip(): return lax.ppermute(value, AXES, [(i, i ^ bit) for i in range(self.count)])]
  transfers between devices with their start and end apart: 127 -> 125, of which waited for: 47 -> 46; matrix products, arithmetic and copies ran while one was open for 27% -> 38% of each run, Pallas kernels for 1% -> 6%
where the time goes in v2:
time: 1380 us; the launch traced here: 1350 us
  waiting for transfers between devices  372 us (27%)
  starting transfers between devices  242 us (18%)
  local copies, waits for them, and re-layouts  239 us (17%)
  matrix products  189 us (14%)
  other arithmetic  163 us (12%)
  Pallas kernels  122 us (9%)
  blocking collectives  15.8 us (1%)
    ppermute x86, waiting for transfers between devices, move(): return lax.ppermute(value, AXES, pairs)  235 us
    dot_general x23, matrix products, dot(): return lax.dot_general(left, right, dims, preferred_element_type=F32)  176 us
    ppermute x86, starting transfers between devices, move(): return lax.ppermute(value, AXES, pairs)  146 us
    pallas_call x4, Pallas kernels, moe_rows(): pl.pallas_call(functools.partial(moe_kernel, ff, local), grid=(total // t...  105 us
    unnamed x380, local copies, waits for them, and re-layouts  90.8 us
    ppermute x26, waiting for transfers between devices, flip(): return lax.ppermute(value, AXES, [(i, i ^ bit) for i in range(self.count)])  88.9 us
    all_to_all x8, starting transfers between devices, swap(): return lax.all_to_all(value, 'dp', split_axis=0, concat_axis=0, tiled=True)  49.6 us
    add x14, other arithmetic, line_reduce(): return slots[0] + sent(slots[1])  40.2 us
  transfers between devices with their start and end apart: 125, of which 46 were waited for; matrix products, arithmetic and copies ran while one was open for 38% of the time, Pallas kernels for 6%

profile of v2, /device:TPU:0, one launch (start us, length us, event | category | flops | bytes accessed | tf_op | source)
XLA Modules:
  0.0 1353.7 jit_solution(8408973260544299558)
XLA Ops:
  4.6 15.8 %all_to_all.70 = bf16[4,64,1536]{2,1,0:T(8,128)(2,1)S(1)} all-to-all(bf16[4,64,1536]{2,1,0:T(8,128)(2,1)S(1)} %reshape.743), channel_id=1, replica_groups=mesh['dp'=8,'expert'=4] {'expert'}, dimensions={0} | all-to-all | bytes 1572864 | tf_op jit(solution)/shard_map/all_to_all | solution.py:325
  81.1 12.8 collective-permute-done.6
  104.1 29.9 %collective-permute-done.16 = bf16[64,2048]{1,0:T(8,128)(2,1)S(1)} collective-permute-done((bf16[64,2048]{1,0:T(8,128)(2,1)}, bf16[64,2048]{1,0:T(8,128)(2,1)S(1)}, u32[]{:S(2)}, u32[]{:S(2)}) %collective-permute-start.16) | collective-permute-done | bytes 262176 | tf_op jit(solution)/shard_map/ppermute | solution.py:122
  158.3 14.9 %collective-permute-done.7 = bf16[8,19,128]{2,1,0:T(8,128)(2,1)S(1)} collective-permute-done((bf16[8,19,128]{2,1,0:T(8,128)(2,1)S(1)}, bf16[8,19,128]{2,1,0:T(8,128)(2,1)S(1)}, u32[]{:S(2)}, u32[]{:S(2)}) %collective-permute-start.7) | collective-permute-done | bytes 38944 | tf_op jit(solution)/shard_map/ppermute | solution.py:298
  302.6 14.0 %collective-permute-start.30 = (bf16[8,64,2048]{2,1,0:T(8,128)(2,1)}, bf16[8,64,2048]{2,1,0:T(8,128)(2,1)}, u32[]{:S(2)}, u32[]{:S(2)}) collective-permute-start(bf16[8,64,2048]{2,1,0:T(8,128)(2,1)} %pad_maximum_fusion.6), channel_id=1, source_target_pairs={{0,1},{1,0},{2,3},{3,2},{4,5},{5,4},{6,7},{7,6},{8,9},{9,8},{10,11... | collective-permute-start | bytes 6291464 | tf_op jit(solution)/shard_map/ppermute | solution.py:122
  390.7 16.4 %all-to-all-done.6 = bf16[8,256,512]{2,1,0:T(8,128)(2,1)} async-done(((bf16[8,256,512]{2,1,0:T(8,128)(2,1)}), bf16[8,256,512]{2,1,0:T(8,128)(2,1)}, u32[]{:S(2)}, u32[]{:S(2)}) %all-to-all-start.6) | async-done | bytes 2097184 | tf_op jit(solution)/shard_map/all_to_all | solution.py:447
  472.6 13.7 %collective-permute-done.45 = bf16[128,2048]{1,0:T(8,128)(2,1)S(1)} collective-permute-done((bf16[128,2048]{1,0:T(8,128)(2,1)S(1)}, bf16[128,2048]{1,0:T(8,128)(2,1)S(1)}, u32[]{:S(2)}, u32[]{:S(2)}) %collective-permute-start.45) | collective-permute-done | bytes 524320 | tf_op jit(solution)/shard_map/ppermute | solution.py:122
  507.1 22.6 %fusion.118.lift_ref = f32[4096,1024]{1,0:T(8,128)} fusion(bf16[4096,2048]{1,0:T(8,128)(2,1)} %bitcast.470, bf16[1024,2048]{1,0:T(8,128)(2,1)S(1)} %bitcast.499), kind=kOutput, calls=%fused_computation.400 | convolution fusion | flops 17179869184 | bytes 37748736 | tf_op jit(solution)/shard_map/dot_general | solution.py:24
  558.3 13.7 %collective-permute-done.58 = f32[16,32,128]{2,1,0:T(8,128)S(1)} collective-permute-done((f32[16,32,128]{2,1,0:T(8,128)S(1)}, f32[16,32,128]{2,1,0:T(8,128)S(1)}, u32[]{:S(2)}, u32[]{:S(2)}) %collective-permute-start.58) | collective-permute-done | bytes 262176 | tf_op jit(solution)/shard_map/ppermute | solution.py:298
  603.4 26.2 %shard_map.234 = (bf16[1024,2048]{1,0:T(8,128)(2,1)}, bf16[1024,1024]{1,0:T(8,128)(2,1)}, f32[1024,8]{1,0:T(8,128)}, bf16[1024,2048]{1,0:T(8,128)(2,1)}) custom-call(bf16[4096,2048]{1,0:T(8,128)(2,1)} %bitcast.62.x_ref, f32[4096,1024]{1,0:T(8,128)} %fusion.118.lift_ref, f32[4096,8]{1,0:T(8,128)} %bitcast.453, bf16[2048,2048]{1,0:T(8,128)(2,1)} %pad_maximum_fusion.w_ref), custom_call_target="tpu_custom_call" | custom-call | flops 17179869184 | bytes 25165824 | tf_op jit(solution)/shard_map/pallas_call | solution.py:365
  643.6 26.3 %shard_map.235 = (bf16[1024,2048]{1,0:T(8,128)(2,1)}, bf16[1024,1024]{1,0:T(8,128)(2,1)}, f32[1024,8]{1,0:T(8,128)}, f32[1024,2048]{1,0:T(8,128)}) custom-call(bf16[4096,2048]{1,0:T(8,128)(2,1)} %bitcast.62.x_ref, f32[4096,1024]{1,0:T(8,128)} %fusion.118.lift_ref, f32[4096,8]{1,0:T(8,128)} %bitcast.454, bf16[2048,2048]{1,0:T(8,128)(2,1)} %pad_maximum_fusion.w_ref), custom_call_target="tpu_custom_call" | custom-call | flops 17179869184 | bytes 25165824 | tf_op jit(solution)/shard_map/pallas_call | solution.py:365
  684.4 26.1 %shard_map.236 = (bf16[1024,2048]{1,0:T(8,128)(2,1)}, bf16[1024,1024]{1,0:T(8,128)(2,1)}, f32[1024,8]{1,0:T(8,128)}, bf16[1024,2048]{1,0:T(8,128)(2,1)}) custom-call(bf16[4096,2048]{1,0:T(8,128)(2,1)} %bitcast.62.x_ref, f32[4096,1024]{1,0:T(8,128)} %fusion.118.lift_ref, f32[4096,8]{1,0:T(8,128)} %bitcast.455, bf16[2048,2048]{1,0:T(8,128)(2,1)} %pad_maximum_fusion.w_ref), custom_call_target="tpu_custom_call" | custom-call | flops 17179869184 | bytes 25165824 | tf_op jit(solution)/shard_map/pallas_call | solution.py:365
  718.5 26.7 %shard_map.237 = (bf16[1024,2048]{1,0:T(8,128)(2,1)}, bf16[1024,1024]{1,0:T(8,128)(2,1)}, f32[1024,8]{1,0:T(8,128)}, f32[1024,2048]{1,0:T(8,128)}) custom-call(bf16[4096,2048]{1,0:T(8,128)(2,1)} %bitcast.62.x_ref, f32[4096,1024]{1,0:T(8,128)} %fusion.118.lift_ref, f32[4096,8]{1,0:T(8,128)} %bitcast.456, bf16[2048,2048]{1,0:T(8,128)(2,1)} %pad_maximum_fusion.w_ref), custom_call_target="tpu_custom_call" | custom-call | flops 17179869184 | bytes 25165824 | tf_op jit(solution)/shard_map/pallas_call | solution.py:365
  764.4 13.6 %fusion.7 = bf16[2048,512]{1,0:T(8,128)(2,1)} fusion(bf16[4096,2048]{1,0:T(8,128)(2,1)} %bitcast.62.x_ref, bf16[4096,2048]{1,0:T(8,128)(2,1)S(1)} %constant_dynamic-update-slice_fusion.36), kind=kOutput, calls=%fused_computation.23 | convolution fusion | flops 8589934592 | bytes 23068672 | tf_op jit(solution)/shard_map/dot_general | solution.py:24
  801.2 23.8 %collective-permute-done.61 = bf16[2,128,2048]{2,1,0:T(8,128)(2,1)} collective-permute-done((bf16[2,128,2048]{2,1,0:T(8,128)(2,1)}, bf16[2,128,2048]{2,1,0:T(8,128)(2,1)}, u32[]{:S(2)}, u32[]{:S(2)}) %collective-permute-start.61) | collective-permute-done | bytes 1048608 | tf_op jit(solution)/shard_map/ppermute | solution.py:122
  858.4 15.3 %fusion.5 = bf16[2048,512]{1,0:T(8,128)(2,1)} fusion(bf16[4096,2048]{1,0:T(8,128)(2,1)} %bitcast.62.x_ref, bf16[4096,2048]{1,0:T(8,128)(2,1)} %copy-done.88), kind=kOutput, calls=%fused_computation.20 | convolution fusion | flops 8589934592 | bytes 23068672 | tf_op jit(solution)/shard_map/dot_general | solution.py:24
  887.6 14.7 %fusion.3 = bf16[2048,512]{1,0:T(8,128)(2,1)} fusion(bf16[4096,2048]{1,0:T(8,128)(2,1)} %bitcast.62.x_ref, bf16[4096,2048]{1,0:T(8,128)(2,1)} %copy-done.88), kind=kOutput, calls=%fused_computation.18 | convolution fusion | flops 8589934592 | bytes 23068672 | tf_op jit(solution)/shard_map/dot_general | solution.py:24
  911.1 14.8 %fusion.1 = bf16[2048,512]{1,0:T(8,128)(2,1)} fusion(bf16[4096,2048]{1,0:T(8,128)(2,1)} %bitcast.62.x_ref, bf16[4096,2048]{1,0:T(8,128)(2,1)} %copy-done.88), kind=kOutput, calls=%fused_computation.16 | convolution fusion | flops 8589934592 | bytes 23068672 | tf_op jit(solution)/shard_map/dot_general | solution.py:24
  976.7 17.3 %collective-permute-done.78 = bf16[2,2,128,2048]{3,2,1,0:T(8,128)(2,1)} collective-permute-done((bf16[2,2,128,2048]{3,2,1,0:T(8,128)(2,1)}, bf16[2,2,128,2048]{3,2,1,0:T(8,128)(2,1)}, u32[]{:S(2)}, u32[]{:S(2)}) %collective-permute-start.78) | collective-permute-done | bytes 2097184 | tf_op jit(solution)/shard_map/ppermute | solution.py:122
  1088.3 14.6 %all-to-all-done.10.refs_2_ = bf16[8,256,512]{2,1,0:T(8,128)(2,1)} async-done(((bf16[8,256,512]{2,1,0:T(8,128)(2,1)}), bf16[8,256,512]{2,1,0:T(8,128)(2,1)}, u32[]{:S(2)}, u32[]{:S(2)}) %all-to-all-start.10) | async-done | bytes 2097184 | tf_op jit(solution)/shard_map/all_to_all | solution.py:447
  1190.1 13.9 %collective-permute-done.94 = bf16[256,1536]{1,0:T(8,128)(2,1)S(1)} collective-permute-done((bf16[256,1536]{1,0:T(8,128)(2,1)S(1)}, bf16[256,1536]{1,0:T(8,128)(2,1)S(1)}, u32[]{:S(2)}, u32[]{:S(2)}) %collective-permute-start.94) | collective-permute-done | bytes 786464 | tf_op jit(solution)/shard_map/ppermute | solution.py:122
  1228.0 15.0 %collective-permute-start.103 = (bf16[256,1536]{1,0:T(8,128)(2,1)S(1)}, bf16[256,1536]{1,0:T(8,128)(2,1)S(1)}, u32[]{:S(2)}, u32[]{:S(2)}) collective-permute-start(bf16[256,1536]{1,0:T(8,128)(2,1)S(1)} %fusion.22), channel_id=1, source_target_pairs={{0,8},{1,9},{2,10},{3,11},{4,12},{5,13},{6,14},{7,15},{8,0},{9,1},... | collective-permute-start | bytes 2359304 | tf_op jit(solution)/shard_map/ppermute | solution.py:122
  1288.1 24.1 %fusion.120 = f32[8,128,2048]{2,1,0:T(8,128)} fusion(bf16[8,128,4096]{2,1,0:T(8,128)(2,1)} %bitcast.425, bf16[4096,2048,1]{1,0,2:T(8,128)(2,1)} %bitcast.471), kind=kOutput, calls=%fused_computation.402 | convolution fusion | flops 17179869184 | bytes 33554432 | tf_op jit(solution)/shard_map/dot_general | solution.py:24
  1341.4 12.0 shard_map.238
  (915 shorter events, 904.0 us)
Async XLA Ops:
  76.2 57.8 %collective-permute-start.13 = (bf16[2,256,1536]{2,1,0:T(8,128)(2,1)S(1)}, bf16[2,256,1536]{2,1,0:T(8,128)(2,1)S(1)}, u32[]{:S(2)}, u32[]{:S(2)}) collective-permute-start(bf16[2,256,1536]{2,1,0:T(8,128)(2,1)S(1)} %pad_maximum_fusion.8), channel_id=1, source_target_pairs={{0,4},{1,5},{2,6},{3,7},{4,0},{5,1},{6,2},{7,3},{8,12},{9,13},{10,... | collective-permute-start | bytes 4718600 | tf_op jit(solution)/shard_map/ppermute | solution.py:122
  79.8 54.3 %collective-permute-start.12 = (bf16[256,1536]{1,0:T(8,128)(2,1)S(1)}, bf16[256,1536]{1,0:T(8,128)(2,1)S(1)}, u32[]{:S(2)}, u32[]{:S(2)}) collective-permute-start(bf16[256,1536]{1,0:T(8,128)(2,1)S(1)} %collective-permute-done.5), channel_id=1, source_target_pairs={{8,0},{9,1},{10,2},{11,3},{12,4},{13,5},{14,6},{15,7},{16,24},{17,... | collective-permute-start | bytes 2359304 | tf_op jit(solution)/shard_map/ppermute | solution.py:122
  135.8 61.7 %all-to-all-start.2 = ((bf16[8,256,512]{2,1,0:T(8,128)(2,1)}), bf16[8,256,512]{2,1,0:T(8,128)(2,1)}, u32[]{:S(2)}, u32[]{:S(2)}) async-start(bf16[8,256,512]{2,1,0:T(8,128)(2,1)} %get-tuple-element.177), calls=%async_computation.2 | async-start | bytes 4194304 | tf_op jit(solution)/shard_map/all_to_all | solution.py:447
  149.0 48.5 %collective-permute-start.19 = (bf16[2,256,1536]{2,1,0:T(8,128)(2,1)}, bf16[2,256,1536]{2,1,0:T(8,128)(2,1)}, u32[]{:S(2)}, u32[]{:S(2)}) collective-permute-start(bf16[2,256,1536]{2,1,0:T(8,128)(2,1)} %pad_maximum_fusion.9), channel_id=1, source_target_pairs={{0,4},{1,5},{2,6},{3,7},{4,0},{5,1},{6,2},{7,3},{8,12},{9,13},{10,... | collective-permute-start | bytes 4718600 | tf_op jit(solution)/shard_map/ppermute | solution.py:122
  197.6 53.8 %all-to-all-start.3 = ((bf16[8,256,512]{2,1,0:T(8,128)(2,1)}), bf16[8,256,512]{2,1,0:T(8,128)(2,1)}, u32[]{:S(2)}, u32[]{:S(2)}) async-start(bf16[8,256,512]{2,1,0:T(8,128)(2,1)} %get-tuple-element.179), calls=%async_computation.3 | async-start | bytes 4194304 | tf_op jit(solution)/shard_map/all_to_all | solution.py:447
  207.9 43.5 %collective-permute-start.28 = (bf16[2,128,2048]{2,1,0:T(8,128)(2,1)S(1)}, bf16[2,128,2048]{2,1,0:T(8,128)(2,1)}, u32[]{:S(2)}, u32[]{:S(2)}) collective-permute-start(bf16[2,128,2048]{2,1,0:T(8,128)(2,1)S(1)} %pad_maximum_fusion.11), channel_id=1, source_target_pairs={{0,4},{1,3},{2,6},{3,1},{4,0},{5,7},{6,2},{7,5},{8,12},{9,11},{10,... | collective-permute-start | bytes 3145736 | tf_op jit(solution)/shard_map/ppermute | solution.py:122
  281.8 66.0 %all-to-all-start.5 = ((bf16[8,256,512]{2,1,0:T(8,128)(2,1)}), bf16[8,256,512]{2,1,0:T(8,128)(2,1)}, u32[]{:S(2)}, u32[]{:S(2)}) async-start(bf16[8,256,512]{2,1,0:T(8,128)(2,1)} %get-tuple-element.187), calls=%async_computation.5 | async-start | bytes 4194304 | tf_op jit(solution)/shard_map/all_to_all | solution.py:447
  302.6 63.7 %collective-permute-start.30 = (bf16[8,64,2048]{2,1,0:T(8,128)(2,1)}, bf16[8,64,2048]{2,1,0:T(8,128)(2,1)}, u32[]{:S(2)}, u32[]{:S(2)}) collective-permute-start(bf16[8,64,2048]{2,1,0:T(8,128)(2,1)} %pad_maximum_fusion.6), channel_id=1, source_target_pairs={{0,1},{1,0},{2,3},{3,2},{4,5},{5,4},{6,7},{7,6},{8,9},{9,8},{10,11... | collective-permute-start | bytes 6291464 | tf_op jit(solution)/shard_map/ppermute | solution.py:122
  347.8 59.3 %all-to-all-start.6 = ((bf16[8,256,512]{2,1,0:T(8,128)(2,1)}), bf16[8,256,512]{2,1,0:T(8,128)(2,1)}, u32[]{:S(2)}, u32[]{:S(2)}) async-start(bf16[8,256,512]{2,1,0:T(8,128)(2,1)} %get-tuple-element.193), calls=%async_computation.6 | async-start | bytes 4194304 | tf_op jit(solution)/shard_map/all_to_all | solution.py:447
  431.4 60.3 %collective-permute-start.53 = (bf16[8,128,2048]{2,1,0:T(8,128)(2,1)S(1)}, bf16[8,128,2048]{2,1,0:T(8,128)(2,1)S(1)}, u32[]{:S(2)}, u32[]{:S(2)}) collective-permute-start(bf16[8,128,2048]{2,1,0:T(8,128)(2,1)S(1)} %pad_maximum_fusion.3), channel_id=1, source_target_pairs={{0,1},{1,0},{2,3},{3,2},{4,5},{5,4},{6,7},{7,6},{8,9},{9,8},{10,11... | collective-permute-start | bytes 12582920 | tf_op jit(solution)/shard_map/ppermute | solution.py:122
  534.2 55.3 %collective-permute-start.54 = (bf16[8,128,2048]{2,1,0:T(8,128)(2,1)}, bf16[8,128,2048]{2,1,0:T(8,128)(2,1)}, u32[]{:S(2)}, u32[]{:S(2)}) collective-permute-start(bf16[8,128,2048]{2,1,0:T(8,128)(2,1)} %pad_maximum_fusion.4), channel_id=1, source_target_pairs={{0,1},{1,0},{2,3},{3,2},{4,5},{5,4},{6,7},{7,6},{8,9},{9,8},{10,11... | collective-permute-start | bytes 12582920 | tf_op jit(solution)/shard_map/ppermute | solution.py:122
  558.0 40.6 %collective-permute-start.57 = (bf16[8,128,2048]{2,1,0:T(8,128)(2,1)}, bf16[8,128,2048]{2,1,0:T(8,128)(2,1)}, u32[]{:S(2)}, u32[]{:S(2)}) collective-permute-start(bf16[8,128,2048]{2,1,0:T(8,128)(2,1)} %pad_maximum_fusion.5), channel_id=1, source_target_pairs={{0,1},{1,0},{2,3},{3,2},{4,5},{5,4},{6,7},{7,6},{8,9},{9,8},{10,11... | collective-permute-start | bytes 12582920 | tf_op jit(solution)/shard_map/ppermute | solution.py:122
  710.5 67.6 %collective-permute-start.62 = (bf16[8,128,2048]{2,1,0:T(8,128)(2,1)}, bf16[8,128,2048]{2,1,0:T(8,128)(2,1)}, u32[]{:S(2)}, u32[]{:S(2)}) collective-permute-start(bf16[8,128,2048]{2,1,0:T(8,128)(2,1)} %bitcast.504), channel_id=1, source_target_pairs={{0,1},{1,0},{2,3},{3,2},{4,5},{5,4},{6,7},{7,6},{8,9},{9,8},{10,11... | collective-permute-start | bytes 12582920 | tf_op jit(solution)/shard_map/ppermute | solution.py:122
  792.4 55.9 %collective-permute-start.63 = (bf16[2,2,128,2048]{3,2,1,0:T(8,128)(2,1)}, bf16[2,2,128,2048]{3,2,1,0:T(8,128)(2,1)}, u32[]{:S(2)}, u32[]{:S(2)}) collective-permute-start(bf16[2,2,128,2048]{3,2,1,0:T(8,128)(2,1)} %fusion.15), channel_id=1, source_target_pairs={{0,2},{1,5},{2,0},{3,7},{4,6},{5,1},{6,4},{7,3},{8,10},{9,13},{10,... | collective-permute-start | bytes 6291464 | tf_op jit(solution)/shard_map/ppermute | solution.py:122
  793.6 109.2 %all-to-all-start.7 = ((bf16[8,256,512]{2,1,0:T(8,128)(2,1)}), bf16[8,256,512]{2,1,0:T(8,128)(2,1)S(1)}, u32[]{:S(2)}, u32[]{:S(2)}) async-start(bf16[8,256,512]{2,1,0:T(8,128)(2,1)} %bitcast.452), calls=%async_computation.7 | async-start | bytes 4194304 | tf_op jit(solution)/shard_map/all_to_all | solution.py:447
  956.8 40.8 %all-to-all-start.8 = ((bf16[4,128,512]{1,2,0:T(8,128)(2,1)}), bf16[4,128,512]{1,2,0:T(8,128)(2,1)}, u32[]{:S(2)}, u32[]{:S(2)}) async-start(bf16[4,128,512]{1,2,0:T(8,128)(2,1)} %bitcast.459), calls=%async_computation.8 | async-start | bytes 1048576 | tf_op jit(solution)/shard_map/all_to_all | solution.py:325
  997.6 55.0 %all-to-all-start.9 = ((bf16[8,256,512]{2,1,0:T(8,128)(2,1)}), bf16[8,256,512]{2,1,0:T(8,128)(2,1)}, u32[]{:S(2)}, u32[]{:S(2)}) async-start(bf16[8,256,512]{2,1,0:T(8,128)(2,1)} %bitcast.451), calls=%async_computation.9 | async-start | bytes 4194304 | tf_op jit(solution)/shard_map/all_to_all | solution.py:447
  1016.2 43.1 %collective-permute-start.84 = (bf16[8,64,2048]{2,1,0:T(8,128)(2,1)}, bf16[8,64,2048]{2,1,0:T(8,128)(2,1)}, u32[]{:S(2)}, u32[]{:S(2)}) collective-permute-start(bf16[8,64,2048]{2,1,0:T(8,128)(2,1)} %bitcast.116), channel_id=1, source_target_pairs={{0,1},{1,0},{2,3},{3,2},{4,5},{5,4},{6,7},{7,6},{8,9},{9,8},{10,11... | collective-permute-start | bytes 6291464 | tf_op jit(solution)/shard_map/ppermute | solution.py:122
  1052.7 50.3 %all-to-all-start.10 = ((bf16[8,256,512]{2,1,0:T(8,128)(2,1)}), bf16[8,256,512]{2,1,0:T(8,128)(2,1)}, u32[]{:S(2)}, u32[]{:S(2)}) async-start(bf16[8,256,512]{2,1,0:T(8,128)(2,1)} %bitcast.450), calls=%async_computation.10 | async-start | bytes 4194304 | tf_op jit(solution)/shard_map/all_to_all | solution.py:447
  1070.1 93.2 %collective-permute-start.86 = (bf16[128,2048]{1,0:T(8,128)(2,1)}, bf16[128,2048]{1,0:T(8,128)(2,1)}, u32[]{:S(2)}, u32[]{:S(2)}) collective-permute-start(bf16[128,2048]{1,0:T(8,128)(2,1)} %get-tuple-element.395), channel_id=1, source_target_pairs={{0,8},{1,9},{2,10},{3,11},{4,12},{5,13},{6,14},{7,15},{24,16},{25,... | collective-permute-start | bytes 1572872 | tf_op jit(solution)/shard_map/ppermute | solution.py:122
  1075.0 88.4 %collective-permute-start.87 = (bf16[128,2048]{1,0:T(8,128)(2,1)}, bf16[128,2048]{1,0:T(8,128)(2,1)}, u32[]{:S(2)}, u32[]{:S(2)}) collective-permute-start(bf16[128,2048]{1,0:T(8,128)(2,1)} %get-tuple-element.394), channel_id=1, source_target_pairs={{0,8},{1,9},{2,10},{3,11},{4,12},{5,13},{6,14},{7,15},{24,16},{25,... | collective-permute-start | bytes 1572872 | tf_op jit(solution)/shard_map/ppermute | solution.py:122
  1078.2 63.9 %collective-permute-start.91 = (bf16[2,2,64,2048]{3,2,1,0:T(8,128)(2,1)}, bf16[2,2,64,2048]{3,2,1,0:T(8,128)(2,1)}, u32[]{:S(2)}, u32[]{:S(2)}) collective-permute-start(bf16[2,2,64,2048]{3,2,1,0:T(8,128)(2,1)} %fusion.36), channel_id=1, source_target_pairs={{0,2},{1,5},{2,0},{3,7},{4,6},{5,1},{6,4},{7,3},{8,10},{9,13},{10,... | collective-permute-start | bytes 3145736 | tf_op jit(solution)/shard_map/ppermute | solution.py:122
  1110.3 43.0 %collective-permute-start.92 = (bf16[2,2,64,2048]{3,2,1,0:T(8,128)(2,1)}, bf16[2,2,64,2048]{3,2,1,0:T(8,128)(2,1)}, u32[]{:S(2)}, u32[]{:S(2)}) collective-permute-start(bf16[2,2,64,2048]{3,2,1,0:T(8,128)(2,1)} %fusion.37), channel_id=1, source_target_pairs={{0,2},{1,5},{2,0},{3,7},{4,6},{5,1},{6,4},{7,3},{8,10},{9,13},{10,... | collective-permute-start | bytes 3145736 | tf_op jit(solution)/shard_map/ppermute | solution.py:122
  1281.0 60.4 %all-to-all-start.13 = ((bf16[8,256,512]{2,1,0:T(8,128)(2,1)}), bf16[8,256,512]{2,1,0:T(8,128)(2,1)}, u32[]{:S(2)}, u32[]{:S(2)}) async-start(bf16[8,256,512]{2,1,0:T(8,128)(2,1)} %bitcast.449), calls=%async_computation.13 | async-start | bytes 4194304 | tf_op jit(solution)/shard_map/all_to_all | solution.py:447
  (273 other events, 4845.6 us)

commit v3 on v2

--- a/solution.py
+++ b/solution.py
@@ -643,10 +643,10 @@
         lifted = dot(cot, weight_down, ROWS_BACK)
         while len(hid_flow.hops) < 5:
             hid_flow.go()
-        hid_flow.go(lifted)
+        total = size * count
+        gate_dense = gates[:, i * size : (i + 1) * size].reshape(total, local)
+        hid_flow.go(lifted, gate_dense)
         hid = jnp.concatenate(hid_flow.finish()).reshape(-1, width)
-        total = hid.shape[0]
-        gate_dense = gates[:, i * size : (i + 1) * size].reshape(total, local)
         part = total // 4
         slotted = (count // 4, size, width)
         done = [None] * 4
@@ -693,8 +693,9 @@
         else:
             flow.go()
         third = weigh(2, *flow.hops[4])
-        fourth = weigh(3, *flow.hops[4])
-        flow.go(third, fourth)
+        flow.go(third)
+        if i < chunks - 1:
+            weigh(3)
         back_flows.append(flow)
         mix_flow = Flow(grid.scatter(mix, BF16))
         mix_flow.go(*flow.hops[4])
@@ -740,7 +741,8 @@
     out_flow = Flow(grid.scatter(out_parts))
     send(1, grad_mid_b)
     mix_flow.go(grad_mid_b)
-    grad_heads = after(grad_heads, *mix_flow.hops[1])
+    fourth = weigh(3, grad_attended)
+    grad_heads = after(grad_heads, fourth, *mix_flow.hops[1])
     send(2, grad_heads)
     mix_flow.go(grad_heads)
     out_flow.go(grad_heads)
@@ -778,14 +780,16 @@
     )
     proj_flow.go(home[1], home[2])
     send(3, grad_projected)
-    proj_flow.go(*mix_flow.hops[3], *out_flow.hops[1])
+    proj_flow.go(home[3], *mix_flow.hops[3], *out_flow.hops[1])
     mix_flow.go(*proj_flow.hops[0])
     out_flow.go(*proj_flow.hops[0])
-    proj_flow.go(*mix_flow.hops[4], *out_flow.hops[2])
+    grad_down_w += dot(after(act_gated, *proj_flow.hops[0]), cot, SUM_ROWS)
+    proj_flow.go(grad_down_w, *mix_flow.hops[4], *out_flow.hops[2])
     mix_flow.go(*proj_flow.hops[1])
     out_flow.go(*proj_flow.hops[1])
-    grad_down_w += dot(after(act_gated, *proj_flow.hops[0]), cot, SUM_ROWS)
-    proj_flow.go(*mix_flow.hops[5], *out_flow.hops[3])
+    home = after(home, *proj_flow.hops[1])
+    grad_expert_in = undeal(home) if ff == 128 else undeal_narrow(home, ff)
+    proj_flow.go(grad_expert_in, *mix_flow.hops[5], *out_flow.hops[3])
     out_flow.go(*proj_flow.hops[2])
     grad_proj = proj_flow.finish()
     block_out = middle + jnp.concatenate([f.finish() for f in mix_flows])
@@ -802,8 +806,6 @@
     gain_one = jnp.sum(grad_hidden1 * own, axis=0)
     input_grad = grad_middle + normalize_back(grad_hidden1 * gains[0], own, own_factor)
 
-    home = after(home, grad_proj)
-    grad_expert_in = undeal(home) if ff == 128 else undeal_narrow(home, ff)
 
     def widen(values):
         return lax.dynamic_update_slice_in_dim(jnp.zeros((width,), F32), values, group * span, 0)
@@ -823,6 +825,7 @@
         ],
         axis=1,
     )
+    last = after(last, *proj_flow.hops[2])
     last = grid.small_scatter(last.reshape(count, -1, 128 if last.shape[1] % 128 == 0 else 64))
     last = last.reshape(-1)
     grad_norm_gains = last[: 4 * rows].reshape(4, rows)

time: 1380 us -> 1340 us (0.971)
  local copies, waits for them, and re-layouts: 239 us -> 203 us
    ppermute x26, starting transfers between devices: 23.9 us -> 48.5 us  [flip(): return lax.ppermute(value, AXES, [(i, i ^ bit) for i in range(self.count)])]
    ppermute x26, waiting for transfers between devices: 88.9 us -> 68.2 us  [flip(): return lax.ppermute(value, AXES, [(i, i ^ bit) for i in range(self.count)])]
    ppermute x86, starting transfers between devices: 146 us -> 129 us  [move(): return lax.ppermute(value, AXES, pairs)]
    ppermute x86, waiting for transfers between devices: 235 us -> 252 us  [move(): return lax.ppermute(value, AXES, pairs)]
    unnamed x380 -> x360, local copies, waits for them, and re-layouts: 90.8 us -> 81.1 us
  transfers between devices with their start and end apart: 125 -> 125, of which waited for: 46 -> 43; matrix products, arithmetic and copies ran while one was open for 38% -> 36% of each run, Pallas kernels for 6% -> 7%
where the time goes in v3:
time: 1340 us; the launch traced here: 1320 us
  waiting for transfers between devices  372 us (28%)
  starting transfers between devices  241 us (18%)
  local copies, waits for them, and re-layouts  203 us (15%)
  matrix products  195 us (15%)
  other arithmetic  165 us (12%)
  Pallas kernels  122 us (9%)
  blocking collectives  15.8 us (1%)
    ppermute x86, waiting for transfers between devices, move(): return lax.ppermute(value, AXES, pairs)  252 us
    dot_general x23, matrix products, dot(): return lax.dot_general(left, right, dims, preferred_element_type=F32)  182 us
    ppermute x86, starting transfers between devices, move(): return lax.ppermute(value, AXES, pairs)  129 us
    pallas_call x4, Pallas kernels, moe_rows(): pl.pallas_call(functools.partial(moe_kernel, ff, local), grid=(total // t...  105 us
    unnamed x360, local copies, waits for them, and re-layouts  81.1 us
    ppermute x26, waiting for transfers between devices, flip(): return lax.ppermute(value, AXES, [(i, i ^ bit) for i in range(self.count)])  68.2 us
    ppermute x26, starting transfers between devices, flip(): return lax.ppermute(value, AXES, [(i, i ^ bit) for i in range(self.count)])  48.5 us
    all_to_all x8, starting transfers between devices, swap(): return lax.all_to_all(value, 'dp', split_axis=0, concat_axis=0, tiled=True)  43.7 us
  transfers between devices with their start and end apart: 125, of which 43 were waited for; matrix products, arithmetic and copies ran while one was open for 36% of the time, Pallas kernels for 7%

profile of v3, /device:TPU:0, one launch (start us, length us, event | category | flops | bytes accessed | tf_op | source)
XLA Modules:
  0.0 1324.9 jit_solution(6581700962900034668)
XLA Ops:
  4.6 15.8 %all_to_all.70 = bf16[4,64,1536]{2,1,0:T(8,128)(2,1)S(1)} all-to-all(bf16[4,64,1536]{2,1,0:T(8,128)(2,1)S(1)} %reshape.749), channel_id=1, replica_groups=mesh['dp'=8,'expert'=4] {'expert'}, dimensions={0} | all-to-all | bytes 1572864 | tf_op jit(solution)/shard_map/all_to_all | solution.py:325
  81.1 12.8 collective-permute-done.6
  103.4 30.6 %collective-permute-done.16 = bf16[64,2048]{1,0:T(8,128)(2,1)S(1)} collective-permute-done((bf16[64,2048]{1,0:T(8,128)(2,1)}, bf16[64,2048]{1,0:T(8,128)(2,1)S(1)}, u32[]{:S(2)}, u32[]{:S(2)}) %collective-permute-start.16) | collective-permute-done | bytes 262176 | tf_op jit(solution)/shard_map/ppermute | solution.py:122
  159.0 14.4 %collective-permute-done.7 = bf16[8,19,128]{2,1,0:T(8,128)(2,1)S(1)} collective-permute-done((bf16[8,19,128]{2,1,0:T(8,128)(2,1)S(1)}, bf16[8,19,128]{2,1,0:T(8,128)(2,1)S(1)}, u32[]{:S(2)}, u32[]{:S(2)}) %collective-permute-start.7) | collective-permute-done | bytes 38944 | tf_op jit(solution)/shard_map/ppermute | solution.py:298
  237.5 11.4 collective-permute-done.25
  293.7 13.7 %collective-permute-start.30 = (bf16[8,64,2048]{2,1,0:T(8,128)(2,1)}, bf16[8,64,2048]{2,1,0:T(8,128)(2,1)}, u32[]{:S(2)}, u32[]{:S(2)}) collective-permute-start(bf16[8,64,2048]{2,1,0:T(8,128)(2,1)} %pad_maximum_fusion.6), channel_id=1, source_target_pairs={{0,1},{1,0},{2,3},{3,2},{4,5},{5,4},{6,7},{7,6},{8,9},{9,8},{10,11... | collective-permute-start | bytes 6291464 | tf_op jit(solution)/shard_map/ppermute | solution.py:122
  320.1 11.2 collective-permute-done.32
  378.2 16.4 %all-to-all-done.6 = bf16[8,256,512]{2,1,0:T(8,128)(2,1)} async-done(((bf16[8,256,512]{2,1,0:T(8,128)(2,1)}), bf16[8,256,512]{2,1,0:T(8,128)(2,1)}, u32[]{:S(2)}, u32[]{:S(2)}) %all-to-all-start.6) | async-done | bytes 2097184 | tf_op jit(solution)/shard_map/all_to_all | solution.py:447
  444.3 12.9 collective-permute-done.47
  501.5 22.6 %fusion.118.lift_ref = f32[4096,1024]{1,0:T(8,128)} fusion(bf16[4096,2048]{1,0:T(8,128)(2,1)S(1)} %bitcast.464, bf16[1024,2048]{1,0:T(8,128)(2,1)} %bitcast.501), kind=kOutput, calls=%fused_computation.400 | convolution fusion | flops 17179869184 | bytes 37748736 | tf_op jit(solution)/shard_map/dot_general | solution.py:24
  570.5 26.2 %shard_map.234 = (bf16[1024,2048]{1,0:T(8,128)(2,1)}, bf16[1024,1024]{1,0:T(8,128)(2,1)}, f32[1024,8]{1,0:T(8,128)}, bf16[1024,2048]{1,0:T(8,128)(2,1)}) custom-call(bf16[4096,2048]{1,0:T(8,128)(2,1)} %bitcast.466, f32[4096,1024]{1,0:T(8,128)} %fusion.118.lift_ref, f32[4096,8]{1,0:T(8,128)} %bitcast.447, bf16[2048,2048]{1,0:T(8,128)(2,1)} %pad_maximum_fusion.w_ref), custom_call_target="tpu_custom_call" | custom-call | flops 17179869184 | bytes 25165824 | tf_op jit(solution)/shard_map/pallas_call | solution.py:365
  597.2 26.2 %shard_map.235 = (bf16[1024,2048]{1,0:T(8,128)(2,1)}, bf16[1024,1024]{1,0:T(8,128)(2,1)}, f32[1024,8]{1,0:T(8,128)}, f32[1024,2048]{1,0:T(8,128)}) custom-call(bf16[4096,2048]{1,0:T(8,128)(2,1)} %bitcast.467, f32[4096,1024]{1,0:T(8,128)} %fusion.118.lift_ref, f32[4096,8]{1,0:T(8,128)} %bitcast.448, bf16[2048,2048]{1,0:T(8,128)(2,1)} %pad_maximum_fusion.w_ref), custom_call_target="tpu_custom_call" | custom-call | flops 17179869184 | bytes 25165824 | tf_op jit(solution)/shard_map/pallas_call | solution.py:365
  636.2 26.1 %shard_map.236 = (bf16[1024,2048]{1,0:T(8,128)(2,1)}, bf16[1024,1024]{1,0:T(8,128)(2,1)}, f32[1024,8]{1,0:T(8,128)}, bf16[1024,2048]{1,0:T(8,128)(2,1)}) custom-call(bf16[4096,2048]{1,0:T(8,128)(2,1)} %bitcast.468, f32[4096,1024]{1,0:T(8,128)} %fusion.118.lift_ref, f32[4096,8]{1,0:T(8,128)} %bitcast.449, bf16[2048,2048]{1,0:T(8,128)(2,1)} %pad_maximum_fusion.w_ref), custom_call_target="tpu_custom_call" | custom-call | flops 17179869184 | bytes 25165824 | tf_op jit(solution)/shard_map/pallas_call | solution.py:365
  668.7 26.7 %shard_map.237 = (bf16[1024,2048]{1,0:T(8,128)(2,1)}, bf16[1024,1024]{1,0:T(8,128)(2,1)}, f32[1024,8]{1,0:T(8,128)}, f32[1024,2048]{1,0:T(8,128)}) custom-call(bf16[4096,2048]{1,0:T(8,128)(2,1)} %bitcast.469, f32[4096,1024]{1,0:T(8,128)} %fusion.118.lift_ref, f32[4096,8]{1,0:T(8,128)} %bitcast.450, bf16[2048,2048]{1,0:T(8,128)(2,1)} %pad_maximum_fusion.w_ref), custom_call_target="tpu_custom_call" | custom-call | flops 17179869184 | bytes 25165824 | tf_op jit(solution)/shard_map/pallas_call | solution.py:365
  708.2 19.5 %fusion.7 = bf16[2048,512]{1,0:T(8,128)(2,1)} fusion(bf16[4096,2048]{1,0:T(8,128)(2,1)} %bitcast.470, bf16[4096,2048]{1,0:T(8,128)(2,1)S(1)} %constant_dynamic-update-slice_fusion.36), kind=kOutput, calls=%fused_computation.23 | convolution fusion | flops 8589934592 | bytes 23068672 | tf_op jit(solution)/shard_map/dot_general | solution.py:24
  751.1 14.7 %fusion.1 = bf16[2048,512]{1,0:T(8,128)(2,1)} fusion(bf16[4096,2048]{1,0:T(8,128)(2,1)} %bitcast.471, bf16[4096,2048]{1,0:T(8,128)(2,1)} %copy-done.83), kind=kOutput, calls=%fused_computation.16 | convolution fusion | flops 8589934592 | bytes 23068672 | tf_op jit(solution)/shard_map/dot_general | solution.py:24
  766.0 22.3 %collective-permute-done.61 = bf16[2,128,2048]{2,1,0:T(8,128)(2,1)S(1)} collective-permute-done((bf16[2,128,2048]{2,1,0:T(8,128)(2,1)}, bf16[2,128,2048]{2,1,0:T(8,128)(2,1)S(1)}, u32[]{:S(2)}, u32[]{:S(2)}) %collective-permute-start.61) | collective-permute-done | bytes 1048608 | tf_op jit(solution)/shard_map/ppermute | solution.py:122
  826.8 14.6 %fusion.5 = bf16[2048,512]{1,0:T(8,128)(2,1)} fusion(bf16[4096,2048]{1,0:T(8,128)(2,1)} %bitcast.472, bf16[4096,2048]{1,0:T(8,128)(2,1)} %copy-done.83), kind=kOutput, calls=%fused_computation.20 | convolution fusion | flops 8589934592 | bytes 23068672 | tf_op jit(solution)/shard_map/dot_general | solution.py:24
  848.4 14.8 %fusion.3 = bf16[2048,512]{1,0:T(8,128)(2,1)} fusion(bf16[4096,2048]{1,0:T(8,128)(2,1)} %bitcast.473, bf16[4096,2048]{1,0:T(8,128)(2,1)} %copy-done.83), kind=kOutput, calls=%fused_computation.18 | convolution fusion | flops 8589934592 | bytes 23068672 | tf_op jit(solution)/shard_map/dot_general | solution.py:24
  914.3 17.0 %collective-permute-done.78 = bf16[2,2,128,2048]{3,2,1,0:T(8,128)(2,1)} collective-permute-done((bf16[2,2,128,2048]{3,2,1,0:T(8,128)(2,1)}, bf16[2,2,128,2048]{3,2,1,0:T(8,128)(2,1)}, u32[]{:S(2)}, u32[]{:S(2)}) %collective-permute-start.78) | collective-permute-done | bytes 2097184 | tf_op jit(solution)/shard_map/ppermute | solution.py:122
  1112.0 41.7 %collective-permute-done.88 = bf16[2,256,1536]{2,1,0:T(8,128)(2,1)} collective-permute-done((bf16[2,256,1536]{2,1,0:T(8,128)(2,1)}, bf16[2,256,1536]{2,1,0:T(8,128)(2,1)}, u32[]{:S(2)}, u32[]{:S(2)}) %collective-permute-start.88) | collective-permute-done | bytes 1572896 | tf_op jit(solution)/shard_map/ppermute | solution.py:122
  1173.4 24.1 %fusion.119 = f32[1024,2048]{1,0:T(8,128)} fusion(bf16[4096,1024]{1,0:T(8,128)(2,1)} %pad_maximum_fusion.1, bf16[4096,2048]{1,0:T(8,128)(2,1)} %bitcast.465), kind=kOutput, calls=%fused_computation.401 | convolution fusion | flops 17179869184 | bytes 33554432 | tf_op jit(solution)/shard_map/dot_general | solution.py:24
  1213.6 11.4 collective-permute-done.94
  1237.6 12.1 shard_map.238
  (893 shorter events, 854.1 us)
Async XLA Ops:
  76.3 57.8 %collective-permute-start.13 = (bf16[2,256,1536]{2,1,0:T(8,128)(2,1)S(1)}, bf16[2,256,1536]{2,1,0:T(8,128)(2,1)S(1)}, u32[]{:S(2)}, u32[]{:S(2)}) collective-permute-start(bf16[2,256,1536]{2,1,0:T(8,128)(2,1)S(1)} %pad_maximum_fusion.8), channel_id=1, source_target_pairs={{0,4},{1,5},{2,6},{3,7},{4,0},{5,1},{6,2},{7,3},{8,12},{9,13},{10,... | collective-permute-start | bytes 4718600 | tf_op jit(solution)/shard_map/ppermute | solution.py:122
  79.8 54.3 %collective-permute-start.12 = (bf16[256,1536]{1,0:T(8,128)(2,1)S(1)}, bf16[256,1536]{1,0:T(8,128)(2,1)S(1)}, u32[]{:S(2)}, u32[]{:S(2)}) collective-permute-start(bf16[256,1536]{1,0:T(8,128)(2,1)S(1)} %collective-permute-done.5), channel_id=1, source_target_pairs={{8,0},{9,1},{10,2},{11,3},{12,4},{13,5},{14,6},{15,7},{16,24},{17,... | collective-permute-start | bytes 2359304 | tf_op jit(solution)/shard_map/ppermute | solution.py:122
  136.0 61.0 %all-to-all-start.2 = ((bf16[8,256,512]{2,1,0:T(8,128)(2,1)}), bf16[8,256,512]{2,1,0:T(8,128)(2,1)}, u32[]{:S(2)}, u32[]{:S(2)}) async-start(bf16[8,256,512]{2,1,0:T(8,128)(2,1)} %get-tuple-element.178), calls=%async_computation.2 | async-start | bytes 4194304 | tf_op jit(solution)/shard_map/all_to_all | solution.py:447
  149.2 47.8 %collective-permute-start.19 = (bf16[2,256,1536]{2,1,0:T(8,128)(2,1)}, bf16[2,256,1536]{2,1,0:T(8,128)(2,1)}, u32[]{:S(2)}, u32[]{:S(2)}) collective-permute-start(bf16[2,256,1536]{2,1,0:T(8,128)(2,1)} %pad_maximum_fusion.9), channel_id=1, source_target_pairs={{0,4},{1,5},{2,6},{3,7},{4,0},{5,1},{6,2},{7,3},{8,12},{9,13},{10,... | collective-permute-start | bytes 4718600 | tf_op jit(solution)/shard_map/ppermute | solution.py:122
  197.0 52.9 %all-to-all-start.3 = ((bf16[8,256,512]{2,1,0:T(8,128)(2,1)}), bf16[8,256,512]{2,1,0:T(8,128)(2,1)}, u32[]{:S(2)}, u32[]{:S(2)}) async-start(bf16[8,256,512]{2,1,0:T(8,128)(2,1)} %get-tuple-element.180), calls=%async_computation.3 | async-start | bytes 4194304 | tf_op jit(solution)/shard_map/all_to_all | solution.py:447
  204.4 44.6 %collective-permute-start.28 = (bf16[2,128,2048]{2,1,0:T(8,128)(2,1)}, bf16[2,128,2048]{2,1,0:T(8,128)(2,1)}, u32[]{:S(2)}, u32[]{:S(2)}) collective-permute-start(bf16[2,128,2048]{2,1,0:T(8,128)(2,1)} %pad_maximum_fusion.11), channel_id=1, source_target_pairs={{0,4},{1,3},{2,6},{3,1},{4,0},{5,7},{6,2},{7,5},{8,12},{9,11},{10,... | collective-permute-start | bytes 3145736 | tf_op jit(solution)/shard_map/ppermute | solution.py:122
  276.7 61.7 %all-to-all-start.5 = ((bf16[8,256,512]{2,1,0:T(8,128)(2,1)}), bf16[8,256,512]{2,1,0:T(8,128)(2,1)S(1)}, u32[]{:S(2)}, u32[]{:S(2)}) async-start(bf16[8,256,512]{2,1,0:T(8,128)(2,1)} %get-tuple-element.188), calls=%async_computation.5 | async-start | bytes 4194304 | tf_op jit(solution)/shard_map/all_to_all | solution.py:447
  293.7 60.2 %collective-permute-start.30 = (bf16[8,64,2048]{2,1,0:T(8,128)(2,1)}, bf16[8,64,2048]{2,1,0:T(8,128)(2,1)}, u32[]{:S(2)}, u32[]{:S(2)}) collective-permute-start(bf16[8,64,2048]{2,1,0:T(8,128)(2,1)} %pad_maximum_fusion.6), channel_id=1, source_target_pairs={{0,1},{1,0},{2,3},{3,2},{4,5},{5,4},{6,7},{7,6},{8,9},{9,8},{10,11... | collective-permute-start | bytes 6291464 | tf_op jit(solution)/shard_map/ppermute | solution.py:122
  338.4 56.2 %all-to-all-start.6 = ((bf16[8,256,512]{2,1,0:T(8,128)(2,1)}), bf16[8,256,512]{2,1,0:T(8,128)(2,1)}, u32[]{:S(2)}, u32[]{:S(2)}) async-start(bf16[8,256,512]{2,1,0:T(8,128)(2,1)} %get-tuple-element.194), calls=%async_computation.6 | async-start | bytes 4194304 | tf_op jit(solution)/shard_map/all_to_all | solution.py:447
  421.0 57.7 %collective-permute-start.53 = (bf16[8,128,2048]{2,1,0:T(8,128)(2,1)S(1)}, bf16[8,128,2048]{2,1,0:T(8,128)(2,1)S(1)}, u32[]{:S(2)}, u32[]{:S(2)}) collective-permute-start(bf16[8,128,2048]{2,1,0:T(8,128)(2,1)S(1)} %pad_maximum_fusion.3), channel_id=1, source_target_pairs={{0,1},{1,0},{2,3},{3,2},{4,5},{5,4},{6,7},{7,6},{8,9},{9,8},{10,11... | collective-permute-start | bytes 12582920 | tf_op jit(solution)/shard_map/ppermute | solution.py:122
  488.1 49.5 %collective-permute-start.52 = (bf16[2,128,2048]{2,1,0:T(8,128)(2,1)S(1)}, bf16[2,128,2048]{2,1,0:T(8,128)(2,1)}, u32[]{:S(2)}, u32[]{:S(2)}) collective-permute-start(bf16[2,128,2048]{2,1,0:T(8,128)(2,1)S(1)} %collective-permute-done.46), channel_id=1, source_target_pairs={{0,2},{1,5},{2,0},{3,7},{4,6},{5,1},{6,4},{7,3},{8,10},{9,13},{10,... | collective-permute-start | bytes 3145736 | tf_op jit(solution)/shard_map/ppermute | solution.py:122
  662.3 67.3 %collective-permute-start.62 = (bf16[8,128,2048]{2,1,0:T(8,128)(2,1)}, bf16[8,128,2048]{2,1,0:T(8,128)(2,1)}, u32[]{:S(2)}, u32[]{:S(2)}) collective-permute-start(bf16[8,128,2048]{2,1,0:T(8,128)(2,1)} %bitcast.506), channel_id=1, source_target_pairs={{0,1},{1,0},{2,3},{3,2},{4,5},{5,4},{6,7},{7,6},{8,9},{9,8},{10,11... | collective-permute-start | bytes 12582920 | tf_op jit(solution)/shard_map/ppermute | solution.py:122
  744.6 60.6 %collective-permute-start.63 = (bf16[2,2,128,2048]{3,2,1,0:T(8,128)(2,1)}, bf16[2,2,128,2048]{3,2,1,0:T(8,128)(2,1)}, u32[]{:S(2)}, u32[]{:S(2)}) collective-permute-start(bf16[2,2,128,2048]{3,2,1,0:T(8,128)(2,1)} %fusion.15), channel_id=1, source_target_pairs={{0,2},{1,5},{2,0},{3,7},{4,6},{5,1},{6,4},{7,3},{8,10},{9,13},{10,... | collective-permute-start | bytes 6291464 | tf_op jit(solution)/shard_map/ppermute | solution.py:122
  746.9 95.0 %all-to-all-start.7 = ((bf16[8,256,512]{2,1,0:T(8,128)(2,1)}), bf16[8,256,512]{2,1,0:T(8,128)(2,1)S(1)}, u32[]{:S(2)}, u32[]{:S(2)}) async-start(bf16[8,256,512]{2,1,0:T(8,128)(2,1)} %bitcast.445), calls=%async_computation.7 | async-start | bytes 4194304 | tf_op jit(solution)/shard_map/all_to_all | solution.py:447
  949.3 53.4 %all-to-all-start.9 = ((bf16[8,256,512]{2,1,0:T(8,128)(2,1)}), bf16[8,256,512]{2,1,0:T(8,128)(2,1)}, u32[]{:S(2)}, u32[]{:S(2)}) async-start(bf16[8,256,512]{2,1,0:T(8,128)(2,1)} %bitcast.444), calls=%async_computation.9 | async-start | bytes 4194304 | tf_op jit(solution)/shard_map/all_to_all | solution.py:447
  1032.9 57.1 %all-to-all-start.10 = ((bf16[8,256,512]{2,1,0:T(8,128)(2,1)}), bf16[8,256,512]{2,1,0:T(8,128)(2,1)}, u32[]{:S(2)}, u32[]{:S(2)}) async-start(bf16[8,256,512]{2,1,0:T(8,128)(2,1)} %bitcast.443), calls=%async_computation.10 | async-start | bytes 4194304 | tf_op jit(solution)/shard_map/all_to_all | solution.py:447
  1059.9 98.5 %collective-permute-start.86 = (bf16[128,2048]{1,0:T(8,128)(2,1)}, bf16[128,2048]{1,0:T(8,128)(2,1)}, u32[]{:S(2)}, u32[]{:S(2)}) collective-permute-start(bf16[128,2048]{1,0:T(8,128)(2,1)} %get-tuple-element.397), channel_id=1, source_target_pairs={{0,8},{1,9},{2,10},{3,11},{4,12},{5,13},{6,14},{7,15},{24,16},{25,... | collective-permute-start | bytes 1572872 | tf_op jit(solution)/shard_map/ppermute | solution.py:122
  1064.7 93.7 %collective-permute-start.87 = (bf16[128,2048]{1,0:T(8,128)(2,1)}, bf16[128,2048]{1,0:T(8,128)(2,1)}, u32[]{:S(2)}, u32[]{:S(2)}) collective-permute-start(bf16[128,2048]{1,0:T(8,128)(2,1)} %get-tuple-element.396), channel_id=1, source_target_pairs={{0,8},{1,9},{2,10},{3,11},{4,12},{5,13},{6,14},{7,15},{24,16},{25,... | collective-permute-start | bytes 1572872 | tf_op jit(solution)/shard_map/ppermute | solution.py:122
  1090.1 73.9 %all-to-all-start.11 = ((bf16[8,256,512]{2,1,0:T(8,128)(2,1)}), bf16[8,256,512]{2,1,0:T(8,128)(2,1)}, u32[]{:S(2)}, u32[]{:S(2)}) async-start(bf16[8,256,512]{2,1,0:T(8,128)(2,1)} %bitcast.442), calls=%async_computation.11 | async-start | bytes 4194304 | tf_op jit(solution)/shard_map/all_to_all | solution.py:447
  1101.4 52.3 %collective-permute-start.88 = (bf16[2,256,1536]{2,1,0:T(8,128)(2,1)}, bf16[2,256,1536]{2,1,0:T(8,128)(2,1)}, u32[]{:S(2)}, u32[]{:S(2)}) collective-permute-start(bf16[2,256,1536]{2,1,0:T(8,128)(2,1)} %fusion.20), channel_id=1, source_target_pairs={{0,4},{1,5},{2,6},{3,7},{4,0},{5,1},{6,2},{7,3},{8,12},{9,13},{10,... | collective-permute-start | bytes 4718600 | tf_op jit(solution)/shard_map/ppermute | solution.py:122
  1161.0 52.6 %collective-permute-start.89 = (bf16[128,2048]{1,0:T(8,128)(2,1)}, bf16[128,2048]{1,0:T(8,128)(2,1)}, u32[]{:S(2)}, u32[]{:S(2)}) collective-permute-start(bf16[128,2048]{1,0:T(8,128)(2,1)} %get-tuple-element.395), channel_id=1, source_target_pairs={{8,16},{9,17},{10,18},{11,19},{12,20},{13,21},{14,22},{15,23},{16,... | collective-permute-start | bytes 1572872 | tf_op jit(solution)/shard_map/ppermute | solution.py:122
  1162.5 51.1 %collective-permute-start.90 = (bf16[128,2048]{1,0:T(8,128)(2,1)}, bf16[128,2048]{1,0:T(8,128)(2,1)}, u32[]{:S(2)}, u32[]{:S(2)}) collective-permute-start(bf16[128,2048]{1,0:T(8,128)(2,1)} %get-tuple-element.394), channel_id=1, source_target_pairs={{8,16},{9,17},{10,18},{11,19},{12,20},{13,21},{14,22},{15,23},{16,... | collective-permute-start | bytes 1572872 | tf_op jit(solution)/shard_map/ppermute | solution.py:122
  1166.1 47.5 %collective-permute-start.93 = (bf16[256,1536]{1,0:T(8,128)(2,1)S(1)}, bf16[256,1536]{1,0:T(8,128)(2,1)S(1)}, u32[]{:S(2)}, u32[]{:S(2)}) collective-permute-start(bf16[256,1536]{1,0:T(8,128)(2,1)S(1)} %get-tuple-element.381), channel_id=1, source_target_pairs={{0,8},{1,9},{2,10},{3,11},{4,12},{5,13},{6,14},{7,15},{24,16},{25,... | collective-permute-start | bytes 2359304 | tf_op jit(solution)/shard_map/ppermute | solution.py:122
  1212.4 65.1 %collective-permute-start.96 = (bf16[2,256,1536]{2,1,0:T(8,128)(2,1)}, bf16[2,256,1536]{2,1,0:T(8,128)(2,1)}, u32[]{:S(2)}, u32[]{:S(2)}) collective-permute-start(bf16[2,256,1536]{2,1,0:T(8,128)(2,1)} %fusion.21), channel_id=1, source_target_pairs={{0,4},{1,5},{2,6},{3,7},{4,0},{5,1},{6,2},{7,3},{8,12},{9,13},{10,... | collective-permute-start | bytes 4718600 | tf_op jit(solution)/shard_map/ppermute | solution.py:122
  (263 other events, 4714.2 us)

commit v4 on v3

--- a/solution.py
+++ b/solution.py
@@ -312,6 +312,16 @@
         while bit:
             held = held[:bit] + self.flip(held[bit:], bit)
             bit //= 2
+        return held[0]
+
+    def small_sum(self, value):
+        held, bit = value[self.linear ^ jnp.arange(self.count)], 1
+        while bit < self.count:
+            events = yield (held,)
+            held = after(held, *events)
+            held = held.reshape((held.shape[0] // 2, 2) + held.shape[1:])
+            held = held[:, 0] + self.flip(held[:, 1], bit)
+            bit *= 2
         return held[0]
 
     def group_sum(self, value):
@@ -740,6 +750,7 @@
     ]
     out_flow = Flow(grid.scatter(out_parts))
     send(1, grad_mid_b)
+    out_flow.go(grad_mid_b)
     mix_flow.go(grad_mid_b)
     fourth = weigh(3, grad_attended)
     grad_heads = after(grad_heads, fourth, *mix_flow.hops[1])
@@ -755,7 +766,7 @@
     up_q, up_k = grad_qscaled * gain_q, grad_kscaled * gain_k
     along = jnp.stack([jnp.sum(up_q * query_normed, axis=-1), jnp.sum(up_k * key_normed, axis=-1)])
     along = (grid.group_sum(along) / width)[:, :, None]
-    along = after(along, *mix_flow.hops[2], *out_flow.hops[0])
+    along = after(along, *mix_flow.hops[2], *out_flow.hops[1])
     mix_flow.go(along)
     out_flow.go(along)
     grad_projected = jnp.concatenate(
@@ -780,16 +791,16 @@
     )
     proj_flow.go(home[1], home[2])
     send(3, grad_projected)
-    proj_flow.go(home[3], *mix_flow.hops[3], *out_flow.hops[1])
+    proj_flow.go(home[3], *mix_flow.hops[3], *out_flow.hops[2])
     mix_flow.go(*proj_flow.hops[0])
     out_flow.go(*proj_flow.hops[0])
     grad_down_w += dot(after(act_gated, *proj_flow.hops[0]), cot, SUM_ROWS)
-    proj_flow.go(grad_down_w, *mix_flow.hops[4], *out_flow.hops[2])
+    proj_flow.go(grad_down_w, *mix_flow.hops[4], *out_flow.hops[3])
     mix_flow.go(*proj_flow.hops[1])
     out_flow.go(*proj_flow.hops[1])
     home = after(home, *proj_flow.hops[1])
     grad_expert_in = undeal(home) if ff == 128 else undeal_narrow(home, ff)
-    proj_flow.go(grad_expert_in, *mix_flow.hops[5], *out_flow.hops[3])
+    proj_flow.go(grad_expert_in, *mix_flow.hops[5], *out_flow.hops[4])
     out_flow.go(*proj_flow.hops[2])
     grad_proj = proj_flow.finish()
     block_out = middle + jnp.concatenate([f.finish() for f in mix_flows])
@@ -825,8 +836,13 @@
         ],
         axis=1,
     )
-    last = after(last, *proj_flow.hops[2])
-    last = grid.small_scatter(last.reshape(count, -1, 128 if last.shape[1] % 128 == 0 else 64))
+    last = last.reshape(count, -1, 128 if last.shape[1] % 128 == 0 else 64)
+    last_flow = Flow(grid.small_sum(last))
+    last_flow.go(*proj_flow.hops[0])
+    last_flow.go(*proj_flow.hops[1])
+    last_flow.go(*proj_flow.hops[1])
+    last_flow.go(grad_proj)
+    last = last_flow.finish()
     last = last.reshape(-1)
     grad_norm_gains = last[: 4 * rows].reshape(4, rows)
     grad_router = last[4 * rows :].reshape(rows, expert_count)

time: 1340 us -> 1390 us (1.037)
  local copies, waits for them, and re-layouts: 203 us -> 230 us
    ppermute x26, starting transfers between devices: 48.5 us -> 25.8 us  [flip(): return lax.ppermute(value, AXES, [(i, i ^ bit) for i in range(self.count)])]
    ppermute x86, starting transfers between devices: 129 us -> 144 us  [move(): return lax.ppermute(value, AXES, pairs)]
    unnamed x360 -> x343, local copies, waits for them, and re-layouts: 81.1 us -> 94 us
  transfers between devices with their start and end apart: 125 -> 125, of which waited for: 43 -> 46; matrix products, arithmetic and copies ran while one was open for 36% -> 39% of each run, Pallas kernels for 7% -> 7%
where the time goes in v4:
time: 1390 us; the launch traced here: 1370 us
  waiting for transfers between devices  374 us (27%)
  starting transfers between devices  242 us (17%)
  local copies, waits for them, and re-layouts  230 us (17%)
  matrix products  201 us (14%)
  other arithmetic  176 us (13%)
  Pallas kernels  122 us (9%)
  blocking collectives  15.8 us (1%)
    ppermute x86, waiting for transfers between devices, move(): return lax.ppermute(value, AXES, pairs)  244 us
    dot_general x23, matrix products, dot(): return lax.dot_general(left, right, dims, preferred_element_type=F32)  188 us
    ppermute x86, starting transfers between devices, move(): return lax.ppermute(value, AXES, pairs)  144 us
    pallas_call x4, Pallas kernels, moe_rows(): pl.pallas_call(functools.partial(moe_kernel, ff, local), grid=(total // t...  105 us
    unnamed x343, local copies, waits for them, and re-layouts  94 us
    ppermute x26, waiting for transfers between devices, flip(): return lax.ppermute(value, AXES, [(i, i ^ bit) for i in range(self.count)])  68.3 us
    add x14, other arithmetic, line_reduce(): return slots[0] + sent(slots[1])  48.3 us
    all_to_all x8, starting transfers between devices, swap(): return lax.all_to_all(value, 'dp', split_axis=0, concat_axis=0, tiled=True)  46.3 us
  transfers between devices with their start and end apart: 125, of which 46 were waited for; matrix products, arithmetic and copies ran while one was open for 39% of the time, Pallas kernels for 7%

profile of v4, /device:TPU:0, one launch (start us, length us, event | category | flops | bytes accessed | tf_op | source)
XLA Modules:
  0.0 1372.0 jit_solution(4861185971064301685)
XLA Ops:
  4.6 15.8 %all_to_all.70 = bf16[4,64,1536]{2,1,0:T(8,128)(2,1)S(1)} all-to-all(bf16[4,64,1536]{2,1,0:T(8,128)(2,1)S(1)} %reshape.760), channel_id=1, replica_groups=mesh['dp'=8,'expert'=4] {'expert'}, dimensions={0} | all-to-all | bytes 1572864 | tf_op jit(solution)/shard_map/all_to_all | solution.py:335
  81.0 12.7 collective-permute-done.6
  104.1 29.9 %collective-permute-done.16 = bf16[64,2048]{1,0:T(8,128)(2,1)S(1)} collective-permute-done((bf16[64,2048]{1,0:T(8,128)(2,1)}, bf16[64,2048]{1,0:T(8,128)(2,1)S(1)}, u32[]{:S(2)}, u32[]{:S(2)}) %collective-permute-start.16) | collective-permute-done | bytes 262176 | tf_op jit(solution)/shard_map/ppermute | solution.py:122
  158.2 14.9 %collective-permute-done.7 = bf16[8,19,128]{2,1,0:T(8,128)(2,1)S(1)} collective-permute-done((bf16[8,19,128]{2,1,0:T(8,128)(2,1)S(1)}, bf16[8,19,128]{2,1,0:T(8,128)(2,1)S(1)}, u32[]{:S(2)}, u32[]{:S(2)}) %collective-permute-start.7) | collective-permute-done | bytes 38944 | tf_op jit(solution)/shard_map/ppermute | solution.py:298
  302.6 14.0 %collective-permute-start.30 = (bf16[8,64,2048]{2,1,0:T(8,128)(2,1)}, bf16[8,64,2048]{2,1,0:T(8,128)(2,1)}, u32[]{:S(2)}, u32[]{:S(2)}) collective-permute-start(bf16[8,64,2048]{2,1,0:T(8,128)(2,1)} %pad_maximum_fusion.6), channel_id=1, source_target_pairs={{0,1},{1,0},{2,3},{3,2},{4,5},{5,4},{6,7},{7,6},{8,9},{9,8},{10,11... | collective-permute-start | bytes 6291464 | tf_op jit(solution)/shard_map/ppermute | solution.py:122
  390.5 16.4 %all-to-all-done.6 = bf16[8,256,512]{2,1,0:T(8,128)(2,1)} async-done(((bf16[8,256,512]{2,1,0:T(8,128)(2,1)}), bf16[8,256,512]{2,1,0:T(8,128)(2,1)}, u32[]{:S(2)}, u32[]{:S(2)}) %all-to-all-start.6) | async-done | bytes 2097184 | tf_op jit(solution)/shard_map/all_to_all | solution.py:457
  473.1 13.7 collective-permute-done.45
  498.2 12.5 collective-permute-done.50
  512.0 22.7 %fusion.124.lift_ref = f32[4096,1024]{1,0:T(8,128)} fusion(bf16[4096,2048]{1,0:T(8,128)(2,1)} %bitcast.60, bf16[1024,2048]{1,0:T(8,128)(2,1)S(1)} %bitcast.542), kind=kOutput, calls=%fused_computation.408 | convolution fusion | flops 17179869184 | bytes 37748736 | tf_op jit(solution)/shard_map/dot_general | solution.py:24
  583.6 26.2 %shard_map.234 = (bf16[1024,2048]{1,0:T(8,128)(2,1)}, bf16[1024,1024]{1,0:T(8,128)(2,1)}, f32[1024,8]{1,0:T(8,128)}, bf16[1024,2048]{1,0:T(8,128)(2,1)}) custom-call(bf16[4096,2048]{1,0:T(8,128)(2,1)} %bitcast.505, f32[4096,1024]{1,0:T(8,128)} %fusion.124.lift_ref, f32[4096,8]{1,0:T(8,128)} %bitcast.479, bf16[2048,2048]{1,0:T(8,128)(2,1)} %pad_maximum_fusion.w_ref), custom_call_target="tpu_custom_call" | custom-call | flops 17179869184 | bytes 25165824 | tf_op jit(solution)/shard_map/pallas_call | solution.py:375
  622.9 26.2 %shard_map.235 = (bf16[1024,2048]{1,0:T(8,128)(2,1)}, bf16[1024,1024]{1,0:T(8,128)(2,1)}, f32[1024,8]{1,0:T(8,128)}, f32[1024,2048]{1,0:T(8,128)}) custom-call(bf16[4096,2048]{1,0:T(8,128)(2,1)} %bitcast.506, f32[4096,1024]{1,0:T(8,128)} %fusion.124.lift_ref, f32[4096,8]{1,0:T(8,128)} %bitcast.480, bf16[2048,2048]{1,0:T(8,128)(2,1)} %pad_maximum_fusion.w_ref), custom_call_target="tpu_custom_call" | custom-call | flops 17179869184 | bytes 25165824 | tf_op jit(solution)/shard_map/pallas_call | solution.py:375
  663.1 26.1 %shard_map.236 = (bf16[1024,2048]{1,0:T(8,128)(2,1)}, bf16[1024,1024]{1,0:T(8,128)(2,1)}, f32[1024,8]{1,0:T(8,128)}, bf16[1024,2048]{1,0:T(8,128)(2,1)}) custom-call(bf16[4096,2048]{1,0:T(8,128)(2,1)} %bitcast.507, f32[4096,1024]{1,0:T(8,128)} %fusion.124.lift_ref, f32[4096,8]{1,0:T(8,128)} %bitcast.481, bf16[2048,2048]{1,0:T(8,128)(2,1)} %pad_maximum_fusion.w_ref), custom_call_target="tpu_custom_call" | custom-call | flops 17179869184 | bytes 25165824 | tf_op jit(solution)/shard_map/pallas_call | solution.py:375
  697.3 26.7 %shard_map.237 = (bf16[1024,2048]{1,0:T(8,128)(2,1)}, bf16[1024,1024]{1,0:T(8,128)(2,1)}, f32[1024,8]{1,0:T(8,128)}, f32[1024,2048]{1,0:T(8,128)}) custom-call(bf16[4096,2048]{1,0:T(8,128)(2,1)} %bitcast.508, f32[4096,1024]{1,0:T(8,128)} %fusion.124.lift_ref, f32[4096,8]{1,0:T(8,128)} %bitcast.482, bf16[2048,2048]{1,0:T(8,128)(2,1)} %pad_maximum_fusion.w_ref), custom_call_target="tpu_custom_call" | custom-call | flops 17179869184 | bytes 25165824 | tf_op jit(solution)/shard_map/pallas_call | solution.py:375
  739.1 19.5 %fusion.7 = bf16[2048,512]{1,0:T(8,128)(2,1)} fusion(bf16[4096,2048]{1,0:T(8,128)(2,1)} %bitcast.509, bf16[4096,2048]{1,0:T(8,128)(2,1)S(1)} %constant_dynamic-update-slice_fusion.36), kind=kOutput, calls=%fused_computation.23 | convolution fusion | flops 8589934592 | bytes 23068672 | tf_op jit(solution)/shard_map/dot_general | solution.py:24
  781.3 15.2 %fusion.1 = bf16[2048,512]{1,0:T(8,128)(2,1)} fusion(bf16[4096,2048]{1,0:T(8,128)(2,1)} %bitcast.510, bf16[4096,2048]{1,0:T(8,128)(2,1)} %copy-done.79), kind=kOutput, calls=%fused_computation.16 | convolution fusion | flops 8589934592 | bytes 23068672 | tf_op jit(solution)/shard_map/dot_general | solution.py:24
  796.5 14.6 %collective-permute-done.75 = f32[2,32,128]{2,1,0:T(8,128)S(1)} collective-permute-done((f32[2,32,128]{2,1,0:T(8,128)S(1)}, f32[2,32,128]{2,1,0:T(8,128)S(1)}, u32[]{:S(2)}, u32[]{:S(2)}) %collective-permute-start.75) | collective-permute-done | bytes 32800 | tf_op jit(solution)/shard_map/ppermute | solution.py:298
  850.0 14.8 %fusion.5 = bf16[2048,512]{1,0:T(8,128)(2,1)} fusion(bf16[4096,2048]{1,0:T(8,128)(2,1)} %bitcast.511, bf16[4096,2048]{1,0:T(8,128)(2,1)} %copy-done.79), kind=kOutput, calls=%fused_computation.20 | convolution fusion | flops 8589934592 | bytes 23068672 | tf_op jit(solution)/shard_map/dot_general | solution.py:24
  887.9 14.8 %fusion.3 = bf16[2048,512]{1,0:T(8,128)(2,1)} fusion(bf16[4096,2048]{1,0:T(8,128)(2,1)} %bitcast.512, bf16[4096,2048]{1,0:T(8,128)(2,1)} %copy-done.79), kind=kOutput, calls=%fused_computation.18 | convolution fusion | flops 8589934592 | bytes 23068672 | tf_op jit(solution)/shard_map/dot_general | solution.py:24
  975.0 18.8 %collective-permute-done.78 = bf16[2,2,128,2048]{3,2,1,0:T(8,128)(2,1)} collective-permute-done((bf16[2,2,128,2048]{3,2,1,0:T(8,128)(2,1)}, bf16[2,2,128,2048]{3,2,1,0:T(8,128)(2,1)}, u32[]{:S(2)}, u32[]{:S(2)}) %collective-permute-start.78) | collective-permute-done | bytes 2097184 | tf_op jit(solution)/shard_map/ppermute | solution.py:122
  1034.1 14.1 %all-to-all-done.9.refs_1_ = bf16[8,256,512]{2,1,0:T(8,128)(2,1)} async-done(((bf16[8,256,512]{2,1,0:T(8,128)(2,1)}), bf16[8,256,512]{2,1,0:T(8,128)(2,1)}, u32[]{:S(2)}, u32[]{:S(2)}) %all-to-all-start.9) | async-done | bytes 2097184 | tf_op jit(solution)/shard_map/all_to_all | solution.py:457
  1054.9 16.8 %collective-permute-done.79 = bf16[2,128,2048]{2,1,0:T(8,128)(2,1)} collective-permute-done((bf16[2,128,2048]{2,1,0:T(8,128)(2,1)}, bf16[2,128,2048]{2,1,0:T(8,128)(2,1)}, u32[]{:S(2)}, u32[]{:S(2)}) %collective-permute-start.79) | collective-permute-done | bytes 1048608 | tf_op jit(solution)/shard_map/ppermute | solution.py:122
  1160.6 40.6 %collective-permute-done.90 = bf16[2,256,1536]{2,1,0:T(8,128)(2,1)} collective-permute-done((bf16[2,256,1536]{2,1,0:T(8,128)(2,1)}, bf16[2,256,1536]{2,1,0:T(8,128)(2,1)}, u32[]{:S(2)}, u32[]{:S(2)}) %collective-permute-start.90) | collective-permute-done | bytes 1572896 | tf_op jit(solution)/shard_map/ppermute | solution.py:122
  1223.2 24.4 %fusion.125 = f32[1024,2048]{1,0:T(8,128)} fusion(bf16[4096,1024]{1,0:T(8,128)(2,1)} %pad_maximum_fusion.1, bf16[4096,2048]{1,0:T(8,128)(2,1)} %bitcast.60), kind=kOutput, calls=%fused_computation.409 | convolution fusion | flops 17179869184 | bytes 33554432 | tf_op jit(solution)/shard_map/dot_general | solution.py:24
  1287.9 29.0 %collective-permute-start.105 = (bf16[256,1536]{1,0:T(8,128)(2,1)S(1)}, bf16[256,1536]{1,0:T(8,128)(2,1)S(1)}, u32[]{:S(2)}, u32[]{:S(2)}) collective-permute-start(bf16[256,1536]{1,0:T(8,128)(2,1)S(1)} %fusion.22), channel_id=1, source_target_pairs={{0,8},{1,9},{2,10},{3,11},{4,12},{5,13},{6,14},{7,15},{8,0},{9,1},... | collective-permute-start | bytes 2359304 | tf_op jit(solution)/shard_map/ppermute | solution.py:122
  (876 shorter events, 880.2 us)
Async XLA Ops:
  76.2 57.8 %collective-permute-start.13 = (bf16[2,256,1536]{2,1,0:T(8,128)(2,1)S(1)}, bf16[2,256,1536]{2,1,0:T(8,128)(2,1)S(1)}, u32[]{:S(2)}, u32[]{:S(2)}) collective-permute-start(bf16[2,256,1536]{2,1,0:T(8,128)(2,1)S(1)} %pad_maximum_fusion.8), channel_id=1, source_target_pairs={{0,4},{1,5},{2,6},{3,7},{4,0},{5,1},{6,2},{7,3},{8,12},{9,13},{10,... | collective-permute-start | bytes 4718600 | tf_op jit(solution)/shard_map/ppermute | solution.py:122
  79.8 54.2 %collective-permute-start.12 = (bf16[256,1536]{1,0:T(8,128)(2,1)S(1)}, bf16[256,1536]{1,0:T(8,128)(2,1)S(1)}, u32[]{:S(2)}, u32[]{:S(2)}) collective-permute-start(bf16[256,1536]{1,0:T(8,128)(2,1)S(1)} %collective-permute-done.5), channel_id=1, source_target_pairs={{8,0},{9,1},{10,2},{11,3},{12,4},{13,5},{14,6},{15,7},{16,24},{17,... | collective-permute-start | bytes 2359304 | tf_op jit(solution)/shard_map/ppermute | solution.py:122
  135.8 61.7 %all-to-all-start.2 = ((bf16[8,256,512]{2,1,0:T(8,128)(2,1)}), bf16[8,256,512]{2,1,0:T(8,128)(2,1)}, u32[]{:S(2)}, u32[]{:S(2)}) async-start(bf16[8,256,512]{2,1,0:T(8,128)(2,1)} %get-tuple-element.184), calls=%async_computation.2 | async-start | bytes 4194304 | tf_op jit(solution)/shard_map/all_to_all | solution.py:457
  149.1 48.4 %collective-permute-start.19 = (bf16[2,256,1536]{2,1,0:T(8,128)(2,1)}, bf16[2,256,1536]{2,1,0:T(8,128)(2,1)}, u32[]{:S(2)}, u32[]{:S(2)}) collective-permute-start(bf16[2,256,1536]{2,1,0:T(8,128)(2,1)} %pad_maximum_fusion.9), channel_id=1, source_target_pairs={{0,4},{1,5},{2,6},{3,7},{4,0},{5,1},{6,2},{7,3},{8,12},{9,13},{10,... | collective-permute-start | bytes 4718600 | tf_op jit(solution)/shard_map/ppermute | solution.py:122
  197.5 53.7 %all-to-all-start.3 = ((bf16[8,256,512]{2,1,0:T(8,128)(2,1)}), bf16[8,256,512]{2,1,0:T(8,128)(2,1)}, u32[]{:S(2)}, u32[]{:S(2)}) async-start(bf16[8,256,512]{2,1,0:T(8,128)(2,1)} %get-tuple-element.186), calls=%async_computation.3 | async-start | bytes 4194304 | tf_op jit(solution)/shard_map/all_to_all | solution.py:457
  281.7 65.9 %all-to-all-start.5 = ((bf16[8,256,512]{2,1,0:T(8,128)(2,1)}), bf16[8,256,512]{2,1,0:T(8,128)(2,1)}, u32[]{:S(2)}, u32[]{:S(2)}) async-start(bf16[8,256,512]{2,1,0:T(8,128)(2,1)} %get-tuple-element.194), calls=%async_computation.5 | async-start | bytes 4194304 | tf_op jit(solution)/shard_map/all_to_all | solution.py:457
  302.6 63.6 %collective-permute-start.30 = (bf16[8,64,2048]{2,1,0:T(8,128)(2,1)}, bf16[8,64,2048]{2,1,0:T(8,128)(2,1)}, u32[]{:S(2)}, u32[]{:S(2)}) collective-permute-start(bf16[8,64,2048]{2,1,0:T(8,128)(2,1)} %pad_maximum_fusion.6), channel_id=1, source_target_pairs={{0,1},{1,0},{2,3},{3,2},{4,5},{5,4},{6,7},{7,6},{8,9},{9,8},{10,11... | collective-permute-start | bytes 6291464 | tf_op jit(solution)/shard_map/ppermute | solution.py:122
  347.7 59.3 %all-to-all-start.6 = ((bf16[8,256,512]{2,1,0:T(8,128)(2,1)}), bf16[8,256,512]{2,1,0:T(8,128)(2,1)}, u32[]{:S(2)}, u32[]{:S(2)}) async-start(bf16[8,256,512]{2,1,0:T(8,128)(2,1)} %get-tuple-element.200), calls=%async_computation.6 | async-start | bytes 4194304 | tf_op jit(solution)/shard_map/all_to_all | solution.py:457
  431.9 61.3 %collective-permute-start.53 = (bf16[8,128,2048]{2,1,0:T(8,128)(2,1)S(1)}, bf16[8,128,2048]{2,1,0:T(8,128)(2,1)S(1)}, u32[]{:S(2)}, u32[]{:S(2)}) collective-permute-start(bf16[8,128,2048]{2,1,0:T(8,128)(2,1)S(1)} %pad_maximum_fusion.3), channel_id=1, source_target_pairs={{0,1},{1,0},{2,3},{3,2},{4,5},{5,4},{6,7},{7,6},{8,9},{9,8},{10,11... | collective-permute-start | bytes 12582920 | tf_op jit(solution)/shard_map/ppermute | solution.py:122
  689.2 69.4 %collective-permute-start.62 = (bf16[8,128,2048]{2,1,0:T(8,128)(2,1)}, bf16[8,128,2048]{2,1,0:T(8,128)(2,1)}, u32[]{:S(2)}, u32[]{:S(2)}) collective-permute-start(bf16[8,128,2048]{2,1,0:T(8,128)(2,1)} %bitcast.547), channel_id=1, source_target_pairs={{0,1},{1,0},{2,3},{3,2},{4,5},{5,4},{6,7},{7,6},{8,9},{9,8},{10,11... | collective-permute-start | bytes 12582920 | tf_op jit(solution)/shard_map/ppermute | solution.py:122
  773.1 65.2 %collective-permute-start.63 = (bf16[2,2,128,2048]{3,2,1,0:T(8,128)(2,1)}, bf16[2,2,128,2048]{3,2,1,0:T(8,128)(2,1)}, u32[]{:S(2)}, u32[]{:S(2)}) collective-permute-start(bf16[2,2,128,2048]{3,2,1,0:T(8,128)(2,1)} %fusion.15), channel_id=1, source_target_pairs={{0,2},{1,5},{2,0},{3,7},{4,6},{5,1},{6,4},{7,3},{8,10},{9,13},{10,... | collective-permute-start | bytes 6291464 | tf_op jit(solution)/shard_map/ppermute | solution.py:122
  774.3 45.2 %collective-permute-start.61 = (bf16[2,128,2048]{2,1,0:T(8,128)(2,1)}, bf16[2,128,2048]{2,1,0:T(8,128)(2,1)}, u32[]{:S(2)}, u32[]{:S(2)}) collective-permute-start(bf16[2,128,2048]{2,1,0:T(8,128)(2,1)} %fusion.34), channel_id=1, source_target_pairs={{0,4},{1,3},{2,6},{3,1},{4,0},{5,7},{6,2},{7,5},{8,12},{9,11},{10,... | collective-permute-start | bytes 3145736 | tf_op jit(solution)/shard_map/ppermute | solution.py:122
  775.8 103.7 %all-to-all-start.7 = ((bf16[8,256,512]{2,1,0:T(8,128)(2,1)}), bf16[8,256,512]{2,1,0:T(8,128)(2,1)S(1)}, u32[]{:S(2)}, u32[]{:S(2)}) async-start(bf16[8,256,512]{2,1,0:T(8,128)(2,1)} %bitcast.478), calls=%async_computation.7 | async-start | bytes 4194304 | tf_op jit(solution)/shard_map/all_to_all | solution.py:457
  878.7 50.8 %collective-permute-start.69 = (bf16[8,128,2048]{2,1,0:T(8,128)(2,1)}, bf16[8,128,2048]{2,1,0:T(8,128)(2,1)}, u32[]{:S(2)}, u32[]{:S(2)}) collective-permute-start(bf16[8,128,2048]{2,1,0:T(8,128)(2,1)} %bitcast.75), channel_id=1, source_target_pairs={{0,1},{1,0},{2,3},{3,2},{4,5},{5,4},{6,7},{7,6},{8,9},{9,8},{10,11... | collective-permute-start | bytes 12582920 | tf_op jit(solution)/shard_map/ppermute | solution.py:122
  879.5 55.6 %collective-permute-start.70 = (bf16[8,128,2048]{2,1,0:T(8,128)(2,1)}, bf16[8,128,2048]{2,1,0:T(8,128)(2,1)}, u32[]{:S(2)}, u32[]{:S(2)}) collective-permute-start(bf16[8,128,2048]{2,1,0:T(8,128)(2,1)} %bitcast.81), channel_id=1, source_target_pairs={{0,1},{1,0},{2,3},{3,2},{4,5},{5,4},{6,7},{7,6},{8,9},{9,8},{10,11... | collective-permute-start | bytes 12582920 | tf_op jit(solution)/shard_map/ppermute | solution.py:122
  944.3 49.5 %collective-permute-start.78 = (bf16[2,2,128,2048]{3,2,1,0:T(8,128)(2,1)}, bf16[2,2,128,2048]{3,2,1,0:T(8,128)(2,1)}, u32[]{:S(2)}, u32[]{:S(2)}) collective-permute-start(bf16[2,2,128,2048]{3,2,1,0:T(8,128)(2,1)} %slice_bitcast_fusion.1), channel_id=1, source_target_pairs={{0,2},{1,5},{2,0},{3,7},{4,6},{5,1},{6,4},{7,3},{8,10},{9,13},{10,... | collective-permute-start | bytes 6291464 | tf_op jit(solution)/shard_map/ppermute | solution.py:122
  946.5 50.9 %all-to-all-start.8 = ((bf16[4,128,512]{1,2,0:T(8,128)(2,1)}), bf16[4,128,512]{1,2,0:T(8,128)(2,1)}, u32[]{:S(2)}, u32[]{:S(2)}) async-start(bf16[4,128,512]{1,2,0:T(8,128)(2,1)} %bitcast.485), calls=%async_computation.8 | async-start | bytes 1048576 | tf_op jit(solution)/shard_map/all_to_all | solution.py:335
  997.5 50.8 %all-to-all-start.9 = ((bf16[8,256,512]{2,1,0:T(8,128)(2,1)}), bf16[8,256,512]{2,1,0:T(8,128)(2,1)}, u32[]{:S(2)}, u32[]{:S(2)}) async-start(bf16[8,256,512]{2,1,0:T(8,128)(2,1)} %bitcast.477), calls=%async_computation.9 | async-start | bytes 4194304 | tf_op jit(solution)/shard_map/all_to_all | solution.py:457
  1016.7 55.0 %collective-permute-start.79 = (bf16[2,128,2048]{2,1,0:T(8,128)(2,1)}, bf16[2,128,2048]{2,1,0:T(8,128)(2,1)}, u32[]{:S(2)}, u32[]{:S(2)}) collective-permute-start(bf16[2,128,2048]{2,1,0:T(8,128)(2,1)} %slice_bitcast_fusion.6), channel_id=1, source_target_pairs={{0,4},{1,3},{2,6},{3,1},{4,0},{5,7},{6,2},{7,5},{8,12},{9,11},{10,... | collective-permute-start | bytes 3145736 | tf_op jit(solution)/shard_map/ppermute | solution.py:122
  1048.2 52.1 %all-to-all-start.10 = ((bf16[8,256,512]{2,1,0:T(8,128)(2,1)}), bf16[8,256,512]{2,1,0:T(8,128)(2,1)}, u32[]{:S(2)}, u32[]{:S(2)}) async-start(bf16[8,256,512]{2,1,0:T(8,128)(2,1)} %bitcast.476), calls=%async_computation.10 | async-start | bytes 4194304 | tf_op jit(solution)/shard_map/all_to_all | solution.py:457
  1081.5 124.2 %collective-permute-start.88 = (bf16[128,2048]{1,0:T(8,128)(2,1)}, bf16[128,2048]{1,0:T(8,128)(2,1)}, u32[]{:S(2)}, u32[]{:S(2)}) collective-permute-start(bf16[128,2048]{1,0:T(8,128)(2,1)} %get-tuple-element.417), channel_id=1, source_target_pairs={{0,8},{1,9},{2,10},{3,11},{4,12},{5,13},{6,14},{7,15},{24,16},{25,... | collective-permute-start | bytes 1572872 | tf_op jit(solution)/shard_map/ppermute | solution.py:122
  1083.7 122.1 %collective-permute-start.89 = (bf16[128,2048]{1,0:T(8,128)(2,1)}, bf16[128,2048]{1,0:T(8,128)(2,1)}, u32[]{:S(2)}, u32[]{:S(2)}) collective-permute-start(bf16[128,2048]{1,0:T(8,128)(2,1)} %get-tuple-element.416), channel_id=1, source_target_pairs={{0,8},{1,9},{2,10},{3,11},{4,12},{5,13},{6,14},{7,15},{24,16},{25,... | collective-permute-start | bytes 1572872 | tf_op jit(solution)/shard_map/ppermute | solution.py:122
  1135.9 75.4 %all-to-all-start.11 = ((bf16[8,256,512]{2,1,0:T(8,128)(2,1)}), bf16[8,256,512]{2,1,0:T(8,128)(2,1)}, u32[]{:S(2)}, u32[]{:S(2)}) async-start(bf16[8,256,512]{2,1,0:T(8,128)(2,1)} %bitcast.475), calls=%async_computation.11 | async-start | bytes 4194304 | tf_op jit(solution)/shard_map/all_to_all | solution.py:457
  1145.1 56.1 %collective-permute-start.90 = (bf16[2,256,1536]{2,1,0:T(8,128)(2,1)}, bf16[2,256,1536]{2,1,0:T(8,128)(2,1)}, u32[]{:S(2)}, u32[]{:S(2)}) collective-permute-start(bf16[2,256,1536]{2,1,0:T(8,128)(2,1)} %fusion.20), channel_id=1, source_target_pairs={{0,4},{1,5},{2,6},{3,7},{4,0},{5,1},{6,2},{7,3},{8,12},{9,13},{10,... | collective-permute-start | bytes 4718600 | tf_op jit(solution)/shard_map/ppermute | solution.py:122
  (254 other events, 4539.5 us)

commit v5 on v4

--- a/solution.py
+++ b/solution.py
@@ -750,7 +750,6 @@
     ]
     out_flow = Flow(grid.scatter(out_parts))
     send(1, grad_mid_b)
-    out_flow.go(grad_mid_b)
     mix_flow.go(grad_mid_b)
     fourth = weigh(3, grad_attended)
     grad_heads = after(grad_heads, fourth, *mix_flow.hops[1])
@@ -766,7 +765,7 @@
     up_q, up_k = grad_qscaled * gain_q, grad_kscaled * gain_k
     along = jnp.stack([jnp.sum(up_q * query_normed, axis=-1), jnp.sum(up_k * key_normed, axis=-1)])
     along = (grid.group_sum(along) / width)[:, :, None]
-    along = after(along, *mix_flow.hops[2], *out_flow.hops[1])
+    along = after(along, *mix_flow.hops[2], *out_flow.hops[0])
     mix_flow.go(along)
     out_flow.go(along)
     grad_projected = jnp.concatenate(
@@ -791,16 +790,16 @@
     )
     proj_flow.go(home[1], home[2])
     send(3, grad_projected)
-    proj_flow.go(home[3], *mix_flow.hops[3], *out_flow.hops[2])
+    proj_flow.go(home[3], *mix_flow.hops[3], *out_flow.hops[1])
     mix_flow.go(*proj_flow.hops[0])
     out_flow.go(*proj_flow.hops[0])
     grad_down_w += dot(after(act_gated, *proj_flow.hops[0]), cot, SUM_ROWS)
-    proj_flow.go(grad_down_w, *mix_flow.hops[4], *out_flow.hops[3])
+    proj_flow.go(grad_down_w, *mix_flow.hops[4], *out_flow.hops[2])
     mix_flow.go(*proj_flow.hops[1])
     out_flow.go(*proj_flow.hops[1])
     home = after(home, *proj_flow.hops[1])
     grad_expert_in = undeal(home) if ff == 128 else undeal_narrow(home, ff)
-    proj_flow.go(grad_expert_in, *mix_flow.hops[5], *out_flow.hops[4])
+    proj_flow.go(grad_expert_in, *mix_flow.hops[5], *out_flow.hops[3])
     out_flow.go(*proj_flow.hops[2])
     grad_proj = proj_flow.finish()
     block_out = middle + jnp.concatenate([f.finish() for f in mix_flows])
@@ -838,9 +837,9 @@
     )
     last = last.reshape(count, -1, 128 if last.shape[1] % 128 == 0 else 64)
     last_flow = Flow(grid.small_sum(last))
-    last_flow.go(*proj_flow.hops[0])
     last_flow.go(*proj_flow.hops[1])
     last_flow.go(*proj_flow.hops[1])
+    last_flow.go(*proj_flow.hops[2])
     last_flow.go(grad_proj)
     last = last_flow.finish()
     last = last.reshape(-1)

time: 1390 us -> 1360 us (0.978)
  starting transfers between devices: 242 us -> 223 us
    unnamed x343 -> x339, local copies, waits for them, and re-layouts: 94 us -> 91.7 us
  transfers between devices with their start and end apart: 125 -> 125, of which waited for: 46 -> 45; matrix products, arithmetic and copies ran while one was open for 39% -> 39% of each run, Pallas kernels for 7% -> 7%
where the time goes in v5:
time: 1360 us; the launch traced here: 1350 us
  waiting for transfers between devices  373 us (27%)
  local copies, waits for them, and re-layouts  229 us (17%)
  starting transfers between devices  223 us (16%)
  matrix products  197 us (14%)
  other arithmetic  179 us (13%)
  Pallas kernels  122 us (9%)
  blocking collectives  15.8 us (1%)
    ppermute x86, waiting for transfers between devices, move(): return lax.ppermute(value, AXES, pairs)  239 us
    dot_general x23, matrix products, dot(): return lax.dot_general(left, right, dims, preferred_element_type=F32)  184 us
    ppermute x86, starting transfers between devices, move(): return lax.ppermute(value, AXES, pairs)  132 us
    pallas_call x4, Pallas kernels, moe_rows(): pl.pallas_call(functools.partial(moe_kernel, ff, local), grid=(total // t...  105 us
    unnamed x339, local copies, waits for them, and re-layouts  91.7 us
    ppermute x26, waiting for transfers between devices, flip(): return lax.ppermute(value, AXES, [(i, i ^ bit) for i in range(self.count)])  71.2 us
    add x14, other arithmetic, line_reduce(): return slots[0] + sent(slots[1])  45.5 us
    all_to_all x8, starting transfers between devices, swap(): return lax.all_to_all(value, 'dp', split_axis=0, concat_axis=0, tiled=True)  44.7 us
  transfers between devices with their start and end apart: 125, of which 45 were waited for; matrix products, arithmetic and copies ran while one was open for 39% of the time, Pallas kernels for 7%

profile of v5, /device:TPU:0, one launch (start us, length us, event | category | flops | bytes accessed | tf_op | source)
XLA Modules:
  0.0 1349.5 jit_solution(12683154558347776016)
XLA Ops:
  4.6 15.8 %all_to_all.70 = bf16[4,64,1536]{2,1,0:T(8,128)(2,1)S(1)} all-to-all(bf16[4,64,1536]{2,1,0:T(8,128)(2,1)S(1)} %reshape.760), channel_id=1, replica_groups=mesh['dp'=8,'expert'=4] {'expert'}, dimensions={0} | all-to-all | bytes 1572864 | tf_op jit(solution)/shard_map/all_to_all | solution.py:335
  81.0 12.7 collective-permute-done.6
  104.1 29.9 %collective-permute-done.16 = bf16[64,2048]{1,0:T(8,128)(2,1)S(1)} collective-permute-done((bf16[64,2048]{1,0:T(8,128)(2,1)}, bf16[64,2048]{1,0:T(8,128)(2,1)S(1)}, u32[]{:S(2)}, u32[]{:S(2)}) %collective-permute-start.16) | collective-permute-done | bytes 262176 | tf_op jit(solution)/shard_map/ppermute | solution.py:122
  158.2 14.9 %collective-permute-done.7 = bf16[8,19,128]{2,1,0:T(8,128)(2,1)S(1)} collective-permute-done((bf16[8,19,128]{2,1,0:T(8,128)(2,1)S(1)}, bf16[8,19,128]{2,1,0:T(8,128)(2,1)S(1)}, u32[]{:S(2)}, u32[]{:S(2)}) %collective-permute-start.7) | collective-permute-done | bytes 38944 | tf_op jit(solution)/shard_map/ppermute | solution.py:298
  302.6 14.0 %collective-permute-start.30 = (bf16[8,64,2048]{2,1,0:T(8,128)(2,1)}, bf16[8,64,2048]{2,1,0:T(8,128)(2,1)}, u32[]{:S(2)}, u32[]{:S(2)}) collective-permute-start(bf16[8,64,2048]{2,1,0:T(8,128)(2,1)} %pad_maximum_fusion.6), channel_id=1, source_target_pairs={{0,1},{1,0},{2,3},{3,2},{4,5},{5,4},{6,7},{7,6},{8,9},{9,8},{10,11... | collective-permute-start | bytes 6291464 | tf_op jit(solution)/shard_map/ppermute | solution.py:122
  390.5 16.4 %all-to-all-done.6 = bf16[8,256,512]{2,1,0:T(8,128)(2,1)} async-done(((bf16[8,256,512]{2,1,0:T(8,128)(2,1)}), bf16[8,256,512]{2,1,0:T(8,128)(2,1)}, u32[]{:S(2)}, u32[]{:S(2)}) %all-to-all-start.6) | async-done | bytes 2097184 | tf_op jit(solution)/shard_map/all_to_all | solution.py:457
  473.1 13.7 %collective-permute-done.45 = bf16[128,2048]{1,0:T(8,128)(2,1)S(1)} collective-permute-done((bf16[128,2048]{1,0:T(8,128)(2,1)S(1)}, bf16[128,2048]{1,0:T(8,128)(2,1)S(1)}, u32[]{:S(2)}, u32[]{:S(2)}) %collective-permute-start.45) | collective-permute-done | bytes 524320 | tf_op jit(solution)/shard_map/ppermute | solution.py:122
  498.2 12.5 collective-permute-done.50
  512.1 22.7 %fusion.124.lift_ref = f32[4096,1024]{1,0:T(8,128)} fusion(bf16[4096,2048]{1,0:T(8,128)(2,1)} %bitcast.60, bf16[1024,2048]{1,0:T(8,128)(2,1)S(1)} %bitcast.543), kind=kOutput, calls=%fused_computation.408 | convolution fusion | flops 17179869184 | bytes 37748736 | tf_op jit(solution)/shard_map/dot_general | solution.py:24
  583.6 26.0 %shard_map.234 = (bf16[1024,2048]{1,0:T(8,128)(2,1)}, bf16[1024,1024]{1,0:T(8,128)(2,1)}, f32[1024,8]{1,0:T(8,128)}, bf16[1024,2048]{1,0:T(8,128)(2,1)}) custom-call(bf16[4096,2048]{1,0:T(8,128)(2,1)} %bitcast.506, f32[4096,1024]{1,0:T(8,128)} %fusion.124.lift_ref, f32[4096,8]{1,0:T(8,128)} %bitcast.481, bf16[2048,2048]{1,0:T(8,128)(2,1)} %pad_maximum_fusion.w_ref), custom_call_target="tpu_custom_call" | custom-call | flops 17179869184 | bytes 25165824 | tf_op jit(solution)/shard_map/pallas_call | solution.py:375
  624.0 26.2 %shard_map.235 = (bf16[1024,2048]{1,0:T(8,128)(2,1)}, bf16[1024,1024]{1,0:T(8,128)(2,1)}, f32[1024,8]{1,0:T(8,128)}, f32[1024,2048]{1,0:T(8,128)}) custom-call(bf16[4096,2048]{1,0:T(8,128)(2,1)} %bitcast.507, f32[4096,1024]{1,0:T(8,128)} %fusion.124.lift_ref, f32[4096,8]{1,0:T(8,128)} %bitcast.482, bf16[2048,2048]{1,0:T(8,128)(2,1)} %pad_maximum_fusion.w_ref), custom_call_target="tpu_custom_call" | custom-call | flops 17179869184 | bytes 25165824 | tf_op jit(solution)/shard_map/pallas_call | solution.py:375
  664.2 26.2 %shard_map.236 = (bf16[1024,2048]{1,0:T(8,128)(2,1)}, bf16[1024,1024]{1,0:T(8,128)(2,1)}, f32[1024,8]{1,0:T(8,128)}, bf16[1024,2048]{1,0:T(8,128)(2,1)}) custom-call(bf16[4096,2048]{1,0:T(8,128)(2,1)} %bitcast.508, f32[4096,1024]{1,0:T(8,128)} %fusion.124.lift_ref, f32[4096,8]{1,0:T(8,128)} %bitcast.483, bf16[2048,2048]{1,0:T(8,128)(2,1)} %pad_maximum_fusion.w_ref), custom_call_target="tpu_custom_call" | custom-call | flops 17179869184 | bytes 25165824 | tf_op jit(solution)/shard_map/pallas_call | solution.py:375
  698.5 26.7 %shard_map.237 = (bf16[1024,2048]{1,0:T(8,128)(2,1)}, bf16[1024,1024]{1,0:T(8,128)(2,1)}, f32[1024,8]{1,0:T(8,128)}, f32[1024,2048]{1,0:T(8,128)}) custom-call(bf16[4096,2048]{1,0:T(8,128)(2,1)} %bitcast.509, f32[4096,1024]{1,0:T(8,128)} %fusion.124.lift_ref, f32[4096,8]{1,0:T(8,128)} %bitcast.484, bf16[2048,2048]{1,0:T(8,128)(2,1)} %pad_maximum_fusion.w_ref), custom_call_target="tpu_custom_call" | custom-call | flops 17179869184 | bytes 25165824 | tf_op jit(solution)/shard_map/pallas_call | solution.py:375
  740.2 19.5 %fusion.7 = bf16[2048,512]{1,0:T(8,128)(2,1)} fusion(bf16[4096,2048]{1,0:T(8,128)(2,1)} %bitcast.510, bf16[4096,2048]{1,0:T(8,128)(2,1)S(1)} %constant_dynamic-update-slice_fusion.36), kind=kOutput, calls=%fused_computation.23 | convolution fusion | flops 8589934592 | bytes 23068672 | tf_op jit(solution)/shard_map/dot_general | solution.py:24
  782.2 15.2 %fusion.1 = bf16[2048,512]{1,0:T(8,128)(2,1)} fusion(bf16[4096,2048]{1,0:T(8,128)(2,1)} %bitcast.511, bf16[4096,2048]{1,0:T(8,128)(2,1)} %copy-done.75), kind=kOutput, calls=%fused_computation.16 | convolution fusion | flops 8589934592 | bytes 23068672 | tf_op jit(solution)/shard_map/dot_general | solution.py:24
  797.5 14.8 %collective-permute-done.75 = f32[2,32,128]{2,1,0:T(8,128)S(1)} collective-permute-done((f32[2,32,128]{2,1,0:T(8,128)S(1)}, f32[2,32,128]{2,1,0:T(8,128)S(1)}, u32[]{:S(2)}, u32[]{:S(2)}) %collective-permute-start.75) | collective-permute-done | bytes 32800 | tf_op jit(solution)/shard_map/ppermute | solution.py:298
  866.2 14.6 %fusion.5 = bf16[2048,512]{1,0:T(8,128)(2,1)} fusion(bf16[4096,2048]{1,0:T(8,128)(2,1)} %bitcast.512, bf16[4096,2048]{1,0:T(8,128)(2,1)} %copy-done.75), kind=kOutput, calls=%fused_computation.20 | convolution fusion | flops 8589934592 | bytes 23068672 | tf_op jit(solution)/shard_map/dot_general | solution.py:24
  882.7 12.8 collective-permute-start.71
  895.5 14.8 %fusion.3 = bf16[2048,512]{1,0:T(8,128)(2,1)} fusion(bf16[4096,2048]{1,0:T(8,128)(2,1)} %bitcast.513, bf16[4096,2048]{1,0:T(8,128)(2,1)} %copy-done.75), kind=kOutput, calls=%fused_computation.18 | convolution fusion | flops 8589934592 | bytes 23068672 | tf_op jit(solution)/shard_map/dot_general | solution.py:24
  961.1 17.2 %collective-permute-done.78 = bf16[2,2,128,2048]{3,2,1,0:T(8,128)(2,1)} collective-permute-done((bf16[2,2,128,2048]{3,2,1,0:T(8,128)(2,1)}, bf16[2,2,128,2048]{3,2,1,0:T(8,128)(2,1)}, u32[]{:S(2)}, u32[]{:S(2)}) %collective-permute-start.78) | collective-permute-done | bytes 2097184 | tf_op jit(solution)/shard_map/ppermute | solution.py:122
  1067.4 17.6 %all-to-all-done.10.refs_2_ = bf16[8,256,512]{2,1,0:T(8,128)(2,1)} async-done(((bf16[8,256,512]{2,1,0:T(8,128)(2,1)}), bf16[8,256,512]{2,1,0:T(8,128)(2,1)}, u32[]{:S(2)}, u32[]{:S(2)}) %all-to-all-start.10) | async-done | bytes 2097184 | tf_op jit(solution)/shard_map/all_to_all | solution.py:457
  1149.8 28.8 %collective-permute-done.88 = bf16[2,256,1536]{2,1,0:T(8,128)(2,1)} collective-permute-done((bf16[2,256,1536]{2,1,0:T(8,128)(2,1)}, bf16[2,256,1536]{2,1,0:T(8,128)(2,1)}, u32[]{:S(2)}, u32[]{:S(2)}) %collective-permute-start.88) | collective-permute-done | bytes 1572896 | tf_op jit(solution)/shard_map/ppermute | solution.py:122
  1197.4 24.1 %fusion.125 = f32[1024,2048]{1,0:T(8,128)} fusion(bf16[4096,1024]{1,0:T(8,128)(2,1)} %pad_maximum_fusion.1, bf16[4096,2048]{1,0:T(8,128)(2,1)} %bitcast.60), kind=kOutput, calls=%fused_computation.409 | convolution fusion | flops 17179869184 | bytes 33554432 | tf_op jit(solution)/shard_map/dot_general | solution.py:24
  1293.0 15.8 %collective-permute-done.103 = bf16[256,1536]{1,0:T(8,128)(2,1)S(1)} collective-permute-done((bf16[256,1536]{1,0:T(8,128)(2,1)S(1)}, bf16[256,1536]{1,0:T(8,128)(2,1)S(1)}, u32[]{:S(2)}, u32[]{:S(2)}) %collective-permute-start.103) | collective-permute-done | bytes 786464 | tf_op jit(solution)/shard_map/ppermute | solution.py:122
  (873 shorter events, 885.1 us)
Async XLA Ops:
  76.2 57.8 %collective-permute-start.13 = (bf16[2,256,1536]{2,1,0:T(8,128)(2,1)S(1)}, bf16[2,256,1536]{2,1,0:T(8,128)(2,1)S(1)}, u32[]{:S(2)}, u32[]{:S(2)}) collective-permute-start(bf16[2,256,1536]{2,1,0:T(8,128)(2,1)S(1)} %pad_maximum_fusion.8), channel_id=1, source_target_pairs={{0,4},{1,5},{2,6},{3,7},{4,0},{5,1},{6,2},{7,3},{8,12},{9,13},{10,... | collective-permute-start | bytes 4718600 | tf_op jit(solution)/shard_map/ppermute | solution.py:122
  79.8 54.2 %collective-permute-start.12 = (bf16[256,1536]{1,0:T(8,128)(2,1)S(1)}, bf16[256,1536]{1,0:T(8,128)(2,1)S(1)}, u32[]{:S(2)}, u32[]{:S(2)}) collective-permute-start(bf16[256,1536]{1,0:T(8,128)(2,1)S(1)} %collective-permute-done.5), channel_id=1, source_target_pairs={{8,0},{9,1},{10,2},{11,3},{12,4},{13,5},{14,6},{15,7},{16,24},{17,... | collective-permute-start | bytes 2359304 | tf_op jit(solution)/shard_map/ppermute | solution.py:122
  135.8 61.7 %all-to-all-start.2 = ((bf16[8,256,512]{2,1,0:T(8,128)(2,1)}), bf16[8,256,512]{2,1,0:T(8,128)(2,1)}, u32[]{:S(2)}, u32[]{:S(2)}) async-start(bf16[8,256,512]{2,1,0:T(8,128)(2,1)} %get-tuple-element.181), calls=%async_computation.2 | async-start | bytes 4194304 | tf_op jit(solution)/shard_map/all_to_all | solution.py:457
  149.1 48.4 %collective-permute-start.19 = (bf16[2,256,1536]{2,1,0:T(8,128)(2,1)}, bf16[2,256,1536]{2,1,0:T(8,128)(2,1)}, u32[]{:S(2)}, u32[]{:S(2)}) collective-permute-start(bf16[2,256,1536]{2,1,0:T(8,128)(2,1)} %pad_maximum_fusion.9), channel_id=1, source_target_pairs={{0,4},{1,5},{2,6},{3,7},{4,0},{5,1},{6,2},{7,3},{8,12},{9,13},{10,... | collective-permute-start | bytes 4718600 | tf_op jit(solution)/shard_map/ppermute | solution.py:122
  197.5 53.8 %all-to-all-start.3 = ((bf16[8,256,512]{2,1,0:T(8,128)(2,1)}), bf16[8,256,512]{2,1,0:T(8,128)(2,1)}, u32[]{:S(2)}, u32[]{:S(2)}) async-start(bf16[8,256,512]{2,1,0:T(8,128)(2,1)} %get-tuple-element.183), calls=%async_computation.3 | async-start | bytes 4194304 | tf_op jit(solution)/shard_map/all_to_all | solution.py:457
  207.8 43.4 %collective-permute-start.28 = (bf16[2,128,2048]{2,1,0:T(8,128)(2,1)S(1)}, bf16[2,128,2048]{2,1,0:T(8,128)(2,1)}, u32[]{:S(2)}, u32[]{:S(2)}) collective-permute-start(bf16[2,128,2048]{2,1,0:T(8,128)(2,1)S(1)} %pad_maximum_fusion.11), channel_id=1, source_target_pairs={{0,4},{1,3},{2,6},{3,1},{4,0},{5,7},{6,2},{7,5},{8,12},{9,11},{10,... | collective-permute-start | bytes 3145736 | tf_op jit(solution)/shard_map/ppermute | solution.py:122
  281.7 65.9 %all-to-all-start.5 = ((bf16[8,256,512]{2,1,0:T(8,128)(2,1)}), bf16[8,256,512]{2,1,0:T(8,128)(2,1)}, u32[]{:S(2)}, u32[]{:S(2)}) async-start(bf16[8,256,512]{2,1,0:T(8,128)(2,1)} %get-tuple-element.191), calls=%async_computation.5 | async-start | bytes 4194304 | tf_op jit(solution)/shard_map/all_to_all | solution.py:457
  302.6 63.6 %collective-permute-start.30 = (bf16[8,64,2048]{2,1,0:T(8,128)(2,1)}, bf16[8,64,2048]{2,1,0:T(8,128)(2,1)}, u32[]{:S(2)}, u32[]{:S(2)}) collective-permute-start(bf16[8,64,2048]{2,1,0:T(8,128)(2,1)} %pad_maximum_fusion.6), channel_id=1, source_target_pairs={{0,1},{1,0},{2,3},{3,2},{4,5},{5,4},{6,7},{7,6},{8,9},{9,8},{10,11... | collective-permute-start | bytes 6291464 | tf_op jit(solution)/shard_map/ppermute | solution.py:122
  347.7 59.3 %all-to-all-start.6 = ((bf16[8,256,512]{2,1,0:T(8,128)(2,1)}), bf16[8,256,512]{2,1,0:T(8,128)(2,1)}, u32[]{:S(2)}, u32[]{:S(2)}) async-start(bf16[8,256,512]{2,1,0:T(8,128)(2,1)} %get-tuple-element.197), calls=%async_computation.6 | async-start | bytes 4194304 | tf_op jit(solution)/shard_map/all_to_all | solution.py:457
  431.9 61.3 %collective-permute-start.53 = (bf16[8,128,2048]{2,1,0:T(8,128)(2,1)S(1)}, bf16[8,128,2048]{2,1,0:T(8,128)(2,1)S(1)}, u32[]{:S(2)}, u32[]{:S(2)}) collective-permute-start(bf16[8,128,2048]{2,1,0:T(8,128)(2,1)S(1)} %pad_maximum_fusion.3), channel_id=1, source_target_pairs={{0,1},{1,0},{2,3},{3,2},{4,5},{5,4},{6,7},{7,6},{8,9},{9,8},{10,11... | collective-permute-start | bytes 12582920 | tf_op jit(solution)/shard_map/ppermute | solution.py:122
  690.4 69.3 %collective-permute-start.62 = (bf16[8,128,2048]{2,1,0:T(8,128)(2,1)}, bf16[8,128,2048]{2,1,0:T(8,128)(2,1)}, u32[]{:S(2)}, u32[]{:S(2)}) collective-permute-start(bf16[8,128,2048]{2,1,0:T(8,128)(2,1)} %bitcast.548), channel_id=1, source_target_pairs={{0,1},{1,0},{2,3},{3,2},{4,5},{5,4},{6,7},{7,6},{8,9},{9,8},{10,11... | collective-permute-start | bytes 12582920 | tf_op jit(solution)/shard_map/ppermute | solution.py:122
  774.2 65.2 %collective-permute-start.63 = (bf16[2,2,128,2048]{3,2,1,0:T(8,128)(2,1)}, bf16[2,2,128,2048]{3,2,1,0:T(8,128)(2,1)}, u32[]{:S(2)}, u32[]{:S(2)}) collective-permute-start(bf16[2,2,128,2048]{3,2,1,0:T(8,128)(2,1)} %fusion.15), channel_id=1, source_target_pairs={{0,2},{1,5},{2,0},{3,7},{4,6},{5,1},{6,4},{7,3},{8,10},{9,13},{10,... | collective-permute-start | bytes 6291464 | tf_op jit(solution)/shard_map/ppermute | solution.py:122
  775.5 45.2 %collective-permute-start.61 = (bf16[2,128,2048]{2,1,0:T(8,128)(2,1)}, bf16[2,128,2048]{2,1,0:T(8,128)(2,1)}, u32[]{:S(2)}, u32[]{:S(2)}) collective-permute-start(bf16[2,128,2048]{2,1,0:T(8,128)(2,1)} %fusion.34), channel_id=1, source_target_pairs={{0,4},{1,3},{2,6},{3,1},{4,0},{5,7},{6,2},{7,5},{8,12},{9,11},{10,... | collective-permute-start | bytes 3145736 | tf_op jit(solution)/shard_map/ppermute | solution.py:122
  776.9 104.4 %all-to-all-start.7 = ((bf16[8,256,512]{2,1,0:T(8,128)(2,1)}), bf16[8,256,512]{2,1,0:T(8,128)(2,1)S(1)}, u32[]{:S(2)}, u32[]{:S(2)}) async-start(bf16[8,256,512]{2,1,0:T(8,128)(2,1)} %bitcast.480), calls=%async_computation.7 | async-start | bytes 4194304 | tf_op jit(solution)/shard_map/all_to_all | solution.py:457
  866.2 47.0 %collective-permute-start.69 = (bf16[8,128,2048]{2,1,0:T(8,128)(2,1)}, bf16[8,128,2048]{2,1,0:T(8,128)(2,1)}, u32[]{:S(2)}, u32[]{:S(2)}) collective-permute-start(bf16[8,128,2048]{2,1,0:T(8,128)(2,1)} %bitcast.75), channel_id=1, source_target_pairs={{0,1},{1,0},{2,3},{3,2},{4,5},{5,4},{6,7},{7,6},{8,9},{9,8},{10,11... | collective-permute-start | bytes 12582920 | tf_op jit(solution)/shard_map/ppermute | solution.py:122
  982.1 50.9 %all-to-all-start.9 = ((bf16[8,256,512]{2,1,0:T(8,128)(2,1)}), bf16[8,256,512]{2,1,0:T(8,128)(2,1)}, u32[]{:S(2)}, u32[]{:S(2)}) async-start(bf16[8,256,512]{2,1,0:T(8,128)(2,1)} %bitcast.479), calls=%async_computation.9 | async-start | bytes 4194304 | tf_op jit(solution)/shard_map/all_to_all | solution.py:457
  1033.0 52.0 %all-to-all-start.10 = ((bf16[8,256,512]{2,1,0:T(8,128)(2,1)}), bf16[8,256,512]{2,1,0:T(8,128)(2,1)}, u32[]{:S(2)}, u32[]{:S(2)}) async-start(bf16[8,256,512]{2,1,0:T(8,128)(2,1)} %bitcast.478), calls=%async_computation.10 | async-start | bytes 4194304 | tf_op jit(solution)/shard_map/all_to_all | solution.py:457
  1051.8 131.4 %collective-permute-start.86 = (bf16[128,2048]{1,0:T(8,128)(2,1)}, bf16[128,2048]{1,0:T(8,128)(2,1)}, u32[]{:S(2)}, u32[]{:S(2)}) collective-permute-start(bf16[128,2048]{1,0:T(8,128)(2,1)} %get-tuple-element.411), channel_id=1, source_target_pairs={{0,8},{1,9},{2,10},{3,11},{4,12},{5,13},{6,14},{7,15},{24,16},{25,... | collective-permute-start | bytes 1572872 | tf_op jit(solution)/shard_map/ppermute | solution.py:122
  1056.3 126.8 %collective-permute-start.87 = (bf16[128,2048]{1,0:T(8,128)(2,1)}, bf16[128,2048]{1,0:T(8,128)(2,1)}, u32[]{:S(2)}, u32[]{:S(2)}) collective-permute-start(bf16[128,2048]{1,0:T(8,128)(2,1)} %get-tuple-element.410), channel_id=1, source_target_pairs={{0,8},{1,9},{2,10},{3,11},{4,12},{5,13},{6,14},{7,15},{24,16},{25,... | collective-permute-start | bytes 1572872 | tf_op jit(solution)/shard_map/ppermute | solution.py:122
  1115.6 73.0 %all-to-all-start.11 = ((bf16[8,256,512]{2,1,0:T(8,128)(2,1)}), bf16[8,256,512]{2,1,0:T(8,128)(2,1)}, u32[]{:S(2)}, u32[]{:S(2)}) async-start(bf16[8,256,512]{2,1,0:T(8,128)(2,1)} %bitcast.477), calls=%async_computation.11 | async-start | bytes 4194304 | tf_op jit(solution)/shard_map/all_to_all | solution.py:457
  1123.4 55.2 %collective-permute-start.88 = (bf16[2,256,1536]{2,1,0:T(8,128)(2,1)}, bf16[2,256,1536]{2,1,0:T(8,128)(2,1)}, u32[]{:S(2)}, u32[]{:S(2)}) collective-permute-start(bf16[2,256,1536]{2,1,0:T(8,128)(2,1)} %fusion.20), channel_id=1, source_target_pairs={{0,4},{1,5},{2,6},{3,7},{4,0},{5,1},{6,2},{7,3},{8,12},{9,13},{10,... | collective-permute-start | bytes 4718600 | tf_op jit(solution)/shard_map/ppermute | solution.py:122
  1185.7 52.5 %collective-permute-start.89 = (bf16[128,2048]{1,0:T(8,128)(2,1)}, bf16[128,2048]{1,0:T(8,128)(2,1)}, u32[]{:S(2)}, u32[]{:S(2)}) collective-permute-start(bf16[128,2048]{1,0:T(8,128)(2,1)} %get-tuple-element.409), channel_id=1, source_target_pairs={{8,16},{9,17},{10,18},{11,19},{12,20},{13,21},{14,22},{15,23},{16,... | collective-permute-start | bytes 1572872 | tf_op jit(solution)/shard_map/ppermute | solution.py:122
  1187.2 51.0 %collective-permute-start.90 = (bf16[128,2048]{1,0:T(8,128)(2,1)}, bf16[128,2048]{1,0:T(8,128)(2,1)}, u32[]{:S(2)}, u32[]{:S(2)}) collective-permute-start(bf16[128,2048]{1,0:T(8,128)(2,1)} %get-tuple-element.408), channel_id=1, source_target_pairs={{8,16},{9,17},{10,18},{11,19},{12,20},{13,21},{14,22},{15,23},{16,... | collective-permute-start | bytes 1572872 | tf_op jit(solution)/shard_map/ppermute | solution.py:122
  1190.8 47.3 %collective-permute-start.93 = (bf16[256,1536]{1,0:T(8,128)(2,1)S(1)}, bf16[256,1536]{1,0:T(8,128)(2,1)S(1)}, u32[]{:S(2)}, u32[]{:S(2)}) collective-permute-start(bf16[256,1536]{1,0:T(8,128)(2,1)S(1)} %get-tuple-element.395), channel_id=1, source_target_pairs={{0,8},{1,9},{2,10},{3,11},{4,12},{5,13},{6,14},{7,15},{24,16},{25,... | collective-permute-start | bytes 2359304 | tf_op jit(solution)/shard_map/ppermute | solution.py:122
  (252 other events, 4515.5 us)

commit v6 on v3

--- a/solution.py
+++ b/solution.py
@@ -825,7 +825,7 @@
         ],
         axis=1,
     )
-    last = after(last, *proj_flow.hops[2])
+    last = after(last, grad_proj)
     last = grid.small_scatter(last.reshape(count, -1, 128 if last.shape[1] % 128 == 0 else 64))
     last = last.reshape(-1)
     grad_norm_gains = last[: 4 * rows].reshape(4, rows)

time: 1340 us -> 1350 us (level)
  other arithmetic: 165 us -> 182 us
    ppermute x26, starting transfers between devices: 48.5 us -> 22.7 us  [flip(): return lax.ppermute(value, AXES, [(i, i ^ bit) for i in range(self.count)])]
    ppermute x86, waiting for transfers between devices: 252 us -> 268 us  [move(): return lax.ppermute(value, AXES, pairs)]
    unnamed x360 -> x340, local copies, waits for them, and re-layouts: 81.1 us -> 84.3 us
  transfers between devices with their start and end apart: 125 -> 125, of which waited for: 43 -> 42; matrix products, arithmetic and copies ran while one was open for 36% -> 39% of each run, Pallas kernels for 7% -> 7%
where the time goes in v6:
time: 1350 us; the launch traced here: 1340 us
  waiting for transfers between devices  370 us (27%)
  starting transfers between devices  228 us (17%)
  local copies, waits for them, and re-layouts  215 us (16%)
  matrix products  198 us (15%)
  other arithmetic  182 us (13%)
  Pallas kernels  122 us (9%)
  blocking collectives  15.8 us (1%)
    ppermute x86, waiting for transfers between devices, move(): return lax.ppermute(value, AXES, pairs)  268 us
    dot_general x23, matrix products, dot(): return lax.dot_general(left, right, dims, preferred_element_type=F32)  185 us
    ppermute x86, starting transfers between devices, move(): return lax.ppermute(value, AXES, pairs)  133 us
    pallas_call x4, Pallas kernels, moe_rows(): pl.pallas_call(functools.partial(moe_kernel, ff, local), grid=(total // t...  105 us
    unnamed x340, local copies, waits for them, and re-layouts  84.3 us
    ppermute x26, waiting for transfers between devices, flip(): return lax.ppermute(value, AXES, [(i, i ^ bit) for i in range(self.count)])  56.7 us
    all_to_all x8, starting transfers between devices, swap(): return lax.all_to_all(value, 'dp', split_axis=0, concat_axis=0, tiled=True)  47.7 us
    add x14, other arithmetic, line_reduce(): return slots[0] + sent(slots[1])  47.4 us
  transfers between devices with their start and end apart: 125, of which 42 were waited for; matrix products, arithmetic and copies ran while one was open for 39% of the time, Pallas kernels for 7%

profile of v6, /device:TPU:0, one launch (start us, length us, event | category | flops | bytes accessed | tf_op | source)
XLA Modules:
  0.0 1342.0 jit_solution(18320054405368874997)
XLA Ops:
  4.6 15.8 %all_to_all.70 = bf16[4,64,1536]{2,1,0:T(8,128)(2,1)S(1)} all-to-all(bf16[4,64,1536]{2,1,0:T(8,128)(2,1)S(1)} %reshape.745), channel_id=1, replica_groups=mesh['dp'=8,'expert'=4] {'expert'}, dimensions={0} | all-to-all | bytes 1572864 | tf_op jit(solution)/shard_map/all_to_all | solution.py:325
  81.0 12.7 collective-permute-done.6
  104.0 29.9 %collective-permute-done.16 = bf16[64,2048]{1,0:T(8,128)(2,1)S(1)} collective-permute-done((bf16[64,2048]{1,0:T(8,128)(2,1)}, bf16[64,2048]{1,0:T(8,128)(2,1)S(1)}, u32[]{:S(2)}, u32[]{:S(2)}) %collective-permute-start.16) | collective-permute-done | bytes 262176 | tf_op jit(solution)/shard_map/ppermute | solution.py:122
  158.2 15.0 %collective-permute-done.7 = bf16[8,19,128]{2,1,0:T(8,128)(2,1)S(1)} collective-permute-done((bf16[8,19,128]{2,1,0:T(8,128)(2,1)S(1)}, bf16[8,19,128]{2,1,0:T(8,128)(2,1)S(1)}, u32[]{:S(2)}, u32[]{:S(2)}) %collective-permute-start.7) | collective-permute-done | bytes 38944 | tf_op jit(solution)/shard_map/ppermute | solution.py:298
  305.1 14.0 %collective-permute-start.30 = (bf16[8,64,2048]{2,1,0:T(8,128)(2,1)}, bf16[8,64,2048]{2,1,0:T(8,128)(2,1)}, u32[]{:S(2)}, u32[]{:S(2)}) collective-permute-start(bf16[8,64,2048]{2,1,0:T(8,128)(2,1)} %pad_maximum_fusion.6), channel_id=1, source_target_pairs={{0,1},{1,0},{2,3},{3,2},{4,5},{5,4},{6,7},{7,6},{8,9},{9,8},{10,11... | collective-permute-start | bytes 6291464 | tf_op jit(solution)/shard_map/ppermute | solution.py:122
  393.4 16.4 %all-to-all-done.6 = bf16[8,256,512]{2,1,0:T(8,128)(2,1)} async-done(((bf16[8,256,512]{2,1,0:T(8,128)(2,1)}), bf16[8,256,512]{2,1,0:T(8,128)(2,1)}, u32[]{:S(2)}, u32[]{:S(2)}) %all-to-all-start.6) | async-done | bytes 2097184 | tf_op jit(solution)/shard_map/all_to_all | solution.py:447
  475.9 13.7 %collective-permute-done.45 = bf16[128,2048]{1,0:T(8,128)(2,1)S(1)} collective-permute-done((bf16[128,2048]{1,0:T(8,128)(2,1)S(1)}, bf16[128,2048]{1,0:T(8,128)(2,1)S(1)}, u32[]{:S(2)}, u32[]{:S(2)}) %collective-permute-start.45) | collective-permute-done | bytes 524320 | tf_op jit(solution)/shard_map/ppermute | solution.py:122
  501.0 12.5 collective-permute-done.50
  514.9 22.7 %fusion.118.lift_ref = f32[4096,1024]{1,0:T(8,128)} fusion(bf16[4096,2048]{1,0:T(8,128)(2,1)} %bitcast.60, bf16[1024,2048]{1,0:T(8,128)(2,1)S(1)} %bitcast.498), kind=kOutput, calls=%fused_computation.400 | convolution fusion | flops 17179869184 | bytes 37748736 | tf_op jit(solution)/shard_map/dot_general | solution.py:24
  554.9 11.6 collective-permute-done.57
  586.4 26.0 %shard_map.234 = (bf16[1024,2048]{1,0:T(8,128)(2,1)}, bf16[1024,1024]{1,0:T(8,128)(2,1)}, f32[1024,8]{1,0:T(8,128)}, bf16[1024,2048]{1,0:T(8,128)(2,1)}) custom-call(bf16[4096,2048]{1,0:T(8,128)(2,1)} %bitcast.463, f32[4096,1024]{1,0:T(8,128)} %fusion.118.lift_ref, f32[4096,8]{1,0:T(8,128)} %bitcast.447, bf16[2048,2048]{1,0:T(8,128)(2,1)} %pad_maximum_fusion.w_ref), custom_call_target="tpu_custom_call" | custom-call | flops 17179869184 | bytes 25165824 | tf_op jit(solution)/shard_map/pallas_call | solution.py:365
  625.8 26.2 %shard_map.235 = (bf16[1024,2048]{1,0:T(8,128)(2,1)}, bf16[1024,1024]{1,0:T(8,128)(2,1)}, f32[1024,8]{1,0:T(8,128)}, f32[1024,2048]{1,0:T(8,128)}) custom-call(bf16[4096,2048]{1,0:T(8,128)(2,1)} %bitcast.464, f32[4096,1024]{1,0:T(8,128)} %fusion.118.lift_ref, f32[4096,8]{1,0:T(8,128)} %bitcast.448, bf16[2048,2048]{1,0:T(8,128)(2,1)} %pad_maximum_fusion.w_ref), custom_call_target="tpu_custom_call" | custom-call | flops 17179869184 | bytes 25165824 | tf_op jit(solution)/shard_map/pallas_call | solution.py:365
  668.8 26.1 %shard_map.236 = (bf16[1024,2048]{1,0:T(8,128)(2,1)}, bf16[1024,1024]{1,0:T(8,128)(2,1)}, f32[1024,8]{1,0:T(8,128)}, bf16[1024,2048]{1,0:T(8,128)(2,1)}) custom-call(bf16[4096,2048]{1,0:T(8,128)(2,1)} %bitcast.465, f32[4096,1024]{1,0:T(8,128)} %fusion.118.lift_ref, f32[4096,8]{1,0:T(8,128)} %bitcast.449, bf16[2048,2048]{1,0:T(8,128)(2,1)} %pad_maximum_fusion.w_ref), custom_call_target="tpu_custom_call" | custom-call | flops 17179869184 | bytes 25165824 | tf_op jit(solution)/shard_map/pallas_call | solution.py:365
  706.8 26.9 %shard_map.237 = (bf16[1024,2048]{1,0:T(8,128)(2,1)}, bf16[1024,1024]{1,0:T(8,128)(2,1)}, f32[1024,8]{1,0:T(8,128)}, f32[1024,2048]{1,0:T(8,128)}) custom-call(bf16[4096,2048]{1,0:T(8,128)(2,1)} %bitcast.466, f32[4096,1024]{1,0:T(8,128)} %fusion.118.lift_ref, f32[4096,8]{1,0:T(8,128)} %bitcast.450, bf16[2048,2048]{1,0:T(8,128)(2,1)} %pad_maximum_fusion.w_ref), custom_call_target="tpu_custom_call" | custom-call | flops 17179869184 | bytes 25165824 | tf_op jit(solution)/shard_map/pallas_call | solution.py:365
  748.9 19.5 %fusion.7 = bf16[2048,512]{1,0:T(8,128)(2,1)} fusion(bf16[4096,2048]{1,0:T(8,128)(2,1)} %bitcast.467, bf16[4096,2048]{1,0:T(8,128)(2,1)S(1)} %constant_dynamic-update-slice_fusion.36), kind=kOutput, calls=%fused_computation.23 | convolution fusion | flops 8589934592 | bytes 23068672 | tf_op jit(solution)/shard_map/dot_general | solution.py:24
  789.7 14.6 %fusion.1 = bf16[2048,512]{1,0:T(8,128)(2,1)} fusion(bf16[4096,2048]{1,0:T(8,128)(2,1)} %bitcast.468, bf16[4096,2048]{1,0:T(8,128)(2,1)} %copy-done.80), kind=kOutput, calls=%fused_computation.16 | convolution fusion | flops 8589934592 | bytes 23068672 | tf_op jit(solution)/shard_map/dot_general | solution.py:24
  804.5 22.7 %collective-permute-done.61 = bf16[2,128,2048]{2,1,0:T(8,128)(2,1)S(1)} collective-permute-done((bf16[2,128,2048]{2,1,0:T(8,128)(2,1)}, bf16[2,128,2048]{2,1,0:T(8,128)(2,1)S(1)}, u32[]{:S(2)}, u32[]{:S(2)}) %collective-permute-start.61) | collective-permute-done | bytes 1048608 | tf_op jit(solution)/shard_map/ppermute | solution.py:122
  866.6 14.6 %fusion.5 = bf16[2048,512]{1,0:T(8,128)(2,1)} fusion(bf16[4096,2048]{1,0:T(8,128)(2,1)} %bitcast.469, bf16[4096,2048]{1,0:T(8,128)(2,1)} %copy-done.80), kind=kOutput, calls=%fused_computation.20 | convolution fusion | flops 8589934592 | bytes 23068672 | tf_op jit(solution)/shard_map/dot_general | solution.py:24
  888.5 15.0 %fusion.3 = bf16[2048,512]{1,0:T(8,128)(2,1)} fusion(bf16[4096,2048]{1,0:T(8,128)(2,1)} %bitcast.470, bf16[4096,2048]{1,0:T(8,128)(2,1)} %copy-done.80), kind=kOutput, calls=%fused_computation.18 | convolution fusion | flops 8589934592 | bytes 23068672 | tf_op jit(solution)/shard_map/dot_general | solution.py:24
  954.1 17.4 %collective-permute-done.78 = bf16[2,2,128,2048]{3,2,1,0:T(8,128)(2,1)} collective-permute-done((bf16[2,2,128,2048]{3,2,1,0:T(8,128)(2,1)}, bf16[2,2,128,2048]{3,2,1,0:T(8,128)(2,1)}, u32[]{:S(2)}, u32[]{:S(2)}) %collective-permute-start.78) | collective-permute-done | bytes 2097184 | tf_op jit(solution)/shard_map/ppermute | solution.py:122
  1067.0 11.3 all-to-all-done.10.refs_2_
  1101.1 40.5 %collective-permute-done.88 = bf16[2,256,1536]{2,1,0:T(8,128)(2,1)S(1)} collective-permute-done((bf16[2,256,1536]{2,1,0:T(8,128)(2,1)S(1)}, bf16[2,256,1536]{2,1,0:T(8,128)(2,1)S(1)}, u32[]{:S(2)}, u32[]{:S(2)}) %collective-permute-start.88) | collective-permute-done | bytes 1572896 | tf_op jit(solution)/shard_map/ppermute | solution.py:122
  1167.5 24.1 %fusion.119 = f32[1024,2048]{1,0:T(8,128)} fusion(bf16[4096,1024]{1,0:T(8,128)(2,1)} %pad_maximum_fusion.1, bf16[4096,2048]{1,0:T(8,128)(2,1)} %bitcast.60), kind=kOutput, calls=%fused_computation.401 | convolution fusion | flops 17179869184 | bytes 33554432 | tf_op jit(solution)/shard_map/dot_general | solution.py:24
  1233.6 12.1 shard_map.238
  (873 shorter events, 869.0 us)
Async XLA Ops:
  76.2 57.8 %collective-permute-start.13 = (bf16[2,256,1536]{2,1,0:T(8,128)(2,1)S(1)}, bf16[2,256,1536]{2,1,0:T(8,128)(2,1)S(1)}, u32[]{:S(2)}, u32[]{:S(2)}) collective-permute-start(bf16[2,256,1536]{2,1,0:T(8,128)(2,1)S(1)} %pad_maximum_fusion.8), channel_id=1, source_target_pairs={{0,4},{1,5},{2,6},{3,7},{4,0},{5,1},{6,2},{7,3},{8,12},{9,13},{10,... | collective-permute-start | bytes 4718600 | tf_op jit(solution)/shard_map/ppermute | solution.py:122
  79.7 54.2 %collective-permute-start.12 = (bf16[256,1536]{1,0:T(8,128)(2,1)S(1)}, bf16[256,1536]{1,0:T(8,128)(2,1)S(1)}, u32[]{:S(2)}, u32[]{:S(2)}) collective-permute-start(bf16[256,1536]{1,0:T(8,128)(2,1)S(1)} %collective-permute-done.5), channel_id=1, source_target_pairs={{8,0},{9,1},{10,2},{11,3},{12,4},{13,5},{14,6},{15,7},{16,24},{17,... | collective-permute-start | bytes 2359304 | tf_op jit(solution)/shard_map/ppermute | solution.py:122
  135.8 61.8 %all-to-all-start.2 = ((bf16[8,256,512]{2,1,0:T(8,128)(2,1)}), bf16[8,256,512]{2,1,0:T(8,128)(2,1)}, u32[]{:S(2)}, u32[]{:S(2)}) async-start(bf16[8,256,512]{2,1,0:T(8,128)(2,1)} %get-tuple-element.178), calls=%async_computation.2 | async-start | bytes 4194304 | tf_op jit(solution)/shard_map/all_to_all | solution.py:447
  149.0 48.5 %collective-permute-start.19 = (bf16[2,256,1536]{2,1,0:T(8,128)(2,1)}, bf16[2,256,1536]{2,1,0:T(8,128)(2,1)}, u32[]{:S(2)}, u32[]{:S(2)}) collective-permute-start(bf16[2,256,1536]{2,1,0:T(8,128)(2,1)} %pad_maximum_fusion.9), channel_id=1, source_target_pairs={{0,4},{1,5},{2,6},{3,7},{4,0},{5,1},{6,2},{7,3},{8,12},{9,13},{10,... | collective-permute-start | bytes 4718600 | tf_op jit(solution)/shard_map/ppermute | solution.py:122
  197.5 56.2 %all-to-all-start.3 = ((bf16[8,256,512]{2,1,0:T(8,128)(2,1)}), bf16[8,256,512]{2,1,0:T(8,128)(2,1)}, u32[]{:S(2)}, u32[]{:S(2)}) async-start(bf16[8,256,512]{2,1,0:T(8,128)(2,1)} %get-tuple-element.180), calls=%async_computation.3 | async-start | bytes 4194304 | tf_op jit(solution)/shard_map/all_to_all | solution.py:447
  208.1 45.7 %collective-permute-start.28 = (bf16[2,128,2048]{2,1,0:T(8,128)(2,1)S(1)}, bf16[2,128,2048]{2,1,0:T(8,128)(2,1)}, u32[]{:S(2)}, u32[]{:S(2)}) collective-permute-start(bf16[2,128,2048]{2,1,0:T(8,128)(2,1)S(1)} %pad_maximum_fusion.11), channel_id=1, source_target_pairs={{0,4},{1,3},{2,6},{3,1},{4,0},{5,7},{6,2},{7,5},{8,12},{9,11},{10,... | collective-permute-start | bytes 3145736 | tf_op jit(solution)/shard_map/ppermute | solution.py:122
  284.2 66.0 %all-to-all-start.5 = ((bf16[8,256,512]{2,1,0:T(8,128)(2,1)}), bf16[8,256,512]{2,1,0:T(8,128)(2,1)}, u32[]{:S(2)}, u32[]{:S(2)}) async-start(bf16[8,256,512]{2,1,0:T(8,128)(2,1)} %get-tuple-element.188), calls=%async_computation.5 | async-start | bytes 4194304 | tf_op jit(solution)/shard_map/all_to_all | solution.py:447
  305.1 64.0 %collective-permute-start.30 = (bf16[8,64,2048]{2,1,0:T(8,128)(2,1)}, bf16[8,64,2048]{2,1,0:T(8,128)(2,1)}, u32[]{:S(2)}, u32[]{:S(2)}) collective-permute-start(bf16[8,64,2048]{2,1,0:T(8,128)(2,1)} %pad_maximum_fusion.6), channel_id=1, source_target_pairs={{0,1},{1,0},{2,3},{3,2},{4,5},{5,4},{6,7},{7,6},{8,9},{9,8},{10,11... | collective-permute-start | bytes 6291464 | tf_op jit(solution)/shard_map/ppermute | solution.py:122
  350.3 59.5 %all-to-all-start.6 = ((bf16[8,256,512]{2,1,0:T(8,128)(2,1)}), bf16[8,256,512]{2,1,0:T(8,128)(2,1)}, u32[]{:S(2)}, u32[]{:S(2)}) async-start(bf16[8,256,512]{2,1,0:T(8,128)(2,1)} %get-tuple-element.194), calls=%async_computation.6 | async-start | bytes 4194304 | tf_op jit(solution)/shard_map/all_to_all | solution.py:447
  434.7 61.3 %collective-permute-start.53 = (bf16[8,128,2048]{2,1,0:T(8,128)(2,1)S(1)}, bf16[8,128,2048]{2,1,0:T(8,128)(2,1)S(1)}, u32[]{:S(2)}, u32[]{:S(2)}) collective-permute-start(bf16[8,128,2048]{2,1,0:T(8,128)(2,1)S(1)} %pad_maximum_fusion.3), channel_id=1, source_target_pairs={{0,1},{1,0},{2,3},{3,2},{4,5},{5,4},{6,7},{7,6},{8,9},{9,8},{10,11... | collective-permute-start | bytes 12582920 | tf_op jit(solution)/shard_map/ppermute | solution.py:122
  694.9 73.7 %collective-permute-start.62 = (bf16[8,128,2048]{2,1,0:T(8,128)(2,1)}, bf16[8,128,2048]{2,1,0:T(8,128)(2,1)}, u32[]{:S(2)}, u32[]{:S(2)}) collective-permute-start(bf16[8,128,2048]{2,1,0:T(8,128)(2,1)} %bitcast.503), channel_id=1, source_target_pairs={{0,1},{1,0},{2,3},{3,2},{4,5},{5,4},{6,7},{7,6},{8,9},{9,8},{10,11... | collective-permute-start | bytes 12582920 | tf_op jit(solution)/shard_map/ppermute | solution.py:122
  782.8 62.0 %collective-permute-start.63 = (bf16[2,2,128,2048]{3,2,1,0:T(8,128)(2,1)}, bf16[2,2,128,2048]{3,2,1,0:T(8,128)(2,1)}, u32[]{:S(2)}, u32[]{:S(2)}) collective-permute-start(bf16[2,2,128,2048]{3,2,1,0:T(8,128)(2,1)} %fusion.15), channel_id=1, source_target_pairs={{0,2},{1,5},{2,0},{3,7},{4,6},{5,1},{6,4},{7,3},{8,10},{9,13},{10,... | collective-permute-start | bytes 6291464 | tf_op jit(solution)/shard_map/ppermute | solution.py:122
  784.6 97.1 %all-to-all-start.7 = ((bf16[8,256,512]{2,1,0:T(8,128)(2,1)}), bf16[8,256,512]{2,1,0:T(8,128)(2,1)S(1)}, u32[]{:S(2)}, u32[]{:S(2)}) async-start(bf16[8,256,512]{2,1,0:T(8,128)(2,1)} %bitcast.446), calls=%async_computation.7 | async-start | bytes 4194304 | tf_op jit(solution)/shard_map/all_to_all | solution.py:447
  975.3 55.4 %all-to-all-start.9 = ((bf16[8,256,512]{2,1,0:T(8,128)(2,1)}), bf16[8,256,512]{2,1,0:T(8,128)(2,1)}, u32[]{:S(2)}, u32[]{:S(2)}) async-start(bf16[8,256,512]{2,1,0:T(8,128)(2,1)} %bitcast.445), calls=%async_computation.9 | async-start | bytes 4194304 | tf_op jit(solution)/shard_map/all_to_all | solution.py:447
  1030.7 47.6 %all-to-all-start.10 = ((bf16[8,256,512]{2,1,0:T(8,128)(2,1)}), bf16[8,256,512]{2,1,0:T(8,128)(2,1)}, u32[]{:S(2)}, u32[]{:S(2)}) async-start(bf16[8,256,512]{2,1,0:T(8,128)(2,1)} %bitcast.444), calls=%async_computation.10 | async-start | bytes 4194304 | tf_op jit(solution)/shard_map/all_to_all | solution.py:447
  1047.5 46.8 %collective-permute-start.91 = (bf16[2,2,64,2048]{3,2,1,0:T(8,128)(2,1)}, bf16[2,2,64,2048]{3,2,1,0:T(8,128)(2,1)}, u32[]{:S(2)}, u32[]{:S(2)}) collective-permute-start(bf16[2,2,64,2048]{3,2,1,0:T(8,128)(2,1)} %fusion.36), channel_id=1, source_target_pairs={{0,2},{1,5},{2,0},{3,7},{4,6},{5,1},{6,4},{7,3},{8,10},{9,13},{10,... | collective-permute-start | bytes 3145736 | tf_op jit(solution)/shard_map/ppermute | solution.py:122
  1078.3 71.7 %all-to-all-start.11 = ((bf16[8,256,512]{2,1,0:T(8,128)(2,1)}), bf16[8,256,512]{2,1,0:T(8,128)(2,1)}, u32[]{:S(2)}, u32[]{:S(2)}) async-start(bf16[8,256,512]{2,1,0:T(8,128)(2,1)} %bitcast.442), calls=%async_computation.11 | async-start | bytes 4194304 | tf_op jit(solution)/shard_map/all_to_all | solution.py:447
  1087.5 54.1 %collective-permute-start.88 = (bf16[2,256,1536]{2,1,0:T(8,128)(2,1)S(1)}, bf16[2,256,1536]{2,1,0:T(8,128)(2,1)S(1)}, u32[]{:S(2)}, u32[]{:S(2)}) collective-permute-start(bf16[2,256,1536]{2,1,0:T(8,128)(2,1)S(1)} %fusion.20), channel_id=1, source_target_pairs={{0,4},{1,5},{2,6},{3,7},{4,0},{5,1},{6,2},{7,3},{8,12},{9,13},{10,... | collective-permute-start | bytes 4718600 | tf_op jit(solution)/shard_map/ppermute | solution.py:122
  1089.5 56.2 %collective-permute-start.86 = (bf16[128,2048]{1,0:T(8,128)(2,1)S(1)}, bf16[128,2048]{1,0:T(8,128)(2,1)S(1)}, u32[]{:S(2)}, u32[]{:S(2)}) collective-permute-start(bf16[128,2048]{1,0:T(8,128)(2,1)S(1)} %get-tuple-element.397), channel_id=1, source_target_pairs={{0,8},{1,9},{2,10},{3,11},{4,12},{5,13},{6,14},{7,15},{24,16},{25,... | collective-permute-start | bytes 1572872 | tf_op jit(solution)/shard_map/ppermute | solution.py:122
  1093.0 52.8 %collective-permute-start.87 = (bf16[128,2048]{1,0:T(8,128)(2,1)S(1)}, bf16[128,2048]{1,0:T(8,128)(2,1)S(1)}, u32[]{:S(2)}, u32[]{:S(2)}) collective-permute-start(bf16[128,2048]{1,0:T(8,128)(2,1)S(1)} %get-tuple-element.396), channel_id=1, source_target_pairs={{0,8},{1,9},{2,10},{3,11},{4,12},{5,13},{6,14},{7,15},{24,16},{25,... | collective-permute-start | bytes 1572872 | tf_op jit(solution)/shard_map/ppermute | solution.py:122
  1147.1 61.3 %collective-permute-start.89 = (bf16[128,2048]{1,0:T(8,128)(2,1)}, bf16[128,2048]{1,0:T(8,128)(2,1)}, u32[]{:S(2)}, u32[]{:S(2)}) collective-permute-start(bf16[128,2048]{1,0:T(8,128)(2,1)} %get-tuple-element.395), channel_id=1, source_target_pairs={{8,16},{9,17},{10,18},{11,19},{12,20},{13,21},{14,22},{15,23},{16,... | collective-permute-start | bytes 1572872 | tf_op jit(solution)/shard_map/ppermute | solution.py:122
  1148.6 59.8 %collective-permute-start.90 = (bf16[128,2048]{1,0:T(8,128)(2,1)}, bf16[128,2048]{1,0:T(8,128)(2,1)}, u32[]{:S(2)}, u32[]{:S(2)}) collective-permute-start(bf16[128,2048]{1,0:T(8,128)(2,1)} %get-tuple-element.394), channel_id=1, source_target_pairs={{8,16},{9,17},{10,18},{11,19},{12,20},{13,21},{14,22},{15,23},{16,... | collective-permute-start | bytes 1572872 | tf_op jit(solution)/shard_map/ppermute | solution.py:122
  1150.1 120.5 %all-to-all-start.12 = ((bf16[4,128,2048]{2,1,0:T(8,128)(2,1)}), bf16[4,128,2048]{2,1,0:T(8,128)(2,1)}, u32[]{:S(2)}, u32[]{:S(2)}) async-start(bf16[4,128,2048]{2,1,0:T(8,128)(2,1)} %bitcast.443), calls=%async_computation.12 | async-start | bytes 4194304 | tf_op jit(solution)/shard_map/all_to_all | solution.py:325
  1161.2 47.2 %collective-permute-start.93 = (bf16[256,1536]{1,0:T(8,128)(2,1)S(1)}, bf16[256,1536]{1,0:T(8,128)(2,1)S(1)}, u32[]{:S(2)}, u32[]{:S(2)}) collective-permute-start(bf16[256,1536]{1,0:T(8,128)(2,1)S(1)} %get-tuple-element.381), channel_id=1, source_target_pairs={{0,8},{1,9},{2,10},{3,11},{4,12},{5,13},{6,14},{7,15},{24,16},{25,... | collective-permute-start | bytes 2359304 | tf_op jit(solution)/shard_map/ppermute | solution.py:122
  (252 other events, 4435.1 us)
